TPU v7x, 32 devices: a whole 2x2x4 slice. The times are simulated.
32 devices in a mesh: grp: 2 (over x), kv: 16 (over z, y, core).
Axes of the slice: x: 2, y: 2, z: 4, core: 2. Of those that a mesh axis runs over, the one named last changes fastest.
Arguments:
- queries: bfloat16 [8192, 640], P(('grp', 'kv')), parts along dimension 0, may hold values from -150 to 150
- ext_kv: bfloat16 [8192, 256], P(('grp', 'kv')), parts along dimension 0, may hold values from -6 to 6
- page_store: bfloat16 [64, 128, 1024], P(('grp', 'kv')), parts along dimension 0, may hold values from -6 to 6
- prefix_hidden: bfloat16 [32, 128, 5120], P(('grp', 'kv')), parts along dimension 0, may hold values from -6 to 6
- kv_weight: bfloat16 [5120, 1024], P('kv'), may hold values from -0.078125 to 0.078125
- kv_bias: bfloat16 [1024], replicated, may hold values from -3 to 3
- reuse: int32 [56, 3], P('grp'), parts along dimension 0, may hold values from 0 to 31, as said below
Outputs:
- attended: bfloat16 [8192, 640], P(('grp', 'kv')), parts along dimension 0
There are 2 independent parts, one for each index of `grp`. A program takes and returns all parts, laid end to end along the dimension named above; an argument that names none is the same for every part. Nothing has to cross between parts.
Inputs may be any that keep to these rules, and one draw needn't show every extreme that they name: `reuse`: row p describes prefix page p. Column 0 is 1 if the page is cached, else 0. For a cached page column 1 is the store slot holding it (device d holds store slots 2 * d to 2 * d + 1); for the others column 2 is the recompute slot whose hidden rows give it (device d holds recompute slot d). The other column of a row is a valid index with no meaning. No store slot and no recompute slot serves two pages. Every device holds at most 2 pages of the prefix in its store and recompute slots together, and some devices hold exactly 2.
All inputs are finite; a program needn't handle non-finite values.
Results may differ from a plain program's by a relative error of at most 0.012.
Values may be sent and summed in bfloat16 or wider, within the bound.
No kernel may reach another device: no remote copies, remote signals or barrier semaphores. Data moves between devices by JAX's collectives and lax.ppermute only.
A program may use at most 128 MiB of HBM per device.

v0:
```python
import jax
import jax.numpy as jnp
from jax import lax
from jax.sharding import PartitionSpec as P

GQ = 5
HEAD_DIM = 128


ROPE_BASE = 1000000.0
MASK_VALUE = -1e30


def shifted(value, axis, steps):
    count = lax.axis_size(axis)
    initial, last = (max(0, -steps), min(count, count - steps))
    return lax.ppermute(value, axis, [(source, source + steps) for source in range(initial, last)])


def rotate(vectors, positions):
    half_dim = vectors.shape[-1] // 2
    frequency = ROPE_BASE ** (-jnp.arange(half_dim, dtype=jnp.float32) * 2.0 / vectors.shape[-1])
    angles = positions.astype(jnp.float32)[:, None] * frequency[None, :]
    cosine = jnp.cos(angles)[:, None, :]
    sine_part = jnp.sin(angles)[:, None, :]
    leading = vectors[..., :half_dim]
    trailing = vectors[..., half_dim:]
    return jnp.concatenate(
        [leading * cosine - trailing * sine_part, trailing * cosine + leading * sine_part], axis=-1
    )


def absorb(softmax_state, rotated, key_rows, value_rows, visible):
    running_max, weight_sum, weighted = softmax_state
    scores = jnp.einsum(
        "tgd,kd->gtk", rotated, key_rows, preferred_element_type=jnp.float32
    ) * HEAD_DIM ** (-0.5)
    if visible is not None:
        scores = jnp.where(visible[None], scores, MASK_VALUE)
    new_max = jnp.maximum(running_max, jnp.max(scores, axis=-1))
    shrink = jnp.exp(running_max - new_max)
    weights = jnp.exp(scores - new_max[..., None])
    weight_sum = weight_sum * shrink + jnp.sum(weights, axis=-1)
    weighted = weighted * shrink[..., None] + jnp.einsum(
        "gtk,kd->gtd", weights.astype(jnp.bfloat16), value_rows, preferred_element_type=jnp.float32
    )
    return (new_max, weight_sum, weighted)


def spread_heads(local_pages, group_size):
    slot_count, page_rows, row_width = local_pages.shape
    head_count = row_width // (2 * HEAD_DIM)
    per_head = local_pages.reshape(slot_count, page_rows, head_count, 2 * HEAD_DIM).transpose(
        2, 0, 1, 3
    )
    copies = jnp.broadcast_to(
        per_head[:, None], (head_count, group_size, slot_count, page_rows, 2 * HEAD_DIM)
    )
    return copies.reshape(head_count * group_size * slot_count, page_rows, 2 * HEAD_DIM)


def on_device(queries, ext_kv, page_store, prefix_hidden, kv_weight, kv_bias, reuse):
    devices = lax.axis_size("kv")
    own_index = lax.axis_index("kv")
    row_count = queries.shape[0]
    head_count = kv_bias.shape[0] // (2 * HEAD_DIM)
    group_size = devices // head_count
    slice_index = own_index % group_size
    page_count = reuse.shape[0]
    store_count = page_store.shape[0]
    page_rows = page_store.shape[1]
    cached = reuse[:, 0] == 1
    store_match = cached[:, None] & (
        reuse[:, 1][:, None] == jnp.arange(devices * store_count, dtype=jnp.int32)[None, :]
    )
    fresh_match = jnp.logical_not(cached)[:, None] & (
        reuse[:, 2][:, None] == jnp.arange(devices, dtype=jnp.int32)[None, :]
    )
    live_slots = jnp.concatenate(
        [
            jnp.any(store_match, axis=0).reshape(devices, store_count),
            jnp.any(fresh_match, axis=0)[:, None],
        ],
        axis=1,
    )
    fresh_page = jnp.sum(
        jnp.where(fresh_match, jnp.arange(page_count, dtype=jnp.int32)[:, None], 0), axis=0
    )
    hidden_rows = prefix_hidden[0]
    row_width = kv_weight.shape[1]
    projected = jnp.dot(
        hidden_rows,
        lax.all_gather(kv_weight, "kv", axis=0, tiled=True),
        preferred_element_type=jnp.float32,
    )
    projected = (projected + kv_bias.astype(jnp.float32)).reshape(
        page_rows, head_count, 2, HEAD_DIM
    )
    positions = fresh_page[own_index] * page_rows + jnp.arange(page_rows, dtype=jnp.int32)
    recomputed = jnp.stack(
        [rotate(projected[:, :, 0, :], positions), projected[:, :, 1, :]], axis=2
    )
    recomputed = recomputed.reshape(page_rows, row_width).astype(jnp.bfloat16)
    local_pages = jnp.concatenate([page_store, recomputed[None]], axis=0)
    arrived = lax.all_to_all(
        spread_heads(local_pages, group_size), "kv", split_axis=0, concat_axis=0, tiled=True
    )
    live_flags = live_slots.reshape(-1)
    chosen = jnp.nonzero(live_flags, size=page_count, fill_value=0)[0]
    prefix_rows = jnp.take(arrived, chosen, axis=0).reshape(page_count * page_rows, 2 * HEAD_DIM)
    offset = page_count * page_rows
    query_pos = slice_index * row_count + jnp.arange(row_count, dtype=jnp.int32)
    rotated = rotate(
        queries.reshape(row_count, GQ, HEAD_DIM).astype(jnp.float32), offset + query_pos
    ).astype(jnp.bfloat16)
    own_keys = rotate(ext_kv[:, None, :HEAD_DIM].astype(jnp.float32), offset + query_pos)[
        :, 0, :
    ].astype(jnp.bfloat16)
    own_block = jnp.concatenate([own_keys, ext_kv[:, HEAD_DIM:]], axis=1)
    softmax_state = (
        jnp.full((GQ, row_count), MASK_VALUE, jnp.float32),
        jnp.zeros((GQ, row_count), jnp.float32),
        jnp.zeros((GQ, row_count, HEAD_DIM), jnp.float32),
    )
    key_span = 4 * page_rows

    def prefix_step(step_index, inner_state):
        key_block = lax.dynamic_slice_in_dim(prefix_rows, step_index * key_span, key_span, 0)
        return absorb(inner_state, rotated, key_block[:, :HEAD_DIM], key_block[:, HEAD_DIM:], None)

    softmax_state = lax.fori_loop(0, page_count // 4, prefix_step, softmax_state)
    diagonal = jnp.arange(row_count)[None, :] <= jnp.arange(row_count)[:, None]
    softmax_state = absorb(
        softmax_state, rotated, own_block[:, :HEAD_DIM], own_block[:, HEAD_DIM:], diagonal
    )

    def pass_step(step_index, carried):
        key_block, inner_state = carried
        key_block = shifted(key_block, "kv", 1)

        def take_block(current):
            return absorb(current, rotated, key_block[:, :HEAD_DIM], key_block[:, HEAD_DIM:], None)

        def keep_block(current):
            return current

        inner_state = lax.cond(step_index <= slice_index, take_block, keep_block, inner_state)
        return (key_block, inner_state)

    softmax_state = lax.fori_loop(1, group_size, pass_step, (own_block, softmax_state))[1]
    running_max, weight_sum, weighted = softmax_state
    normed = weighted / weight_sum[..., None]
    return normed.transpose(1, 0, 2).reshape(row_count, GQ * HEAD_DIM).astype(jnp.bfloat16)


def solution(mesh):
    placed = (
        P(("grp", "kv"), None),
        P(("grp", "kv"), None),
        P(("grp", "kv"), None, None),
        P(("grp", "kv"), None, None),
        P("kv", None),
        P(),
        P("grp", None),
    )
    return jax.shard_map(
        on_device, mesh=mesh, in_specs=placed, out_specs=P(("grp", "kv"), None), check_vma=False
    )
```

profile of v0, /device:TPU:5, one launch (start us, length us, event | category | flops | bytes accessed | tf_op | source)
XLA Modules:
  0.0 246.7 jit_solution(18152996083247242103)
XLA Ops:
  6.5 0.7 all-gather.2.cloned.1.call-update
  7.3 0.7 convert_element_type.101
  7.9 1.4 concatenate.27
  9.4 0.7 compare_bitcast_fusion
  10.1 0.8 slice_bitcast_fusion.1
  12.5 85.7 %all-gather.2.cloned.1.call-done = bf16[5120,1024]{1,0:T(8,128)(2,1)} async-done(((bf16[320,1024]{1,0:T(8,128)(2,1)}), bf16[5120,1024]{1,0:T(8,128)(2,1)}) %all-gather.2.cloned.1.call-update) | async-done | bytes 10485776 | tf_op jit(solution)/shard_map/all_gather | solution.py:93
  98.3 5.5 %fusion.27 = f32[128,1024]{1,0:T(8,128)S(1)} fusion(bf16[5120,1024]{1,0:T(8,128)(2,1)} %all-gather.2.cloned.1.call-done, bf16[1,128,5120]{2,1,0:T(8,128)(2,1)S(1)} %copy-done, f32[1024]{0:T(1024)S(1)} %convert_element_type.101), kind=kOutput, calls=%fused_computation.42 | convolution fusion | flops 1342308352 | bytes 12324864 | tf_op jit(solution)/shard_map/dot_general | solution.py:91
  106.1 2.1 broadcast_in_dim.116
  108.2 5.7 %all-to-all-start = ((bf16[48,128,256]{2,1,0:T(8,128)(2,1)}), bf16[48,128,256]{2,1,0:T(8,128)(2,1)}, u32[]{:S(2)}, u32[]{:S(2)}) async-start(bf16[48,128,256]{2,1,0:T(8,128)(2,1)} %bitcast.99), calls=%async_computation | async-start | bytes 6291456 | tf_op jit(solution)/shard_map/all_to_all | solution.py:105
  114.7 1.0 scatter_custom_fusion
  116.6 0.8 copy.100
  117.5 0.8 fusion.58
  118.5 1.2 copy.113
  119.8 0.6 fusion.55
  120.4 0.8 remainder_reduce_fusion
  122.1 0.7 compare_and_fusion
  122.9 1.5 fusion.60
  124.3 52.5 %all-to-all-done = bf16[48,128,256]{2,1,0:T(8,128)(2,1)} async-done(((bf16[48,128,256]{2,1,0:T(8,128)(2,1)}), bf16[48,128,256]{2,1,0:T(8,128)(2,1)}, u32[]{:S(2)}, u32[]{:S(2)}) %all-to-all-start) | async-done | bytes 3145760 | tf_op jit(solution)/shard_map/all_to_all | solution.py:105
  176.9 3.8 %gather_fusion = bf16[28,128,256]{2,1,0:T(8,128)(2,1)} fusion(bf16[48,128,256]{2,1,0:T(8,128)(2,1)} %all-to-all-done, s32[1024]{0:T(1024)S(1)} %pad_clamp_fusion), kind=kCustom, calls=%fused_computation | custom fusion | bytes 3670128 | tf_op jit(solution)/shard_map/jit(_take)/gather | solution.py:110
  180.7 3.9 %bitcast_select_fusion = bf16[3584,256]{1,0:T(8,128)(2,1)} fusion(bf16[28,128,256]{2,1,0:T(8,128)(2,1)} %gather_fusion, pred[3584]{0:T(1024)(128)(4,1)S(1)} %broadcast_bitcast_fusion), kind=kLoop, calls=%fused_computation.34 | loop fusion | flops 917504 | bytes 3673600 | tf_op jit(solution)/shard_map/jit(_take)/select_n | solution.py:110
  184.7 25.3 %while.38 = (s32[]{:T(128)}, f32[5,256]{1,0:T(8,128)S(1)}, f32[5,256]{1,0:T(8,128)S(1)}, f32[5,256,128]{2,1,0:T(8,128)S(1)}, bf16[3584,256]{1,0:T(8,128)(2,1)}, ...) while((s32[]{:T(128)}, f32[5,256]{1,0:T(8,128)S(1)}, ...), condition=%wide.region_10.11_spmd.clone, body=%wide.region_7.10_spmd.clone.sunk | while | flops 341285120 | bytes 9846983 | solution.py:131
  184.7 1.4 bitcast_reduce_fusion.2
  186.6 1.7 fusion.74
  188.3 1.4 bitcast_reduce_fusion.2
  190.2 1.7 fusion.74
  191.9 1.4 bitcast_reduce_fusion.2
  193.8 1.7 fusion.74
  195.5 1.4 bitcast_reduce_fusion.2
  197.4 1.7 fusion.74
  199.1 1.4 bitcast_reduce_fusion.2
  201.0 1.7 fusion.74
  202.8 1.4 bitcast_reduce_fusion.2
  204.7 1.7 fusion.74
  206.4 1.4 bitcast_reduce_fusion.2
  208.3 1.7 fusion.74
  210.0 1.6 fusion.31
  212.3 26.3 %while.37 = (s32[]{:T(128)}, bf16[256,256]{1,0:T(8,128)(2,1)S(1)}, f32[5,256]{1,0:T(8,128)S(1)}, f32[5,256]{1,0:T(8,128)S(1)}, f32[5,256,128]{2,1,0:T(8,128)S(1)...) while((s32[]{:T(128)}, bf16[256,256]{1,0:T(8,128)(2,1)S(1)}, f32[5,256]{1,0:T(8,128)S(1)}, ...), condition=%wide.region_18.19_spmd, body=%wide.region_13.18_spmd.sunk | while | flops 170068480 | bytes 6576363 | solution.py:150
  212.3 8.7 %collective-permute-start = (bf16[256,256]{1,0:T(8,128)(2,1)S(1)}, bf16[256,256]{1,0:T(8,128)(2,1)S(1)}, u32[]{:S(2)}, u32[]{:S(2)}) collective-permute-start(bf16[256,256]{1,0:T(8,128)(2,1)S(1)} %get-tuple-element.504), channel_id=1, source_target_pairs={{0,1},{1,2},{2,3},{3,4},{4,5},{5,6},{6,7},{7,8},{8,9},{9,10},{10,1... | collective-permute-start | bytes 393224 | tf_op jit(solution)/shard_map/while/body/eval_jaxpr/ppermute | solution.py:17
  221.1 1.9 collective-permute-done
  223.0 1.2 conditional.2
  224.2 4.0 %collective-permute-start = (bf16[256,256]{1,0:T(8,128)(2,1)S(1)}, bf16[256,256]{1,0:T(8,128)(2,1)S(1)}, u32[]{:S(2)}, u32[]{:S(2)}) collective-permute-start(bf16[256,256]{1,0:T(8,128)(2,1)S(1)} %get-tuple-element.504), channel_id=1, source_target_pairs={{0,1},{1,2},{2,3},{3,4},{4,5},{5,6},{6,7},{7,8},{8,9},{9,10},{10,1... | collective-permute-start | bytes 393224 | tf_op jit(solution)/shard_map/while/body/eval_jaxpr/ppermute | solution.py:17
  228.3 1.9 collective-permute-done
  230.2 1.2 conditional.2
  230.8 0.6 convolution_add_fusion
  231.5 4.0 %collective-permute-start = (bf16[256,256]{1,0:T(8,128)(2,1)S(1)}, bf16[256,256]{1,0:T(8,128)(2,1)S(1)}, u32[]{:S(2)}, u32[]{:S(2)}) collective-permute-start(bf16[256,256]{1,0:T(8,128)(2,1)S(1)} %get-tuple-element.504), channel_id=1, source_target_pairs={{0,1},{1,2},{2,3},{3,4},{4,5},{5,6},{6,7},{7,8},{8,9},{9,10},{10,1... | collective-permute-start | bytes 393224 | tf_op jit(solution)/shard_map/while/body/eval_jaxpr/ppermute | solution.py:17
  235.5 1.9 collective-permute-done
  237.4 1.2 conditional.2
  239.0 0.9 copy.102
  (112 shorter events, 13.3 us)
Async XLA Ops:
  6.5 91.7 %copy-start = (bf16[1,128,5120]{2,1,0:T(8,128)(2,1)S(1)}, bf16[1,128,5120]{2,1,0:T(8,128)(2,1)}, u32[]{:S(2)}) copy-start(bf16[1,128,5120]{2,1,0:T(8,128)(2,1)} %param.16) | copy-start | bytes 3932164
  6.5 91.7 %all-gather.2.cloned.1.call-start = ((), (), s32[]{:S(2)}) async-start(), calls=%async_computation.1 | async-start | bytes 11141120 | tf_op jit(solution)/shard_map/all_gather | solution.py:93
  108.2 7.8 %copy-start.3 = (bf16[256,256]{1,0:T(8,128)(2,1)S(1)}, bf16[256,256]{1,0:T(8,128)(2,1)}, u32[]{:S(2)}) copy-start(bf16[256,256]{1,0:T(8,128)(2,1)} %param.14) | copy-start | bytes 393220
  108.2 68.7 %all-to-all-start = ((bf16[48,128,256]{2,1,0:T(8,128)(2,1)}), bf16[48,128,256]{2,1,0:T(8,128)(2,1)}, u32[]{:S(2)}, u32[]{:S(2)}) async-start(bf16[48,128,256]{2,1,0:T(8,128)(2,1)} %bitcast.99), calls=%async_computation | async-start | bytes 6291456 | tf_op jit(solution)/shard_map/all_to_all | solution.py:105
  113.9 3.4 %copy-start.2 = (bf16[256,640]{1,0:T(8,128)(2,1)S(1)}, bf16[256,640]{1,0:T(8,128)(2,1)}, u32[]{:S(2)}) copy-start(bf16[256,640]{1,0:T(8,128)(2,1)} %param.13) | copy-start | bytes 983044
  210.0 1.7 copy-start.1
  210.0 2.3 copy-start.4
  212.3 10.7 %collective-permute-start = (bf16[256,256]{1,0:T(8,128)(2,1)S(1)}, bf16[256,256]{1,0:T(8,128)(2,1)S(1)}, u32[]{:S(2)}, u32[]{:S(2)}) collective-permute-start(bf16[256,256]{1,0:T(8,128)(2,1)S(1)} %get-tuple-element.504), channel_id=1, source_target_pairs={{0,1},{1,2},{2,3},{3,4},{4,5},{5,6},{6,7},{7,8},{8,9},{9,10},{10,1... | collective-permute-start | bytes 393224 | tf_op jit(solution)/shard_map/while/body/eval_jaxpr/ppermute | solution.py:17
  224.2 6.0 %collective-permute-start = (bf16[256,256]{1,0:T(8,128)(2,1)S(1)}, bf16[256,256]{1,0:T(8,128)(2,1)S(1)}, u32[]{:S(2)}, u32[]{:S(2)}) collective-permute-start(bf16[256,256]{1,0:T(8,128)(2,1)S(1)} %get-tuple-element.504), channel_id=1, source_target_pairs={{0,1},{1,2},{2,3},{3,4},{4,5},{5,6},{6,7},{7,8},{8,9},{9,10},{10,1... | collective-permute-start | bytes 393224 | tf_op jit(solution)/shard_map/while/body/eval_jaxpr/ppermute | solution.py:17
  231.5 6.0 %collective-permute-start = (bf16[256,256]{1,0:T(8,128)(2,1)S(1)}, bf16[256,256]{1,0:T(8,128)(2,1)S(1)}, u32[]{:S(2)}, u32[]{:S(2)}) collective-permute-start(bf16[256,256]{1,0:T(8,128)(2,1)S(1)} %get-tuple-element.504), channel_id=1, source_target_pairs={{0,1},{1,2},{2,3},{3,4},{4,5},{5,6},{6,7},{7,8},{8,9},{9,10},{10,1... | collective-permute-start | bytes 393224 | tf_op jit(solution)/shard_map/while/body/eval_jaxpr/ppermute | solution.py:17
Sparse Core Ops, SparseCore 0:
  9.6 88.5 all-gather.1
where the time goes:
time: 250 us; the launch traced here: 247 us
  waiting for transfers between devices  145 us (58%)
  matrix products  32.1 us (13%)
  starting transfers between devices  22.5 us (9%)
  other arithmetic  17 us (7%)
  local copies, waits for them, and re-layouts  15.2 us (6%)
  between operations  14.5 us (6%)
    all_gather x1, waiting for transfers between devices, on_device(): lax.all_gather(kv_weight, 'kv', axis=0, tiled=True)  85.7 us
    all_to_all x1, waiting for transfers between devices, on_device(): lax.all_to_all(spread_heads(local_pages, group_size), 'kv', split_axis=0,...  52.5 us
    ppermute x3, starting transfers between devices, shifted(): lax.ppermute(value, axis, [(source, source + steps) for source in range(i...  16.8 us
    dot_general x11, matrix products, absorb(): jnp.einsum('gtk,kd->gtd', weights.astype(jnp.bfloat16), value_rows, prefe...  14.2 us
    dot_general x11, matrix products, absorb(): jnp.einsum('tgd,kd->gtk', rotated, key_rows, preferred_element_type=jnp.f...  12.4 us
    ppermute x3, waiting for transfers between devices, shifted(): lax.ppermute(value, axis, [(source, source + steps) for source in range(i...  5.76 us
    all_to_all x1, starting transfers between devices, on_device(): lax.all_to_all(spread_heads(local_pages, group_size), 'kv', split_axis=0,...  5.71 us
    dot_general x1, matrix products, on_device(): jnp.dot(hidden_rows, lax.all_gather(kv_weight, 'kv', axis=0, tiled=True),...  5.5 us
  transfers between devices with their start and end apart: 5, of which 5 were waited for; matrix products, arithmetic and copies ran while one was open for 6% of the time, Pallas kernels for 0%

commit v1 on v0

v1 whole, which is shorter than its diff:
```python
import functools

import jax
import jax.numpy as jnp
from jax import lax
from jax.experimental import pallas as pl
from jax.experimental.pallas import tpu as pltpu
from jax.sharding import PartitionSpec as P

GQ = 5
HEAD_DIM = 128
PAIR = 2 * HEAD_DIM
HEADS = 4

ROPE_BASE = 1000000.0
MASK_VALUE = -1e30


def swap(value, axis, bit, count):
    return lax.ppermute(value, axis, [(i, i ^ bit) for i in range(count)])


def angle_tables(positions):
    half_dim = HEAD_DIM // 2
    frequency = ROPE_BASE ** (-jnp.arange(half_dim, dtype=jnp.float32) * 2.0 / HEAD_DIM)
    angles = positions.astype(jnp.float32)[..., None] * frequency
    cosine = jnp.cos(angles)
    sine = jnp.sin(angles)
    return (
        jnp.concatenate([cosine, cosine], axis=-1),
        jnp.concatenate([-sine, sine], axis=-1),
    )


def project_kernel(blocks, meta, *refs):
    pages, weights = refs[:4], refs[4:-6]
    bias, cosine, sine, out_first, out_second, total = refs[-6:]
    rows = cosine.shape[1]
    span = pages[0].shape[2] // blocks
    single = len(weights) == 1

    for block in range(blocks):
        chip = block if single else meta[2 + block]
        start = pl.multiple_of(chip * span, HEAD_DIM)
        left = jnp.concatenate([page[0, :, pl.ds(start, span)] for page in pages], axis=0)
        right = weights[0][pl.ds(block * span, span)] if single else weights[block][...]
        product = jnp.dot(left, right, preferred_element_type=jnp.float32)
        total[...] = product + (bias[...] if block == 0 else total[...])
    for out, place in ((out_first, 0), (out_second, 1)):
        base = meta[place] * 2
        for rel in range(2):
            page = total[pl.ds(pl.multiple_of((base + rel) * rows, rows), rows)]
            keys = page[:, :HEAD_DIM]
            turned = keys * cosine[base + rel] + pltpu.roll(keys, HEAD_DIM // 2, 1) * sine[
                base + rel
            ]
            out[rel, :, :HEAD_DIM] = turned.astype(jnp.bfloat16)
            out[rel, :, HEAD_DIM:] = page[:, HEAD_DIM:].astype(jnp.bfloat16)


def project(meta, pages, weights, bias, cosine, sine):
    rows, depth = pages[0].shape[1:]
    width = weights[0].shape[1]
    in_smem = pl.BlockSpec(memory_space=pltpu.SMEM)
    in_vmem = pl.BlockSpec(memory_space=pltpu.VMEM)
    return pl.pallas_call(
        functools.partial(project_kernel, 8),
        in_specs=[in_smem] + [in_vmem] * (4 + len(weights) + 3),
        out_specs=[in_vmem] * 2,
        out_shape=[jax.ShapeDtypeStruct((2, rows, width), jnp.bfloat16)] * 2,
        scratch_shapes=[pltpu.VMEM((4 * rows, width), jnp.float32)],
        compiler_params=pltpu.CompilerParams(vmem_limit_bytes=24 << 20),
        cost_estimate=pl.CostEstimate(
            flops=2 * 4 * rows * depth * width,
            bytes_accessed=2 * (4 * rows + width) * depth,
            transcendentals=0,
        ),
        name="project",
    )(meta, *pages, *weights, bias, cosine, sine)


def fold(query_ref, rows, top_ref, sum_ref, mask=None, first=False):
    key_rows, value_rows = rows[:, :HEAD_DIM], rows[:, HEAD_DIM:]
    copies = rows.shape[0] // HEAD_DIM
    extended = jnp.concatenate([value_rows, jnp.ones_like(value_rows)], axis=1)

    def scores_of(group):
        scores = lax.dot_general(
            query_ref[group],
            key_rows,
            (((1,), (1,)), ((), ())),
            preferred_element_type=jnp.float32,
        )
        return scores if mask is None else jnp.where(mask, scores, MASK_VALUE)

    ahead = scores_of(0)
    for group in range(GQ):
        scores = ahead
        if group + 1 < GQ:
            ahead = scores_of(group + 1)
        row_top = jnp.broadcast_to(
            jnp.max(scores, axis=1, keepdims=True), (scores.shape[0], HEAD_DIM)
        )
        if not first:
            old_top = top_ref[group]
            row_top = jnp.maximum(old_top, row_top)
        weights = jnp.exp(scores - jnp.concatenate([row_top] * copies, axis=1))
        product = jnp.dot(
            weights.astype(jnp.bfloat16), extended, preferred_element_type=jnp.float32
        )
        if not first:
            shrink = jnp.exp(old_top - row_top)
            product += sum_ref[group] * jnp.concatenate([shrink, shrink], axis=1)
        sum_ref[group] = product
        top_ref[group] = row_top


def fold_pages(query_ref, buffer, wait_page, count, top_ref, sum_ref):
    def part(start, size):
        for offset in range(size):
            wait_page(start + offset)
        rows = buffer[pl.ds(start, size)].reshape(size * buffer.shape[1], PAIR)
        fold(query_ref, rows, top_ref, sum_ref)

    full = count // 4

    def body(index, carry):
        part(index * 4, 4)
        return carry

    lax.fori_loop(0, full, body, 0)

    @pl.when((count & 2) != 0)
    def _():
        part(full * 4, 2)

    @pl.when((count & 1) != 0)
    def _():
        part(count - 1, 1)


def start_pages(reuse, flag, place, pieces, buffer, semaphores):
    page_count = reuse.shape[0]

    def body(page, count):
        chosen = reuse[page, 0] == flag

        @pl.when(chosen)
        def _():
            piece, index = place(reuse[page, 2 - flag])
            for number, source in enumerate(pieces):

                @pl.when(piece == number)
                def _():
                    pltpu.make_async_copy(
                        source.at[index], buffer.at[count], semaphores.at[count]
                    ).start()

        return count + chosen.astype(jnp.int32)

    return lax.fori_loop(0, page_count, body, jnp.int32(0))


def early_kernel(place, extension_at, count, slots, reuse, meta, query, cosine, sine, *refs):
    pieces = refs[:count]
    turned, top_ref, sum_ref, buffer, blocks, semaphores, block_semaphores = refs[count:]
    group_size, pages_each = blocks.shape[0], blocks.shape[1]
    slice_index = meta[1]

    def block_copy(relative):
        piece, index = extension_at(relative)
        return pltpu.make_async_copy(
            pieces[piece].at[pl.ds(index, pages_each)],
            blocks.at[relative],
            block_semaphores.at[relative],
        )

    for relative in range(group_size):
        block_copy(relative).start()
    found = start_pages(
        reuse, 1, functools.partial(place, slots, meta), pieces, buffer, semaphores
    )
    scale = HEAD_DIM**-0.5
    cos_rows, sin_rows = cosine[...], sine[...]
    for group in range(GQ):
        values = query[:, group * HEAD_DIM : (group + 1) * HEAD_DIM].astype(jnp.float32)
        rotated = values * cos_rows + pltpu.roll(values, HEAD_DIM // 2, 1) * sin_rows
        turned[group] = (rotated * scale).astype(jnp.bfloat16)

    row_count = query.shape[0]
    rows = lax.broadcasted_iota(jnp.int32, (row_count, row_count), 0)
    columns = lax.broadcasted_iota(jnp.int32, (row_count, row_count), 1)

    def attend(index, **options):
        fold(turned, blocks[index].reshape(row_count, PAIR), top_ref, sum_ref, **options)

    for relative in range(group_size):
        block_copy(relative).wait()
    attend(0, mask=columns <= rows, first=True)

    def earlier(index, carry):
        attend(index ^ slice_index)
        return carry

    lax.fori_loop(0, slice_index, earlier, 0)

    def wait_page(index):
        pltpu.make_async_copy(pieces[0].at[0], buffer.at[index], semaphores.at[index]).wait()

    fold_pages(turned, buffer, wait_page, found, top_ref, sum_ref)


def attend_early(
    place, extension_at, group_size, slots, reuse, meta, queries, row_cos, row_sin, pieces
):
    page_count, row_count, page_rows = reuse.shape[0], queries.shape[0], pieces[0].shape[1]
    in_smem = pl.BlockSpec(memory_space=pltpu.SMEM)
    in_vmem = pl.BlockSpec(memory_space=pltpu.VMEM)
    anywhere = pl.BlockSpec(memory_space=pl.ANY)
    shape = (GQ, row_count, HEAD_DIM)
    work = GQ * row_count * page_count * page_rows
    return pl.pallas_call(
        functools.partial(early_kernel, place, extension_at, len(pieces), slots),
        in_specs=[in_smem] * 2 + [in_vmem] * 3 + [anywhere] * len(pieces),
        out_specs=[in_vmem] * 3,
        out_shape=[
            jax.ShapeDtypeStruct(shape, jnp.bfloat16),
            jax.ShapeDtypeStruct(shape, jnp.float32),
            jax.ShapeDtypeStruct((GQ, row_count, PAIR), jnp.float32),
        ],
        scratch_shapes=[
            pltpu.VMEM((page_count, page_rows, PAIR), jnp.bfloat16),
            pltpu.VMEM((group_size, row_count // page_rows, page_rows, PAIR), jnp.bfloat16),
            pltpu.SemaphoreType.DMA((page_count,)),
            pltpu.SemaphoreType.DMA((group_size,)),
        ],
        compiler_params=pltpu.CompilerParams(vmem_limit_bytes=24 << 20),
        cost_estimate=pl.CostEstimate(
            flops=4 * work * HEAD_DIM,
            bytes_accessed=page_rows * page_count * PAIR * 2,
            transcendentals=work,
        ),
        name="early",
    )(reuse, meta, queries, row_cos, row_sin, *pieces)


def place_spread(group_size, slots, meta, slot):
    device = slot // slots
    return meta[1] ^ (device % group_size), device // group_size * slots + slot % slots


def place_apart(slots, meta, slot):
    device = slot // slots
    source, relative = device // 4, meta[1] ^ (device % 4)
    shift = (meta[0] - source) & 3
    return (relative & 1) * 2 + (relative >> 1), (shift ^ (shift >> 1)) * slots + slot % slots


def fresh_place(group_size, meta, device):
    source, spot = device // group_size, device % group_size
    holder = (spot - (spot & 1)) + (source & 1)
    index = ((source >> 1) ^ meta[2]) * 2 + ((spot ^ meta[0]) & 1)
    return meta[1] ^ holder, index


def late_kernel(group_size, reuse, meta, turned, top_in, sum_in, *refs):
    pieces = refs[:group_size]
    out, top_ref, sum_ref, buffer, semaphores = refs[group_size:]
    place = functools.partial(fresh_place, group_size, meta)
    count = start_pages(reuse, 0, place, pieces, buffer, semaphores)
    top_ref[...] = jnp.full_like(top_ref, MASK_VALUE)
    sum_ref[...] = jnp.zeros_like(sum_ref)

    def wait_page(index):
        pltpu.make_async_copy(pieces[0].at[0], buffer.at[index], semaphores.at[index]).wait()

    fold_pages(turned, buffer, wait_page, count, top_ref, sum_ref)
    for group in range(GQ):
        first_top, last_top = top_in[group], top_ref[group]
        row_top = jnp.maximum(first_top, last_top)
        first_share, last_share = jnp.exp(first_top - row_top), jnp.exp(last_top - row_top)
        total = sum_in[group] * jnp.concatenate([first_share, first_share], axis=1)
        total += sum_ref[group] * jnp.concatenate([last_share, last_share], axis=1)
        out[:, group * HEAD_DIM : (group + 1) * HEAD_DIM] = (
            total[:, :HEAD_DIM] / total[:, HEAD_DIM:]
        ).astype(out.dtype)


def attend_late(reuse, meta, turned, top, total, pieces):
    page_count, row_count, page_rows = reuse.shape[0], turned.shape[1], pieces[0].shape[1]
    group_size = len(pieces)
    most = min(page_count, group_size * pieces[0].shape[0])
    in_smem = pl.BlockSpec(memory_space=pltpu.SMEM)
    in_vmem = pl.BlockSpec(memory_space=pltpu.VMEM)
    anywhere = pl.BlockSpec(memory_space=pl.ANY)
    work = GQ * row_count * page_rows * page_count // 2
    return pl.pallas_call(
        functools.partial(late_kernel, group_size),
        in_specs=[in_smem] * 2 + [in_vmem] * 3 + [anywhere] * group_size,
        out_specs=in_vmem,
        out_shape=jax.ShapeDtypeStruct((row_count, GQ * HEAD_DIM), jnp.bfloat16),
        scratch_shapes=[
            pltpu.VMEM(top.shape, top.dtype),
            pltpu.VMEM(total.shape, total.dtype),
            pltpu.VMEM((most, page_rows, PAIR), jnp.bfloat16),
            pltpu.SemaphoreType.DMA((most,)),
        ],
        compiler_params=pltpu.CompilerParams(vmem_limit_bytes=24 << 20),
        cost_estimate=pl.CostEstimate(
            flops=4 * work * HEAD_DIM,
            bytes_accessed=page_rows * page_count * PAIR,
            transcendentals=work,
        ),
        name="late",
    )(reuse, meta, turned, top, total, *pieces)


def on_device(parts, queries, ext_kv, page_store, prefix_hidden, kv_weight, kv_bias, reuse):
    devices = lax.axis_size("kv")
    own_index = lax.axis_index("kv")
    part_index = lax.axis_index("grp")
    row_count = queries.shape[0]
    group_size = devices // HEADS
    group_bits = group_size.bit_length() - 1
    head = own_index >> group_bits
    slice_index = own_index & (group_size - 1)
    core = own_index & 1
    side = part_index & 1
    page_count = reuse.shape[0]
    slots, page_rows = page_store.shape[0], page_store.shape[1]

    def exchange(value, bit):
        return swap(value, "kv", bit, devices)

    def between_planes(value):
        groups = [list(range(spot, devices, group_size)) for spot in range(group_size)]
        return lax.all_to_all(value, "kv", 0, 0, axis_index_groups=groups, tiled=True)

    hidden_across = swap(prefix_hidden, "grp", 1, parts)

    target = 2 * side + core
    spare = 2 * side + (1 - core)
    mine = lax.dynamic_slice_in_dim(kv_weight, target * PAIR, PAIR, 1)
    other = exchange(lax.dynamic_slice_in_dim(kv_weight, spare * PAIR, PAIR, 1), 1)
    chip_rows = jnp.where(
        core == 0,
        jnp.concatenate([mine, other], axis=0),
        jnp.concatenate([other, mine], axis=0),
    )

    def as_pages(*blocks):
        return jnp.concatenate(blocks, axis=0).reshape(-1, page_rows, PAIR)

    def stored_for(store, plane):
        part = lax.dynamic_slice_in_dim(store, plane * PAIR, PAIR, 2)
        return part.reshape(slots * page_rows, PAIR)

    order = []
    if group_size == 4:
        def to_plane(value, shift):
            step = shift * group_size
            return lax.ppermute(value, "kv", [(i, (i + step) % devices) for i in range(devices)])

        own_part = stored_for(page_store, head)
        others = [
            to_plane(stored_for(page_store, (head + shift) & (HEADS - 1)), shift)
            for shift in (1, 3, 2)
        ]
        near = to_plane(chip_rows, 1)
        again, others = lax.optimization_barrier((chip_rows, others))
        back = to_plane(again, 3)
        beside_own = exchange(chip_rows, 2)
        far = to_plane(near, 1)
        near_sent, _ = lax.optimization_barrier((near, beside_own))
        beside_near = exchange(near_sent, 2)
        back_sent, _ = lax.optimization_barrier((back, beside_near))
        beside_back = exchange(back_sent, 2)
        far_sent, hidden_mine, hidden_passed, reuse_sent, _ = lax.optimization_barrier(
            (far, prefix_hidden, hidden_across, reuse, beside_back)
        )
        hidden_core = exchange(hidden_mine, 1)
        beside_far = exchange(far_sent, 2)
        weights = [chip_rows, beside_own, near, beside_near, back, beside_back, far, beside_far]
        for shift in (0, 1, 3, 2):
            chip = (((head - shift) & (HEADS - 1)) << 1) | (slice_index >> 1)
            order += [chip, chip ^ 1]
    else:
        hidden_core, hidden_passed, reuse_sent = exchange(prefix_hidden, 1), hidden_across, reuse
        weights = [
            lax.all_gather(
                chip_rows,
                "kv",
                axis=0,
                tiled=True,
                axis_index_groups=[list(range(first, devices, 2)) for first in range(2)],
            )
        ]
    hidden_diagonal = exchange(hidden_passed, 1)
    reuse_across = swap(reuse_sent, "grp", 1, parts)
    offset = page_count * page_rows
    (ext_kv, first_row), _ = lax.optimization_barrier(
        ((ext_kv, slice_index * row_count), weights[min(2, len(weights) - 1)])
    )
    query_pos = offset + first_row + jnp.arange(row_count, dtype=jnp.int32)
    row_cos, row_sin = angle_tables(query_pos)
    raw_keys = ext_kv[:, :HEAD_DIM].astype(jnp.float32)
    own_keys = raw_keys * row_cos + jnp.roll(raw_keys, HEAD_DIM // 2, axis=1) * row_sin
    own_block = jnp.concatenate([own_keys.astype(jnp.bfloat16), ext_kv[:, HEAD_DIM:]], axis=1)

    if group_size == 4:
        gathered, beside_far = lax.optimization_barrier(
            (as_pages(own_part, *others, own_block), weights[-1])
        )
        gathered_beside = exchange(gathered, 2)

    def page_numbers(table):
        match = (table[:, 0] == 0)[:, None] & (
            table[:, 2][:, None] == jnp.stack([own_index, own_index ^ 1])[None, :]
        )
        return jnp.sum(
            jnp.where(match, jnp.arange(page_count, dtype=jnp.int32)[:, None], 0), axis=0
        )

    numbers = jnp.concatenate([page_numbers(reuse), page_numbers(reuse_across)])
    page_cos, page_sin = angle_tables(
        numbers[:, None] * page_rows + jnp.arange(page_rows, dtype=jnp.int32)[None, :]
    )

    bias = lax.dynamic_slice_in_dim(kv_bias, target * PAIR, PAIR, 0).astype(jnp.float32)[None, :]
    first_side = (head >> 1) ^ side
    choice = jnp.stack([first_side, first_side ^ 1] + order).astype(jnp.int32)
    messages = project(
        choice,
        (prefix_hidden, hidden_core, hidden_across, hidden_diagonal),
        weights,
        bias,
        page_cos,
        page_sin,
    )
    received = []
    for turn, message in enumerate(messages):
        routes = []
        for part in range(parts):
            for device in range(devices):
                plane, spot = device // group_size, device % group_size
                to_part = (part & ~1) | ((plane >> 1) ^ turn)
                to_spot = (spot & ~1) | (plane & 1)
                to_head = 2 * (part & 1) + (spot & 1)
                routes.append(
                    (part * devices + device, to_part * devices + to_head * group_size + to_spot)
                )
        received.append(lax.ppermute(message, ("grp", "kv"), routes))
    meta = jnp.stack([head, slice_index, side]).astype(jnp.int32)
    bits = []
    while 1 << len(bits) < group_size:
        bits.insert(0, 1 << len(bits))

    def spread(own, first):
        pieces = {0: own, bits[0]: first}
        for bit in bits[1:]:
            pieces.update({known ^ bit: exchange(value, bit) for known, value in pieces.items()})
        return [pieces[relative] for relative in range(group_size)]

    if group_size == 4:
        pieces, _ = lax.optimization_barrier(([gathered, gathered_beside], received))
        pieces += [exchange(piece, 1) for piece in pieces]
        place = place_apart
        extension_at = lambda relative: ((relative & 1) * 2 + (relative >> 1), HEADS * slots)
    else:
        per_head = page_store.reshape(slots, page_rows, HEADS, PAIR).transpose(2, 0, 1, 3)
        arrived = between_planes(per_head.reshape(HEADS * slots, page_rows, PAIR))
        gathered = as_pages(arrived.reshape(-1, PAIR), own_block)
        pieces = spread(gathered, exchange(gathered, bits[0]))
        place = functools.partial(place_spread, group_size)
        extension_at = lambda relative: (relative, HEADS * slots)
    turned, top, total = attend_early(
        place, extension_at, group_size, slots, reuse, meta, queries, row_cos, row_sin, pieces
    )
    late_own = jnp.concatenate(received, axis=0)
    late_first = exchange(late_own, bits[0])
    late_first, turned = lax.optimization_barrier((late_first, turned))
    late_pieces = spread(late_own, late_first)
    return attend_late(reuse, meta, turned, top, total, late_pieces)


def solution(mesh):
    placed = (
        P(("grp", "kv"), None),
        P(("grp", "kv"), None),
        P(("grp", "kv"), None, None),
        P(("grp", "kv"), None, None),
        P("kv", None),
        P(),
        P("grp", None),
    )
    return jax.shard_map(
        functools.partial(on_device, mesh.shape["grp"]),
        mesh=mesh,
        in_specs=placed,
        out_specs=P(("grp", "kv"), None),
        check_vma=False,
    )
```

time: 250 us -> 107 us (0.43); the launches traced: 247 us -> 106 us
  waiting for transfers between devices: 145 us -> 41.9 us
  matrix products: 32.1 us -> 0 us
  Pallas kernels: 0 us -> 20.9 us
  between operations: 14.5 us -> 0.17 us
  other arithmetic: 17 us -> 6.65 us
  local copies, waits for them, and re-layouts: 15.2 us -> 8.3 us
  starting transfers between devices: 22.5 us -> 28.4 us
    all_gather x1 -> x0, waiting for transfers between devices: 85.7 us -> none  [on_device(): lax.all_gather(kv_weight, 'kv', axis=0, tiled=True)]
    all_to_all x1 -> x0, waiting for transfers between devices: 52.5 us -> none  [on_device(): lax.all_to_all(spread_heads(local_pages, group_size), 'kv', split_axis=0,...]
    ppermute x3 -> x23, waiting for transfers between devices: 5.76 us -> 41.9 us  [the longest x15 23.2 us: swap(): return lax.ppermute(value, axis, [(i, i ^ bit) for i in range(count)])]
    dot_general x23 -> x0, matrix products: 32.1 us -> none  [the longest x11 14.2 us: absorb(): jnp.einsum('gtk,kd->gtd', weights.astype(jnp.bfloat16), value_rows, prefe...]
    pallas_call x0 -> x3, Pallas kernels: none -> 20.9 us  [the longest x1 12.2 us: attend_early(): pl.pallas_call(functools.partial(early_kernel, place, extension_at, len(p...]
    ppermute x3 -> x23, starting transfers between devices: 16.8 us -> 28.4 us  [the longest x15 17.6 us: swap(): return lax.ppermute(value, axis, [(i, i ^ bit) for i in range(count)])]
    all_to_all x1 -> x0, starting transfers between devices: 5.71 us -> none  [on_device(): lax.all_to_all(spread_heads(local_pages, group_size), 'kv', split_axis=0,...]
    reduce_sum x13 -> x1, other arithmetic: 6 us -> 0.89 us  [page_numbers(): jnp.sum(jnp.where(match, jnp.arange(page_count, dtype=jnp.int32)[:, None]...]
  transfers between devices with their start and end apart: 5 -> 23, of which waited for: 5 -> 12; matrix products, arithmetic and copies ran while one was open for 6% -> 11% of each run, Pallas kernels for 0% -> 14%
where the time goes in v1:
time: 107 us; the launch traced here: 106 us
  waiting for transfers between devices  41.9 us (39%)
  starting transfers between devices  28.4 us (27%)
  Pallas kernels  20.9 us (20%)
  local copies, waits for them, and re-layouts  8.3 us (8%)
  other arithmetic  6.65 us (6%)
    ppermute x15, waiting for transfers between devices, swap(): return lax.ppermute(value, axis, [(i, i ^ bit) for i in range(count)])  23.2 us
    ppermute x6, waiting for transfers between devices, to_plane(): lax.ppermute(value, 'kv', [(i, (i + step) % devices) for i in range(devic...  17.9 us
    ppermute x15, starting transfers between devices, swap(): return lax.ppermute(value, axis, [(i, i ^ bit) for i in range(count)])  17.6 us
    pallas_call x1, Pallas kernels, attend_early(): pl.pallas_call(functools.partial(early_kernel, place, extension_at, len(p...  12.2 us
    ppermute x6, starting transfers between devices, to_plane(): lax.ppermute(value, 'kv', [(i, (i + step) % devices) for i in range(devic...  6.61 us
    pallas_call x1, Pallas kernels, attend_late(): pl.pallas_call(functools.partial(late_kernel, group_size), in_specs=[in_s...  5.69 us
    unnamed x20, local copies, waits for them, and re-layouts  5.49 us
    ppermute x2, starting transfers between devices, on_device(): received.append(lax.ppermute(message, ('grp', 'kv'), routes))  4.2 us
  transfers between devices with their start and end apart: 23, of which 12 were waited for; matrix products, arithmetic and copies ran while one was open for 11% of the time, Pallas kernels for 14%

profile of v1, /device:TPU:5, one launch (start us, length us, event | category | flops | bytes accessed | tf_op | source)
XLA Modules:
  0.0 106.3 jit_solution(4457410108985437109)
XLA Ops:
  0.0 1.0 constant_dynamic-slice_fusion.5
  1.0 0.7 collective-permute-start
  1.8 1.2 %collective-permute-start.3 = (bf16[1,128,5120]{2,1,0:T(8,128)(2,1)}, bf16[1,128,5120]{2,1,0:T(8,128)(2,1)S(1)}, u32[]{:S(2)}, u32[]{:S(2)}) collective-permute-start(bf16[1,128,5120]{2,1,0:T(8,128)(2,1)} %refs_0_.1), channel_id=1, source_target_pairs={{0,16},{16,0},{1,17},{17,1},{2,18},{18,2},{3,19},{19,3},{4,20},{20... | collective-permute-start | bytes 3932168 | tf_op jit(solution)/shard_map/ppermute | solution.py:20
  3.0 1.2 %constant_dynamic-slice_fusion = (bf16[2,128,256]{2,1,0:T(8,128)(2,1)S(1)}, bf16[2,128,256]{2,1,0:T(8,128)(2,1)S(1)}, bf16[2,128,256]{2,1,0:T(8,128)(2,1)S(1)}, bf16[2,128,256]{2,1,0:T(8,128)(2,1)S(1)}) fusion(bf16[2,128,1024]{2,1,0:T(8,128)(2,1)} %param.9, s32[]{:T(128)S(6)} %select_n.43, s32[]{:T(128)S(6)} %select_n.39, s32[]{:T(128)S(6)} %select_n.38, ...), kind=kLoop, calls=%fused_computation.27 | loop fusion | bytes 1048592 | tf_op jit(solution)/shard_map/dynamic_slice | solution.py:355
  4.2 1.3 %collective-permute-start.4 = (bf16[256,256]{1,0:T(8,128)(2,1)S(1)}, bf16[256,256]{1,0:T(8,128)(2,1)S(1)}, u32[]{:S(2)}, u32[]{:S(2)}) collective-permute-start(bf16[256,256]{1,0:T(8,128)(2,1)S(1)} %bitcast.33), channel_id=1, source_target_pairs={{0,4},{1,5},{2,6},{3,7},{4,8},{5,9},{6,10},{7,11},{8,12},{9,13},{1... | collective-permute-start | bytes 393224 | tf_op jit(solution)/shard_map/ppermute | solution.py:362
  5.5 2.1 %collective-permute-start.5 = (bf16[256,256]{1,0:T(8,128)(2,1)S(1)}, bf16[256,256]{1,0:T(8,128)(2,1)S(1)}, u32[]{:S(2)}, u32[]{:S(2)}) collective-permute-start(bf16[256,256]{1,0:T(8,128)(2,1)S(1)} %bitcast.32), channel_id=1, source_target_pairs={{0,12},{1,13},{2,14},{3,15},{4,0},{5,1},{6,2},{7,3},{8,4},{9,5},{1... | collective-permute-start | bytes 393224 | tf_op jit(solution)/shard_map/ppermute | solution.py:362
  7.6 0.4 collective-permute-start.6
  8.0 0.5 compare_bitcast_fusion.1
  8.6 0.5 slice_bitcast_fusion.1
  9.1 0.8 dynamic-slice_convert_fusion
  9.8 0.7 constant_dynamic-update-slice_fusion.5
  10.5 0.7 pad_add_fusion.1
  11.4 1.3 %collective-permute-start.1 = (bf16[640,256]{1,0:T(8,128)(2,1)S(1)}, bf16[640,256]{1,0:T(8,128)(2,1)S(1)}, u32[]{:S(2)}, u32[]{:S(2)}) collective-permute-start(bf16[640,256]{1,0:T(8,128)(2,1)S(1)} %maximum_select_fusion.refs_4_), channel_id=1, source_target_pairs={{0,4},{1,5},{2,6},{3,7},{4,8},{5,9},{6,10},{7,11},{8,12},{9,13},{1... | collective-permute-start | bytes 983048 | tf_op jit(solution)/shard_map/ppermute | solution.py:362
  12.7 0.2 collective-permute-start.8
  12.9 0.2 collective-permute-done.5
  13.2 13.8 %collective-permute-done.6 = bf16[256,256]{1,0:T(8,128)(2,1)S(1)} collective-permute-done((bf16[256,256]{1,0:T(8,128)(2,1)S(1)}, bf16[256,256]{1,0:T(8,128)(2,1)S(1)}, u32[]{:S(2)}, u32[]{:S(2)}) %collective-permute-start.6) | collective-permute-done | bytes 131104 | tf_op jit(solution)/shard_map/ppermute | solution.py:362
  27.0 0.7 constant_dynamic-update-slice_fusion.4
  27.6 0.7 constant_dynamic-update-slice_fusion.3
  28.3 1.7 %constant_dynamic-update-slice_fusion.2 = bf16[1280,256]{1,0:T(8,128)(2,1)} fusion(bf16[1280,256]{1,0:T(8,128)(2,1)} %constant_dynamic-update-slice_fusion.3, bf16[256,256]{1,0:T(8,128)(2,1)} %copy-done.5), kind=kLoop, calls=%fused_computation.18 | loop fusion | bytes 262144
  30.0 0.7 copy-done.1
  30.7 0.2 collective-permute-start.9
  30.9 1.4 %collective-permute-start.2 = (bf16[640,256]{1,0:T(8,128)(2,1)S(1)}, bf16[640,256]{1,0:T(8,128)(2,1)S(1)}, u32[]{:S(2)}, u32[]{:S(2)}) collective-permute-start(bf16[640,256]{1,0:T(8,128)(2,1)S(1)} %collective-permute-done.1.refs_6_), channel_id=1, source_target_pairs={{0,4},{1,5},{2,6},{3,7},{4,8},{5,9},{6,10},{7,11},{8,12},{9,13},{1... | collective-permute-start | bytes 983048 | tf_op jit(solution)/shard_map/ppermute | solution.py:362
  32.4 3.6 %collective-permute-done.7.refs_8_ = bf16[640,256]{1,0:T(8,128)(2,1)} collective-permute-done((bf16[640,256]{1,0:T(8,128)(2,1)S(1)}, bf16[640,256]{1,0:T(8,128)(2,1)}, u32[]{:S(2)}, u32[]{:S(2)}) %collective-permute-start.7) | collective-permute-done | bytes 327712 | tf_op jit(solution)/shard_map/ppermute | solution.py:362
  36.0 3.6 %collective-permute-done.9.refs_7_ = bf16[640,256]{1,0:T(8,128)(2,1)} collective-permute-done((bf16[640,256]{1,0:T(8,128)(2,1)S(1)}, bf16[640,256]{1,0:T(8,128)(2,1)}, u32[]{:S(2)}, u32[]{:S(2)}) %collective-permute-start.9) | collective-permute-done | bytes 327712 | tf_op jit(solution)/shard_map/ppermute | solution.py:20
  39.8 0.5 fusion.3
  40.4 1.0 fusion.1
  41.4 0.2 collective-permute-done.2.refs_10_
  41.7 4.1 %collective-permute-done.10.refs_9_ = bf16[640,256]{1,0:T(8,128)(2,1)S(1)} collective-permute-done((bf16[640,256]{1,0:T(8,128)(2,1)}, bf16[640,256]{1,0:T(8,128)(2,1)S(1)}, u32[]{:S(2)}, u32[]{:S(2)}) %collective-permute-start.10) | collective-permute-done | bytes 327712 | tf_op jit(solution)/shard_map/ppermute | solution.py:20
  45.8 5.8 %collective-permute-start.11 = (bf16[1,128,5120]{2,1,0:T(8,128)(2,1)S(1)}, bf16[1,128,5120]{2,1,0:T(8,128)(2,1)S(1)}, u32[]{:S(2)}, u32[]{:S(2)}) collective-permute-start(bf16[1,128,5120]{2,1,0:T(8,128)(2,1)S(1)} %copy-done), channel_id=1, source_target_pairs={{0,1},{1,0},{2,3},{3,2},{4,5},{5,4},{6,7},{7,6},{8,9},{9,8},{10,11... | collective-permute-start | bytes 3932168 | tf_op jit(solution)/shard_map/ppermute | solution.py:20
  51.6 0.3 collective-permute-start.14
  51.8 0.7 maximum_dynamic-update-slice_fusion
  52.7 1.3 %collective-permute-done.14 = s32[28,3]{0,1:T(4,128)S(1)} collective-permute-done((s32[28,3]{0,1:T(4,128)S(1)}, s32[28,3]{0,1:T(4,128)S(1)}, u32[]{:S(2)}, u32[]{:S(2)}) %collective-permute-start.14) | collective-permute-done | bytes 368 | tf_op jit(solution)/shard_map/ppermute | solution.py:20
  54.0 0.9 fusion.4
  55.0 6.0 %collective-permute-done.13.refs_11_ = bf16[640,256]{1,0:T(8,128)(2,1)S(1)} collective-permute-done((bf16[640,256]{1,0:T(8,128)(2,1)S(1)}, bf16[640,256]{1,0:T(8,128)(2,1)S(1)}, u32[]{:S(2)}, u32[]{:S(2)}) %collective-permute-start.13) | collective-permute-done | bytes 327712 | tf_op jit(solution)/shard_map/ppermute | solution.py:20
  61.3 1.0 fusion.2
  62.6 3.0 %project.1 = (bf16[2,128,256]{2,1,0:T(8,128)(2,1)S(1)}, bf16[2,128,256]{2,1,0:T(8,128)(2,1)S(1)}) custom-call(s32[10]{0:T(128)S(1)} %stack.71.meta, bf16[1,128,5120]{2,1,0:T(8,128)(2,1)S(1)} %copy-done, bf16[1,128,5120]{2,1,0:T(8,128)(2,1)S(1)} %collective-permute-done.11.refs_1_, bf16[1,128,5120]{2,1,0:T(8,128)(2,1)S(1)} %collective-permute-done.3.refs_2_, ...), custom_call_target="tpu_custom_call" | custom-call | flops 1342177280 | bytes 7864320 | tf_op jit(solution)/shard_map/project/pallas_call | solution.py:66
  65.6 3.2 %collective-permute-start.15 = (bf16[2,128,256]{2,1,0:T(8,128)(2,1)S(1)}, bf16[2,128,256]{2,1,0:T(8,128)(2,1)S(1)}, u32[]{:S(2)}, u32[]{:S(2)}) collective-permute-start(bf16[2,128,256]{2,1,0:T(8,128)(2,1)S(1)} %get-tuple-element.34), channel_id=1, source_target_pairs={{0,0},{1,4},{2,2},{3,6},{4,1},{5,5},{6,3},{7,7},{8,16},{9,20},{10,... | collective-permute-start | bytes 393224 | tf_op jit(solution)/shard_map/ppermute | solution.py:452
  68.9 1.0 collective-permute-start.16
  69.8 6.1 %collective-permute-done.18.refs_1_ = bf16[10,128,256]{2,1,0:T(8,128)(2,1)} collective-permute-done((bf16[10,128,256]{2,1,0:T(8,128)(2,1)}, bf16[10,128,256]{2,1,0:T(8,128)(2,1)}, u32[]{:S(2)}, u32[]{:S(2)}) %collective-permute-start.18) | collective-permute-done | bytes 655392 | tf_op jit(solution)/shard_map/ppermute | solution.py:20
  76.0 0.8 collective-permute-done.16
  76.7 6.2 %collective-permute-start.19 = (bf16[10,128,256]{2,1,0:T(8,128)(2,1)}, bf16[10,128,256]{2,1,0:T(8,128)(2,1)S(1)}, u32[]{:S(2)}, u32[]{:S(2)}) collective-permute-start(bf16[10,128,256]{2,1,0:T(8,128)(2,1)} %bitcast.24.refs_0_), channel_id=1, source_target_pairs={{0,1},{1,0},{2,3},{3,2},{4,5},{5,4},{6,7},{7,6},{8,9},{9,8},{10,11... | collective-permute-start | bytes 1966088 | tf_op jit(solution)/shard_map/ppermute | solution.py:20
  83.0 1.3 %collective-permute-start.17 = (bf16[4,128,256]{2,1,0:T(8,128)(2,1)S(1)}, bf16[4,128,256]{2,1,0:T(8,128)(2,1)S(1)}, u32[]{:S(2)}, u32[]{:S(2)}) collective-permute-start(bf16[4,128,256]{2,1,0:T(8,128)(2,1)S(1)} %constant_dynamic-update-slice_fusion.refs_0_), channel_id=1, source_target_pairs={{0,2},{1,3},{2,0},{3,1},{4,6},{5,7},{6,4},{7,5},{8,10},{9,11},{10,... | collective-permute-start | bytes 786440 | tf_op jit(solution)/shard_map/ppermute | solution.py:20
  84.5 0.8 collective-permute-start.21
  85.2 0.6 collective-permute-done.20.refs_3_
  85.8 1.0 copy-done.3
  86.8 12.2 %early.1 = (bf16[5,256,128]{2,1,0:T(8,128)(2,1)S(1)}, f32[5,256,128]{2,1,0:T(8,128)S(1)}, f32[5,256,256]{2,1,0:T(8,128)S(1)}) custom-call(s32[28,3]{1,0:T(8,128)S(1)} %copy.11.reuse, s32[3]{0:T(128)S(1)} %pad_add_fusion.meta, bf16[256,640]{1,0:T(8,128)(2,1)S(1)} %copy-done.3, f32[256,128]{1,0:T(8,128)S(1)} %get-tuple-element.61.cosine, ...), custom_call_target="tpu_custom_call" | custom-call | flops 2348810240 | bytes 1835008 | tf_op jit(solution)/shard_map/early/pallas_call | solution.py:222
  99.1 1.5 %collective-permute-done.22.refs_3_ = bf16[4,128,256]{2,1,0:T(8,128)(2,1)S(1)} collective-permute-done((bf16[4,128,256]{2,1,0:T(8,128)(2,1)S(1)}, bf16[4,128,256]{2,1,0:T(8,128)(2,1)S(1)}, u32[]{:S(2)}, u32[]{:S(2)}) %collective-permute-start.22) | collective-permute-done | bytes 262176 | tf_op jit(solution)/shard_map/ppermute | solution.py:20
  100.6 5.7 %late.1 = bf16[256,640]{1,0:T(8,128)(2,1)} custom-call(s32[28,3]{1,0:T(8,128)S(1)} %copy.11.reuse, s32[3]{0:T(128)S(1)} %pad_add_fusion.meta, bf16[5,256,128]{2,1,0:T(8,128)(2,1)S(1)} %get-tuple-element.45.turned, f32[5,256,128]{2,1,0:T(8,128)S(1)} %get-tuple-element.46.top_in, f32[5,256,256]{2,1,0:T(8,128)S(1)} %get-tuple-element.47.sum_in, ...), custom_call_target="tpu_custom_call" | custom-call | flops 1174405120 | bytes 917504 | tf_op jit(solution)/shard_map/late/pallas_call | solution.py:297
  (44 shorter events, 1.7 us)
Async XLA Ops:
  0.0 8.0 %copy-start.6 = (s32[28,3]{0,1:T(4,128)S(1)}, s32[28,3]{0,1:T(4,128)}, u32[]{:S(2)}) copy-start(s32[28,3]{0,1:T(4,128)} %param.13) | copy-start | bytes 1012
  1.0 10.2 %collective-permute-start = (bf16[320,256]{1,0:T(8,128)(2,1)S(1)}, bf16[320,256]{1,0:T(8,128)(2,1)S(1)}, u32[]{:S(2)}, u32[]{:S(2)}) collective-permute-start(bf16[320,256]{1,0:T(8,128)(2,1)S(1)} %get-tuple-element.54), channel_id=1, source_target_pairs={{0,1},{1,0},{2,3},{3,2},{4,5},{5,4},{6,7},{7,6},{8,9},{9,8},{10,11... | collective-permute-start | bytes 491528 | tf_op jit(solution)/shard_map/ppermute | solution.py:20
  1.8 44.0 %collective-permute-start.3 = (bf16[1,128,5120]{2,1,0:T(8,128)(2,1)}, bf16[1,128,5120]{2,1,0:T(8,128)(2,1)S(1)}, u32[]{:S(2)}, u32[]{:S(2)}) collective-permute-start(bf16[1,128,5120]{2,1,0:T(8,128)(2,1)} %refs_0_.1), channel_id=1, source_target_pairs={{0,16},{16,0},{1,17},{17,1},{2,18},{18,2},{3,19},{19,3},{4,20},{20... | collective-permute-start | bytes 3932168 | tf_op jit(solution)/shard_map/ppermute | solution.py:20
  3.0 29.4 %copy-start.4 = (bf16[256,256]{1,0:T(8,128)(2,1)S(1)}, bf16[256,256]{1,0:T(8,128)(2,1)}, u32[]{:S(2)}) copy-start(bf16[256,256]{1,0:T(8,128)(2,1)} %param.8) | copy-start | bytes 393220
  4.2 8.5 %collective-permute-start.4 = (bf16[256,256]{1,0:T(8,128)(2,1)S(1)}, bf16[256,256]{1,0:T(8,128)(2,1)S(1)}, u32[]{:S(2)}, u32[]{:S(2)}) collective-permute-start(bf16[256,256]{1,0:T(8,128)(2,1)S(1)} %bitcast.33), channel_id=1, source_target_pairs={{0,4},{1,5},{2,6},{3,7},{4,8},{5,9},{6,10},{7,11},{8,12},{9,13},{1... | collective-permute-start | bytes 393224 | tf_op jit(solution)/shard_map/ppermute | solution.py:362
  5.5 7.7 %collective-permute-start.5 = (bf16[256,256]{1,0:T(8,128)(2,1)S(1)}, bf16[256,256]{1,0:T(8,128)(2,1)S(1)}, u32[]{:S(2)}, u32[]{:S(2)}) collective-permute-start(bf16[256,256]{1,0:T(8,128)(2,1)S(1)} %bitcast.32), channel_id=1, source_target_pairs={{0,12},{1,13},{2,14},{3,15},{4,0},{5,1},{6,2},{7,3},{8,4},{9,5},{1... | collective-permute-start | bytes 393224 | tf_op jit(solution)/shard_map/ppermute | solution.py:362
  7.6 19.3 %collective-permute-start.6 = (bf16[256,256]{1,0:T(8,128)(2,1)S(1)}, bf16[256,256]{1,0:T(8,128)(2,1)S(1)}, u32[]{:S(2)}, u32[]{:S(2)}) collective-permute-start(bf16[256,256]{1,0:T(8,128)(2,1)S(1)} %bitcast.31), channel_id=1, source_target_pairs={{0,8},{1,9},{2,10},{3,11},{4,12},{5,13},{6,14},{7,15},{8,0},{9,1},... | collective-permute-start | bytes 393224 | tf_op jit(solution)/shard_map/ppermute | solution.py:362
  11.4 18.6 %collective-permute-start.1 = (bf16[640,256]{1,0:T(8,128)(2,1)S(1)}, bf16[640,256]{1,0:T(8,128)(2,1)S(1)}, u32[]{:S(2)}, u32[]{:S(2)}) collective-permute-start(bf16[640,256]{1,0:T(8,128)(2,1)S(1)} %maximum_select_fusion.refs_4_), channel_id=1, source_target_pairs={{0,4},{1,5},{2,6},{3,7},{4,8},{5,9},{6,10},{7,11},{8,12},{9,13},{1... | collective-permute-start | bytes 983048 | tf_op jit(solution)/shard_map/ppermute | solution.py:362
  12.7 17.3 %collective-permute-start.8 = (bf16[640,256]{1,0:T(8,128)(2,1)S(1)}, bf16[640,256]{1,0:T(8,128)(2,1)S(1)}, u32[]{:S(2)}, u32[]{:S(2)}) collective-permute-start(bf16[640,256]{1,0:T(8,128)(2,1)S(1)} %maximum_select_fusion.refs_4_), channel_id=1, source_target_pairs={{0,2},{1,3},{2,0},{3,1},{4,6},{5,7},{6,4},{7,5},{8,10},{9,11},{10,... | collective-permute-start | bytes 983048 | tf_op jit(solution)/shard_map/ppermute | solution.py:20
  27.0 0.7 copy-start.5
  27.0 9.1 %collective-permute-start.7 = (bf16[640,256]{1,0:T(8,128)(2,1)S(1)}, bf16[640,256]{1,0:T(8,128)(2,1)}, u32[]{:S(2)}, u32[]{:S(2)}) collective-permute-start(bf16[640,256]{1,0:T(8,128)(2,1)S(1)} %maximum_select_fusion.refs_4_), channel_id=1, source_target_pairs={{0,12},{1,13},{2,14},{3,15},{4,0},{5,1},{6,2},{7,3},{8,4},{9,5},{1... | collective-permute-start | bytes 983048 | tf_op jit(solution)/shard_map/ppermute | solution.py:362
  28.3 17.4 %copy-start = (bf16[1,128,5120]{2,1,0:T(8,128)(2,1)S(1)}, bf16[1,128,5120]{2,1,0:T(8,128)(2,1)}, u32[]{:S(2)}) copy-start(bf16[1,128,5120]{2,1,0:T(8,128)(2,1)} %refs_0_.1) | copy-start | bytes 3932164
  30.0 0.7 copy-start.1
  30.7 8.9 %collective-permute-start.9 = (bf16[640,256]{1,0:T(8,128)(2,1)S(1)}, bf16[640,256]{1,0:T(8,128)(2,1)}, u32[]{:S(2)}, u32[]{:S(2)}) collective-permute-start(bf16[640,256]{1,0:T(8,128)(2,1)S(1)} %collective-permute-done.1.refs_6_), channel_id=1, source_target_pairs={{0,2},{1,3},{2,0},{3,1},{4,6},{5,7},{6,4},{7,5},{8,10},{9,11},{10,... | collective-permute-start | bytes 983048 | tf_op jit(solution)/shard_map/ppermute | solution.py:20
  30.9 10.7 %collective-permute-start.2 = (bf16[640,256]{1,0:T(8,128)(2,1)S(1)}, bf16[640,256]{1,0:T(8,128)(2,1)S(1)}, u32[]{:S(2)}, u32[]{:S(2)}) collective-permute-start(bf16[640,256]{1,0:T(8,128)(2,1)S(1)} %collective-permute-done.1.refs_6_), channel_id=1, source_target_pairs={{0,4},{1,5},{2,6},{3,7},{4,8},{5,9},{6,10},{7,11},{8,12},{9,13},{1... | collective-permute-start | bytes 983048 | tf_op jit(solution)/shard_map/ppermute | solution.py:362
  39.6 6.1 %collective-permute-start.10 = (bf16[640,256]{1,0:T(8,128)(2,1)}, bf16[640,256]{1,0:T(8,128)(2,1)S(1)}, u32[]{:S(2)}, u32[]{:S(2)}) collective-permute-start(bf16[640,256]{1,0:T(8,128)(2,1)} %collective-permute-done.7.refs_8_), channel_id=1, source_target_pairs={{0,2},{1,3},{2,0},{3,1},{4,6},{5,7},{6,4},{7,5},{8,10},{9,11},{10,... | collective-permute-start | bytes 983048 | tf_op jit(solution)/shard_map/ppermute | solution.py:20
  41.4 21.2 %copy-start.2 = (bf16[640,256]{1,0:T(8,128)(2,1)S(1)}, bf16[640,256]{1,0:T(8,128)(2,1)}, u32[]{:S(2)}) copy-start(bf16[640,256]{1,0:T(8,128)(2,1)} %copy-done.1) | copy-start | bytes 983044
  45.8 16.8 %collective-permute-start.11 = (bf16[1,128,5120]{2,1,0:T(8,128)(2,1)S(1)}, bf16[1,128,5120]{2,1,0:T(8,128)(2,1)S(1)}, u32[]{:S(2)}, u32[]{:S(2)}) collective-permute-start(bf16[1,128,5120]{2,1,0:T(8,128)(2,1)S(1)} %copy-done), channel_id=1, source_target_pairs={{0,1},{1,0},{2,3},{3,2},{4,5},{5,4},{6,7},{7,6},{8,9},{9,8},{10,11... | collective-permute-start | bytes 3932168 | tf_op jit(solution)/shard_map/ppermute | solution.py:20
  51.5 11.0 %collective-permute-start.12 = (bf16[1,128,5120]{2,1,0:T(8,128)(2,1)S(1)}, bf16[1,128,5120]{2,1,0:T(8,128)(2,1)S(1)}, u32[]{:S(2)}, u32[]{:S(2)}) collective-permute-start(bf16[1,128,5120]{2,1,0:T(8,128)(2,1)S(1)} %collective-permute-done.3.refs_2_), channel_id=1, source_target_pairs={{0,1},{1,0},{2,3},{3,2},{4,5},{5,4},{6,7},{7,6},{8,9},{9,8},{10,11... | collective-permute-start | bytes 3932168 | tf_op jit(solution)/shard_map/ppermute | solution.py:20
  51.6 2.4 %collective-permute-start.14 = (s32[28,3]{0,1:T(4,128)S(1)}, s32[28,3]{0,1:T(4,128)S(1)}, u32[]{:S(2)}, u32[]{:S(2)}) collective-permute-start(s32[28,3]{0,1:T(4,128)S(1)} %copy-done.6), channel_id=1, source_target_pairs={{0,16},{16,0},{1,17},{17,1},{2,18},{18,2},{3,19},{19,3},{4,20},{20... | collective-permute-start | bytes 1016 | tf_op jit(solution)/shard_map/ppermute | solution.py:20
  52.5 8.5 %collective-permute-start.13 = (bf16[640,256]{1,0:T(8,128)(2,1)S(1)}, bf16[640,256]{1,0:T(8,128)(2,1)S(1)}, u32[]{:S(2)}, u32[]{:S(2)}) collective-permute-start(bf16[640,256]{1,0:T(8,128)(2,1)S(1)} %collective-permute-done.2.refs_10_), channel_id=1, source_target_pairs={{0,2},{1,3},{2,0},{3,1},{4,6},{5,7},{6,4},{7,5},{8,10},{9,11},{10,... | collective-permute-start | bytes 983048 | tf_op jit(solution)/shard_map/ppermute | solution.py:20
  61.0 14.9 %collective-permute-start.18 = (bf16[10,128,256]{2,1,0:T(8,128)(2,1)}, bf16[10,128,256]{2,1,0:T(8,128)(2,1)}, u32[]{:S(2)}, u32[]{:S(2)}) collective-permute-start(bf16[10,128,256]{2,1,0:T(8,128)(2,1)} %bitcast.24.refs_0_), channel_id=1, source_target_pairs={{0,2},{1,3},{2,0},{3,1},{4,6},{5,7},{6,4},{7,5},{8,10},{9,11},{10,... | collective-permute-start | bytes 1966088 | tf_op jit(solution)/shard_map/ppermute | solution.py:20
  65.6 10.4 %collective-permute-start.15 = (bf16[2,128,256]{2,1,0:T(8,128)(2,1)S(1)}, bf16[2,128,256]{2,1,0:T(8,128)(2,1)S(1)}, u32[]{:S(2)}, u32[]{:S(2)}) collective-permute-start(bf16[2,128,256]{2,1,0:T(8,128)(2,1)S(1)} %get-tuple-element.34), channel_id=1, source_target_pairs={{0,0},{1,4},{2,2},{3,6},{4,1},{5,5},{6,3},{7,7},{8,16},{9,20},{10,... | collective-permute-start | bytes 393224 | tf_op jit(solution)/shard_map/ppermute | solution.py:452
  68.9 7.9 %collective-permute-start.16 = (bf16[2,128,256]{2,1,0:T(8,128)(2,1)S(1)}, bf16[2,128,256]{2,1,0:T(8,128)(2,1)S(1)}, u32[]{:S(2)}, u32[]{:S(2)}) collective-permute-start(bf16[2,128,256]{2,1,0:T(8,128)(2,1)S(1)} %get-tuple-element.35), channel_id=1, source_target_pairs={{0,16},{1,20},{2,18},{3,22},{4,17},{5,21},{6,19},{7,23},{8,0},{9,4... | collective-permute-start | bytes 393224 | tf_op jit(solution)/shard_map/ppermute | solution.py:452
  76.7 8.5 %collective-permute-start.19 = (bf16[10,128,256]{2,1,0:T(8,128)(2,1)}, bf16[10,128,256]{2,1,0:T(8,128)(2,1)S(1)}, u32[]{:S(2)}, u32[]{:S(2)}) collective-permute-start(bf16[10,128,256]{2,1,0:T(8,128)(2,1)} %bitcast.24.refs_0_), channel_id=1, source_target_pairs={{0,1},{1,0},{2,3},{3,2},{4,5},{5,4},{6,7},{7,6},{8,9},{9,8},{10,11... | collective-permute-start | bytes 1966088 | tf_op jit(solution)/shard_map/ppermute | solution.py:20
  82.9 2.9 %collective-permute-start.20 = (bf16[10,128,256]{2,1,0:T(8,128)(2,1)}, bf16[10,128,256]{2,1,0:T(8,128)(2,1)S(1)}, u32[]{:S(2)}, u32[]{:S(2)}) collective-permute-start(bf16[10,128,256]{2,1,0:T(8,128)(2,1)} %collective-permute-done.18.refs_1_), channel_id=1, source_target_pairs={{0,1},{1,0},{2,3},{3,2},{4,5},{5,4},{6,7},{7,6},{8,9},{9,8},{10,11... | collective-permute-start | bytes 1966088 | tf_op jit(solution)/shard_map/ppermute | solution.py:20
  83.0 16.0 %collective-permute-start.17 = (bf16[4,128,256]{2,1,0:T(8,128)(2,1)S(1)}, bf16[4,128,256]{2,1,0:T(8,128)(2,1)S(1)}, u32[]{:S(2)}, u32[]{:S(2)}) collective-permute-start(bf16[4,128,256]{2,1,0:T(8,128)(2,1)S(1)} %constant_dynamic-update-slice_fusion.refs_0_), channel_id=1, source_target_pairs={{0,2},{1,3},{2,0},{3,1},{4,6},{5,7},{6,4},{7,5},{8,10},{9,11},{10,... | collective-permute-start | bytes 786440 | tf_op jit(solution)/shard_map/ppermute | solution.py:20
  84.5 14.6 %collective-permute-start.21 = (bf16[4,128,256]{2,1,0:T(8,128)(2,1)S(1)}, bf16[4,128,256]{2,1,0:T(8,128)(2,1)S(1)}, u32[]{:S(2)}, u32[]{:S(2)}) collective-permute-start(bf16[4,128,256]{2,1,0:T(8,128)(2,1)S(1)} %constant_dynamic-update-slice_fusion.refs_0_), channel_id=1, source_target_pairs={{0,1},{1,0},{2,3},{3,2},{4,5},{5,4},{6,7},{7,6},{8,9},{9,8},{10,11... | collective-permute-start | bytes 786440 | tf_op jit(solution)/shard_map/ppermute | solution.py:20
  85.8 1.0 copy-start.3
  99.0 1.6 %collective-permute-start.22 = (bf16[4,128,256]{2,1,0:T(8,128)(2,1)S(1)}, bf16[4,128,256]{2,1,0:T(8,128)(2,1)S(1)}, u32[]{:S(2)}, u32[]{:S(2)}) collective-permute-start(bf16[4,128,256]{2,1,0:T(8,128)(2,1)S(1)} %collective-permute-done.17.refs_2_), channel_id=1, source_target_pairs={{0,1},{1,0},{2,3},{3,2},{4,5},{5,4},{6,7},{7,6},{8,9},{9,8},{10,11... | collective-permute-start | bytes 786440 | tf_op jit(solution)/shard_map/ppermute | solution.py:20

commit v2 on v1

v2 whole, which is shorter than its diff:
```python
import functools

import jax
import jax.numpy as jnp
from jax import lax
from jax.experimental import pallas as pl
from jax.experimental.pallas import tpu as pltpu
from jax.sharding import PartitionSpec as P

GQ = 5
HEAD_DIM = 128
PAIR = 2 * HEAD_DIM
HEADS = 4

ROPE_BASE = 1000000.0
MASK_VALUE = -1e30


def swap(value, axis, bit, count):
    return lax.ppermute(value, axis, [(i, i ^ bit) for i in range(count)])


def angle_tables(positions):
    half_dim = HEAD_DIM // 2
    frequency = ROPE_BASE ** (-jnp.arange(half_dim, dtype=jnp.float32) * 2.0 / HEAD_DIM)
    angles = positions.astype(jnp.float32)[..., None] * frequency
    cosine = jnp.cos(angles)
    sine = jnp.sin(angles)
    return (
        jnp.concatenate([cosine, cosine], axis=-1),
        jnp.concatenate([-sine, sine], axis=-1),
    )


def project_kernel(blocks, meta, *refs):
    pages, weights = refs[:4], refs[4:-10]
    store, store_across, store_core, bias, cosine, sine = refs[-10:-4]
    out_first, out_second, total, stored = refs[-4:]
    rows = cosine.shape[1]
    span = pages[0].shape[2] // blocks
    single = len(weights) == 1

    for block in range(blocks):
        chip = block if single else meta[12 + block]
        start = pl.multiple_of(chip * span, HEAD_DIM)
        left = jnp.concatenate([page[0, :, pl.ds(start, span)] for page in pages], axis=0)
        right = weights[0][pl.ds(block * span, span)] if single else weights[block][...]
        product = jnp.dot(left, right, preferred_element_type=jnp.float32)
        total[...] = product + (bias[...] if block == 0 else total[...])
    core, target = meta[2], meta[3]
    for slot in range(2):
        stored[0, slot] = store[slot, :, pl.ds(pl.multiple_of(target * PAIR, PAIR), PAIR)]
        stored[1, slot] = store_core[slot]
        stored[2, slot] = store_across[slot, :, pl.ds(pl.multiple_of(core * PAIR, PAIR), PAIR)]
        stored[3, slot] = store_core[2 + slot]
    for out, place in ((out_first, 0), (out_second, 1)):
        base = meta[place] * 2
        for rel in range(2):
            number = base + rel
            page = total[pl.ds(pl.multiple_of(number * rows, rows), rows)]
            keys = page[:, :HEAD_DIM]
            turned = keys * cosine[number] + pltpu.roll(keys, HEAD_DIM // 2, 1) * sine[number]
            fresh = meta[4 + number] > 0
            swapped = fresh & (meta[8 + number] == 0)
            out[2 * rel] = stored[number, swapped.astype(jnp.int32)]

            @pl.when(fresh)
            def _():
                out[2 * rel + 1, :, :HEAD_DIM] = turned.astype(jnp.bfloat16)
                out[2 * rel + 1, :, HEAD_DIM:] = page[:, HEAD_DIM:].astype(jnp.bfloat16)

            @pl.when(jnp.logical_not(fresh))
            def _():
                out[2 * rel + 1] = stored[number, 1]


def project(meta, pages, weights, stores, bias, cosine, sine):
    rows, depth = pages[0].shape[1:]
    width = weights[0].shape[1]
    in_smem = pl.BlockSpec(memory_space=pltpu.SMEM)
    in_vmem = pl.BlockSpec(memory_space=pltpu.VMEM)
    return pl.pallas_call(
        functools.partial(project_kernel, 8),
        in_specs=[in_smem] + [in_vmem] * (4 + len(weights) + 6),
        out_specs=[in_vmem] * 2,
        out_shape=[jax.ShapeDtypeStruct((4, rows, width), jnp.bfloat16)] * 2,
        scratch_shapes=[
            pltpu.VMEM((4 * rows, width), jnp.float32),
            pltpu.VMEM((4, 2, rows, width), jnp.bfloat16),
        ],
        compiler_params=pltpu.CompilerParams(vmem_limit_bytes=24 << 20),
        cost_estimate=pl.CostEstimate(
            flops=2 * 4 * rows * depth * width,
            bytes_accessed=2 * (4 * rows + width) * depth,
            transcendentals=0,
        ),
        name="project",
    )(meta, *pages, *weights, *stores, bias, cosine, sine)


def fold(query_ref, rows, top_ref, sum_ref, mask=None, first=False):
    key_rows, value_rows = rows[:, :HEAD_DIM], rows[:, HEAD_DIM:]
    copies = rows.shape[0] // HEAD_DIM
    extended = jnp.concatenate([value_rows, jnp.ones_like(value_rows)], axis=1)

    def scores_of(group):
        scores = lax.dot_general(
            query_ref[group],
            key_rows,
            (((1,), (1,)), ((), ())),
            preferred_element_type=jnp.float32,
        )
        return scores if mask is None else jnp.where(mask, scores, MASK_VALUE)

    ahead = scores_of(0)
    for group in range(GQ):
        scores = ahead
        if group + 1 < GQ:
            ahead = scores_of(group + 1)
        row_top = jnp.broadcast_to(
            jnp.max(scores, axis=1, keepdims=True), (scores.shape[0], HEAD_DIM)
        )
        if not first:
            old_top = top_ref[group]
            row_top = jnp.maximum(old_top, row_top)
        weights = jnp.exp(scores - jnp.concatenate([row_top] * copies, axis=1))
        product = jnp.dot(
            weights.astype(jnp.bfloat16), extended, preferred_element_type=jnp.float32
        )
        if not first:
            shrink = jnp.exp(old_top - row_top)
            product += sum_ref[group] * jnp.concatenate([shrink, shrink], axis=1)
        sum_ref[group] = product
        top_ref[group] = row_top


def fold_pages(query_ref, buffer, wait_page, count, top_ref, sum_ref):
    def part(start, size):
        for offset in range(size):
            wait_page(start + offset)
        rows = buffer[pl.ds(start, size)].reshape(size * buffer.shape[1], PAIR)
        fold(query_ref, rows, top_ref, sum_ref)

    full = count // 4

    def body(index, carry):
        part(index * 4, 4)
        return carry

    lax.fori_loop(0, full, body, 0)

    @pl.when((count & 2) != 0)
    def _():
        part(full * 4, 2)

    @pl.when((count & 1) != 0)
    def _():
        part(count - 1, 1)


def extension_kernel(group_size, meta, query, cosine, sine, *refs):
    pieces, (turned, top_ref, sum_ref) = refs[:group_size], refs[group_size:]
    slice_index = meta[1]
    scale = HEAD_DIM**-0.5
    cos_rows, sin_rows = cosine[...], sine[...]
    for group in range(GQ):
        values = query[:, group * HEAD_DIM : (group + 1) * HEAD_DIM].astype(jnp.float32)
        rotated = values * cos_rows + pltpu.roll(values, HEAD_DIM // 2, 1) * sin_rows
        turned[group] = (rotated * scale).astype(jnp.bfloat16)
    row_count = query.shape[0]
    rows = lax.broadcasted_iota(jnp.int32, (row_count, row_count), 0)
    columns = lax.broadcasted_iota(jnp.int32, (row_count, row_count), 1)

    fold(turned, pieces[0][...], top_ref, sum_ref, mask=columns <= rows, first=True)
    for relative in range(1, group_size):

        @pl.when((slice_index ^ relative) < slice_index)
        def _():
            fold(turned, pieces[relative][...], top_ref, sum_ref)


def attend_extension(meta, queries, row_cos, row_sin, pieces):
    row_count = queries.shape[0]
    in_smem = pl.BlockSpec(memory_space=pltpu.SMEM)
    in_vmem = pl.BlockSpec(memory_space=pltpu.VMEM)
    shape = (GQ, row_count, HEAD_DIM)
    work = GQ * row_count * row_count * len(pieces)
    return pl.pallas_call(
        functools.partial(extension_kernel, len(pieces)),
        in_specs=[in_smem] + [in_vmem] * (3 + len(pieces)),
        out_specs=[in_vmem] * 3,
        out_shape=[
            jax.ShapeDtypeStruct(shape, jnp.bfloat16),
            jax.ShapeDtypeStruct(shape, jnp.float32),
            jax.ShapeDtypeStruct((GQ, row_count, PAIR), jnp.float32),
        ],
        compiler_params=pltpu.CompilerParams(vmem_limit_bytes=24 << 20),
        cost_estimate=pl.CostEstimate(
            flops=4 * work * HEAD_DIM,
            bytes_accessed=row_count * PAIR * 2 * len(pieces),
            transcendentals=work,
        ),
        name="extension",
    )(meta, queries, row_cos, row_sin, *pieces)


def pages_kernel(
    group_size, beside, last, reuse, meta, turned, top_in, sum_in, *refs
):
    count_pieces = group_size // 2
    pieces, outs = refs[:count_pieces], refs[count_pieces : count_pieces + (1 if last else 2)]
    top_ref, sum_ref, buffer, in_use, semaphores = refs[-5:]
    page_count, devices = reuse.shape[0], in_use.shape[0]
    head, slice_index, side = meta[0], meta[1], meta[2]

    def clear(device, carry):
        in_use[device] = 0
        return carry

    lax.fori_loop(0, devices, clear, 0)

    def note(page, carry):
        @pl.when(reuse[page, 0] == 0)
        def _():
            in_use[reuse[page, 2]] = 1

        return carry

    lax.fori_loop(0, page_count, note, 0)

    def start(page, count):
        cached = reuse[page, 0] == 1
        slot = reuse[page, 1]
        device = jnp.where(cached, slot >> 1, reuse[page, 2])
        source, spot = device // group_size, device % group_size
        holder = (spot - (spot & 1)) + (source & 1)
        relative = slice_index ^ holder
        half = jnp.where(
            cached, jnp.where((slot & 1) == 0, 0, 1 - in_use[device]), 1
        )
        index = (((source >> 1) ^ side) * 2 + ((spot ^ head) & 1)) * 2 + half
        chosen = (relative & (group_size // 2)) == (group_size // 2 if beside else 0)

        @pl.when(chosen)
        def _():
            for number, piece in enumerate(pieces):

                @pl.when((relative & (group_size // 2 - 1)) == number)
                def _():
                    pltpu.make_async_copy(
                        piece.at[index], buffer.at[count], semaphores.at[count]
                    ).start()

        return count + chosen.astype(jnp.int32)

    count = lax.fori_loop(0, page_count, start, jnp.int32(0))
    top_ref[...] = jnp.full_like(top_ref, MASK_VALUE)
    sum_ref[...] = jnp.zeros_like(sum_ref)

    def wait_page(index):
        pltpu.make_async_copy(pieces[0].at[0], buffer.at[index], semaphores.at[index]).wait()

    fold_pages(turned, buffer, wait_page, count, top_ref, sum_ref)
    for group in range(GQ):
        first_top, last_top = top_in[group], top_ref[group]
        row_top = jnp.maximum(first_top, last_top)
        first_share, last_share = jnp.exp(first_top - row_top), jnp.exp(last_top - row_top)
        total = sum_in[group] * jnp.concatenate([first_share, first_share], axis=1)
        total += sum_ref[group] * jnp.concatenate([last_share, last_share], axis=1)
        if last:
            outs[0][:, group * HEAD_DIM : (group + 1) * HEAD_DIM] = (
                total[:, :HEAD_DIM] / total[:, HEAD_DIM:]
            ).astype(outs[0].dtype)
        else:
            outs[0][group] = row_top
            outs[1][group] = total


def attend_pages(group_size, devices, last, reuse, meta, turned, top, total, pieces):
    page_count, row_count, page_rows = reuse.shape[0], turned.shape[1], pieces[0].shape[1]
    most = min(page_count, len(pieces) * pieces[0].shape[0])
    in_smem = pl.BlockSpec(memory_space=pltpu.SMEM)
    in_vmem = pl.BlockSpec(memory_space=pltpu.VMEM)
    anywhere = pl.BlockSpec(memory_space=pl.ANY)
    work = GQ * row_count * page_rows * page_count // 2
    state = [
        jax.ShapeDtypeStruct(top.shape, top.dtype),
        jax.ShapeDtypeStruct(total.shape, total.dtype),
    ]
    final = [jax.ShapeDtypeStruct((row_count, GQ * HEAD_DIM), jnp.bfloat16)]
    return pl.pallas_call(
        functools.partial(pages_kernel, group_size, last, last),
        in_specs=[in_smem] * 2 + [in_vmem] * 3 + [anywhere] * len(pieces),
        out_specs=[in_vmem] if last else [in_vmem] * 2,
        out_shape=final if last else state,
        scratch_shapes=[
            pltpu.VMEM(top.shape, top.dtype),
            pltpu.VMEM(total.shape, total.dtype),
            pltpu.VMEM((most, page_rows, PAIR), jnp.bfloat16),
            pltpu.SMEM((devices,), jnp.int32),
            pltpu.SemaphoreType.DMA((most,)),
        ],
        compiler_params=pltpu.CompilerParams(vmem_limit_bytes=24 << 20),
        cost_estimate=pl.CostEstimate(
            flops=4 * work * HEAD_DIM,
            bytes_accessed=page_rows * page_count * PAIR,
            transcendentals=work,
        ),
        name="beside" if last else "column",
    )(reuse, meta, turned, top, total, *pieces)


def on_device(parts, queries, ext_kv, page_store, prefix_hidden, kv_weight, kv_bias, reuse):
    devices = lax.axis_size("kv")
    own_index = lax.axis_index("kv")
    part_index = lax.axis_index("grp")
    row_count = queries.shape[0]
    group_size = devices // HEADS
    group_bits = group_size.bit_length() - 1
    head = own_index >> group_bits
    slice_index = own_index & (group_size - 1)
    core = own_index & 1
    side = part_index & 1
    page_count = reuse.shape[0]
    slots, page_rows = page_store.shape[0], page_store.shape[1]

    def exchange(value, bit):
        return swap(value, "kv", bit, devices)

    hidden_across = swap(prefix_hidden, "grp", 1, parts)

    target = 2 * side + core
    spare = 2 * side + (1 - core)
    mine = lax.dynamic_slice_in_dim(kv_weight, target * PAIR, PAIR, 1)
    other = exchange(lax.dynamic_slice_in_dim(kv_weight, spare * PAIR, PAIR, 1), 1)
    chip_rows = jnp.where(
        core == 0,
        jnp.concatenate([mine, other], axis=0),
        jnp.concatenate([other, mine], axis=0),
    )

    order = []
    if group_size == 4:
        def to_plane(value, shift):
            step = shift * group_size
            return lax.ppermute(value, "kv", [(i, (i + step) % devices) for i in range(devices)])

        near, back = to_plane(chip_rows, 1), to_plane(chip_rows, 3)
        beside_own = exchange(chip_rows, 2)
        far = to_plane(near, 1)
        near_sent, _ = lax.optimization_barrier((near, beside_own))
        beside_near = exchange(near_sent, 2)
        back_sent, _ = lax.optimization_barrier((back, beside_near))
        beside_back = exchange(back_sent, 2)
        far_sent, hidden_mine, hidden_passed, reuse_sent, store_sent, _ = (
            lax.optimization_barrier(
                (far, prefix_hidden, hidden_across, reuse, page_store, beside_back)
            )
        )
        hidden_core = exchange(hidden_mine, 1)
        beside_far = exchange(far_sent, 2)
        weights = [chip_rows, beside_own, near, beside_near, back, beside_back, far, beside_far]
        for shift in (0, 1, 3, 2):
            chip = (((head - shift) & (HEADS - 1)) << 1) | (slice_index >> 1)
            order += [chip, chip ^ 1]
    else:
        hidden_core, hidden_passed = exchange(prefix_hidden, 1), hidden_across
        reuse_sent, store_sent = reuse, page_store
        weights = [
            lax.all_gather(
                chip_rows,
                "kv",
                axis=0,
                tiled=True,
                axis_index_groups=[list(range(first, devices, 2)) for first in range(2)],
            )
        ]
    hidden_diagonal = exchange(hidden_passed, 1)
    reuse_across = swap(reuse_sent, "grp", 1, parts)
    offset = page_count * page_rows
    (ext_kv, first_row), _ = lax.optimization_barrier(
        ((ext_kv, slice_index * row_count), weights[min(2, len(weights) - 1)])
    )
    query_pos = offset + first_row + jnp.arange(row_count, dtype=jnp.int32)
    row_cos, row_sin = angle_tables(query_pos)
    raw_keys = ext_kv[:, :HEAD_DIM].astype(jnp.float32)
    own_keys = raw_keys * row_cos + jnp.roll(raw_keys, HEAD_DIM // 2, axis=1) * row_sin
    own_block = jnp.concatenate([own_keys.astype(jnp.bfloat16), ext_kv[:, HEAD_DIM:]], axis=1)

    bits = []
    while 1 << len(bits) < group_size:
        bits.insert(0, 1 << len(bits))

    def spread(pieces, bits):
        pieces = dict(pieces)
        for bit in bits:
            pieces.update({known ^ bit: exchange(value, bit) for known, value in pieces.items()})
        return [pieces[relative] for relative in sorted(pieces)]

    meta = jnp.stack([head, slice_index, side]).astype(jnp.int32)
    turned, top, total = attend_extension(
        meta, queries, row_cos, row_sin, spread({0: own_block}, bits)
    )
    hidden_diagonal, turned = lax.optimization_barrier((hidden_diagonal, turned))

    other_part = lax.dynamic_slice_in_dim(store_sent, (1 - side) * 2 * PAIR, 2 * PAIR, 2)
    store_across = swap(other_part, "grp", 1, parts)
    store_core = exchange(
        jnp.concatenate(
            [
                lax.dynamic_slice_in_dim(page_store, spare * PAIR, PAIR, 2),
                lax.dynamic_slice_in_dim(store_across, (1 - core) * PAIR, PAIR, 2),
            ],
            axis=0,
        ),
        1,
    )

    def page_numbers(table):
        match = (table[:, 0] == 0)[:, None] & (
            table[:, 2][:, None] == jnp.stack([own_index, own_index ^ 1])[None, :]
        )
        return jnp.sum(
            jnp.where(match, jnp.arange(page_count, dtype=jnp.int32)[:, None], 0), axis=0
        )

    def in_use(table):
        pair = jnp.stack([own_index, own_index ^ 1])[None, :]
        cached = (table[:, 0] == 1)[:, None]
        fresh = jnp.any(jnp.logical_not(cached) & (table[:, 2][:, None] == pair), axis=0)
        first = jnp.any(cached & (table[:, 1][:, None] == 2 * pair), axis=0)
        return fresh.astype(jnp.int32), first.astype(jnp.int32)

    numbers = jnp.concatenate([page_numbers(reuse), page_numbers(reuse_across)])
    flags = [jnp.concatenate(pair) for pair in zip(in_use(reuse), in_use(reuse_across))]
    page_cos, page_sin = angle_tables(
        numbers[:, None] * page_rows + jnp.arange(page_rows, dtype=jnp.int32)[None, :]
    )

    bias = lax.dynamic_slice_in_dim(kv_bias, target * PAIR, PAIR, 0).astype(jnp.float32)[None, :]
    first_side = (head >> 1) ^ side
    choice = jnp.concatenate(
        [jnp.stack([first_side, first_side ^ 1, core, target]), *flags]
        + ([jnp.stack(order)] if order else [])
    ).astype(jnp.int32)
    messages = project(
        choice,
        (prefix_hidden, hidden_core, hidden_across, hidden_diagonal),
        weights,
        (page_store, store_across, store_core),
        bias,
        page_cos,
        page_sin,
    )
    received = []
    for turn, message in enumerate(messages):
        routes = []
        for part in range(parts):
            for device in range(devices):
                plane, spot = device // group_size, device % group_size
                to_part = (part & ~1) | ((plane >> 1) ^ turn)
                to_spot = (spot & ~1) | (plane & 1)
                to_head = 2 * (part & 1) + (spot & 1)
                routes.append(
                    (part * devices + device, to_part * devices + to_head * group_size + to_spot)
                )
        received.append(lax.ppermute(message, ("grp", "kv"), routes))
    arrived = jnp.concatenate(received, axis=0)
    crossed = exchange(arrived, bits[0])
    top, total = attend_pages(
        group_size, devices, False, reuse, meta, turned, top, total,
        spread({0: arrived}, bits[1:]),
    )
    crossed, top = lax.optimization_barrier((crossed, top))
    return attend_pages(
        group_size, devices, True, reuse, meta, turned, top, total,
        spread({0: crossed}, bits[1:]),
    )[0]


def solution(mesh):
    placed = (
        P(("grp", "kv"), None),
        P(("grp", "kv"), None),
        P(("grp", "kv"), None, None),
        P(("grp", "kv"), None, None),
        P("kv", None),
        P(),
        P("grp", None),
    )
    return jax.shard_map(
        functools.partial(on_device, mesh.shape["grp"]),
        mesh=mesh,
        in_specs=placed,
        out_specs=P(("grp", "kv"), None),
        check_vma=False,
    )
```

time: 107 us -> 119 us (1.11)
  waiting for transfers between devices: 41.9 us -> 31.3 us
  local copies, waits for them, and re-layouts: 8.3 us -> 18.7 us
  starting transfers between devices: 28.4 us -> 38.3 us
  Pallas kernels: 20.9 us -> 24.8 us
  other arithmetic: 6.65 us -> 5.25 us
    ppermute x15 -> x17, waiting for transfers between devices: 23.2 us -> 9.92 us  [swap(): return lax.ppermute(value, axis, [(i, i ^ bit) for i in range(count)])]
    ppermute x2, waiting for transfers between devices: 0.75 us -> 11.1 us  [on_device(): received.append(lax.ppermute(message, ('grp', 'kv'), routes))]
    ppermute x15 -> x17, starting transfers between devices: 17.6 us -> 26.8 us  [swap(): return lax.ppermute(value, axis, [(i, i ^ bit) for i in range(count)])]
    unnamed x20 -> x52, local copies, waits for them, and re-layouts: 5.49 us -> 14.4 us
    ppermute x6 -> x3, waiting for transfers between devices: 17.9 us -> 10.3 us  [to_plane(): lax.ppermute(value, 'kv', [(i, (i + step) % devices) for i in range(devic...]
    ppermute x2, starting transfers between devices: 4.2 us -> 7.66 us  [on_device(): received.append(lax.ppermute(message, ('grp', 'kv'), routes))]
    ppermute x6 -> x3, starting transfers between devices: 6.61 us -> 3.79 us  [to_plane(): lax.ppermute(value, 'kv', [(i, (i + step) % devices) for i in range(devic...]
    pallas_call x2 -> x3, Pallas kernels: 17.9 us -> 20.4 us  [the longest x2 16.5 us: attend_pages(): pl.pallas_call(functools.partial(pages_kernel, group_size, last, last), i...]
  transfers between devices with their start and end apart: 23 -> 22, of which waited for: 12 -> 8; matrix products, arithmetic and copies ran while one was open for 11% -> 7% of each run, Pallas kernels for 14% -> 9%
where the time goes in v2:
time: 119 us
  starting transfers between devices  38.3 us (32%)
  waiting for transfers between devices  31.3 us (26%)
  Pallas kernels  24.8 us (21%)
  local copies, waits for them, and re-layouts  18.7 us (16%)
  other arithmetic  5.25 us (4%)
    ppermute x17, starting transfers between devices, swap(): return lax.ppermute(value, axis, [(i, i ^ bit) for i in range(count)])  26.8 us
    pallas_call x2, Pallas kernels, attend_pages(): pl.pallas_call(functools.partial(pages_kernel, group_size, last, last), i...  16.5 us
    unnamed x52, local copies, waits for them, and re-layouts  14.4 us
    ppermute x2, waiting for transfers between devices, on_device(): received.append(lax.ppermute(message, ('grp', 'kv'), routes))  11.1 us
    ppermute x3, waiting for transfers between devices, to_plane(): lax.ppermute(value, 'kv', [(i, (i + step) % devices) for i in range(devic...  10.3 us
    ppermute x17, waiting for transfers between devices, swap(): return lax.ppermute(value, axis, [(i, i ^ bit) for i in range(count)])  9.92 us
    ppermute x2, starting transfers between devices, on_device(): received.append(lax.ppermute(message, ('grp', 'kv'), routes))  7.66 us
    pallas_call x1, Pallas kernels, project(): pl.pallas_call(functools.partial(project_kernel, 8), in_specs=[in_smem] +...  4.45 us
  transfers between devices with their start and end apart: 22, of which 8 were waited for; matrix products, arithmetic and copies ran while one was open for 7% of the time, Pallas kernels for 9%

profile of v2, /device:TPU:5, one launch (start us, length us, event | category | flops | bytes accessed | tf_op | source)
XLA Modules:
  0.0 118.7 jit_solution(3294790102624768686)
XLA Ops:
  0.0 1.1 constant_dynamic-slice_fusion.4
  1.1 0.7 collective-permute-start
  1.8 1.2 %collective-permute-start.3 = (bf16[1,128,5120]{2,1,0:T(8,128)(2,1)}, bf16[1,128,5120]{2,1,0:T(8,128)(2,1)S(1)}, u32[]{:S(2)}, u32[]{:S(2)}) collective-permute-start(bf16[1,128,5120]{2,1,0:T(8,128)(2,1)} %refs_0_.1), channel_id=1, source_target_pairs={{0,16},{16,0},{1,17},{17,1},{2,18},{18,2},{3,19},{19,3},{4,20},{20... | collective-permute-start | bytes 3932168 | tf_op jit(solution)/shard_map/ppermute | solution.py:20
  3.0 0.8 slice_bitcast_fusion.1
  3.9 1.3 %collective-permute-start.1 = (bf16[640,256]{1,0:T(8,128)(2,1)S(1)}, bf16[640,256]{1,0:T(8,128)(2,1)}, u32[]{:S(2)}, u32[]{:S(2)}) collective-permute-start(bf16[640,256]{1,0:T(8,128)(2,1)S(1)} %maximum_select_fusion.refs_4_), channel_id=1, source_target_pairs={{0,4},{1,5},{2,6},{3,7},{4,8},{5,9},{6,10},{7,11},{8,12},{9,13},{1... | collective-permute-start | bytes 983048 | tf_op jit(solution)/shard_map/ppermute | solution.py:346
  5.5 2.2 %collective-permute-start.4 = (bf16[640,256]{1,0:T(8,128)(2,1)S(1)}, bf16[640,256]{1,0:T(8,128)(2,1)}, u32[]{:S(2)}, u32[]{:S(2)}) collective-permute-start(bf16[640,256]{1,0:T(8,128)(2,1)S(1)} %maximum_select_fusion.refs_4_), channel_id=1, source_target_pairs={{0,12},{1,13},{2,14},{3,15},{4,0},{5,1},{6,2},{7,3},{8,4},{9,5},{1... | collective-permute-start | bytes 983048 | tf_op jit(solution)/shard_map/ppermute | solution.py:346
  7.7 7.3 %collective-permute-done.1.refs_6_ = bf16[640,256]{1,0:T(8,128)(2,1)} collective-permute-done((bf16[640,256]{1,0:T(8,128)(2,1)S(1)}, bf16[640,256]{1,0:T(8,128)(2,1)}, u32[]{:S(2)}, u32[]{:S(2)}) %collective-permute-start.1) | collective-permute-done | bytes 327712 | tf_op jit(solution)/shard_map/ppermute | solution.py:346
  15.8 0.9 fusion.1
  16.7 1.3 %collective-permute-start.10 = (bf16[256,256]{1,0:T(8,128)(2,1)S(1)}, bf16[256,256]{1,0:T(8,128)(2,1)S(1)}, u32[]{:S(2)}, u32[]{:S(2)}) collective-permute-start(bf16[256,256]{1,0:T(8,128)(2,1)S(1)} %pad_maximum_fusion.5.refs_0_), channel_id=1, source_target_pairs={{0,2},{1,3},{2,0},{3,1},{4,6},{5,7},{6,4},{7,5},{8,10},{9,11},{10,... | collective-permute-start | bytes 393224 | tf_op jit(solution)/shard_map/ppermute | solution.py:20
  18.0 0.8 dynamic-slice_convert_fusion
  19.1 3.0 %collective-permute-done.4.refs_8_ = bf16[640,256]{1,0:T(8,128)(2,1)} collective-permute-done((bf16[640,256]{1,0:T(8,128)(2,1)S(1)}, bf16[640,256]{1,0:T(8,128)(2,1)}, u32[]{:S(2)}, u32[]{:S(2)}) %collective-permute-start.4) | collective-permute-done | bytes 327712 | tf_op jit(solution)/shard_map/ppermute | solution.py:346
  23.0 5.0 %collective-permute-start.9 = (bf16[256,256]{1,0:T(8,128)(2,1)S(1)}, bf16[256,256]{1,0:T(8,128)(2,1)S(1)}, u32[]{:S(2)}, u32[]{:S(2)}) collective-permute-start(bf16[256,256]{1,0:T(8,128)(2,1)S(1)} %pad_maximum_fusion.5.refs_0_), channel_id=1, source_target_pairs={{0,1},{1,0},{2,3},{3,2},{4,5},{5,4},{6,7},{7,6},{8,9},{9,8},{10,11... | collective-permute-start | bytes 393224 | tf_op jit(solution)/shard_map/ppermute | solution.py:20
  28.0 0.6 copy-done.6
  28.7 1.6 %collective-permute-start.11 = (bf16[256,256]{1,0:T(8,128)(2,1)S(1)}, bf16[256,256]{1,0:T(8,128)(2,1)S(1)}, u32[]{:S(2)}, u32[]{:S(2)}) collective-permute-start(bf16[256,256]{1,0:T(8,128)(2,1)S(1)} %collective-permute-done.10.refs_2_), channel_id=1, source_target_pairs={{0,1},{1,0},{2,3},{3,2},{4,5},{5,4},{6,7},{7,6},{8,9},{9,8},{10,11... | collective-permute-start | bytes 393224 | tf_op jit(solution)/shard_map/ppermute | solution.py:20
  31.0 0.7 constant_dynamic-slice_fusion.1
  32.3 0.6 copy-done.15
  33.0 0.9 copy-done.7
  33.9 0.9 copy-done.8
  34.8 0.9 copy-done.9
  35.7 1.0 copy-done.10
  36.7 0.9 copy-done.12
  37.6 0.9 copy-done.14
  38.5 0.9 copy-done.16
  39.4 3.8 %extension.1 = (bf16[5,256,128]{2,1,0:T(8,128)(2,1)S(1)}, f32[5,256,128]{2,1,0:T(8,128)S(1)}, f32[5,256,256]{2,1,0:T(8,128)S(1)}) custom-call(s32[3]{0:T(128)S(1)} %pad_add_fusion.meta, bf16[256,640]{1,0:T(8,128)(2,1)S(1)} %copy-done.10, f32[256,128]{1,0:T(8,128)S(1)} %copy-done.9, f32[256,128]{1,0:T(8,128)S(1)} %copy-done.8, ...), custom_call_target="tpu_custom_call" | custom-call | flops 671088640 | bytes 524288 | tf_op jit(solution)/shard_map/extension/pallas_call | solution.py:188
  43.3 1.1 copy-done.17
  44.4 0.8 copy-done.21
  45.6 0.7 constant_dynamic-slice_fusion.2
  46.3 1.2 %collective-permute-start.15 = (bf16[2,128,512]{2,1,0:T(8,128)(2,1)}, bf16[2,128,512]{2,1,0:T(8,128)(2,1)}, u32[]{:S(2)}, u32[]{:S(2)}) collective-permute-start(bf16[2,128,512]{2,1,0:T(8,128)(2,1)} %constant_dynamic-slice_fusion.2), channel_id=1, source_target_pairs={{0,16},{16,0},{1,17},{17,1},{2,18},{18,2},{3,19},{19,3},{4,20},{20... | collective-permute-start | bytes 786440 | tf_op jit(solution)/shard_map/ppermute | solution.py:20
  47.5 0.8 collective-permute-start.13
  49.0 5.0 %collective-permute-done.15.refs_13_ = bf16[2,128,512]{2,1,0:T(8,128)(2,1)} collective-permute-done((bf16[2,128,512]{2,1,0:T(8,128)(2,1)}, bf16[2,128,512]{2,1,0:T(8,128)(2,1)}, u32[]{:S(2)}, u32[]{:S(2)}) %collective-permute-start.15) | collective-permute-done | bytes 262176 | tf_op jit(solution)/shard_map/ppermute | solution.py:20
  53.9 0.9 constant_dynamic-slice_fusion
  54.9 1.0 pad_maximum_fusion
  55.9 1.4 %collective-permute-start.16 = (bf16[4,128,256]{2,1,0:T(8,128)(2,1)S(1)}, bf16[4,128,256]{2,1,0:T(8,128)(2,1)S(1)}, u32[]{:S(2)}, u32[]{:S(2)}) collective-permute-start(bf16[4,128,256]{2,1,0:T(8,128)(2,1)S(1)} %pad_maximum_fusion), channel_id=1, source_target_pairs={{0,1},{1,0},{2,3},{3,2},{4,5},{5,4},{6,7},{7,6},{8,9},{9,8},{10,11... | collective-permute-start | bytes 786440 | tf_op jit(solution)/shard_map/ppermute | solution.py:20
  57.3 1.0 fusion.2
  58.6 4.5 %project.1 = (bf16[4,128,256]{2,1,0:T(8,128)(2,1)S(1)}, bf16[4,128,256]{2,1,0:T(8,128)(2,1)S(1)}) custom-call(s32[20]{0:T(128)S(1)} %concatenate.51.meta, bf16[1,128,5120]{2,1,0:T(8,128)(2,1)S(1)} %copy-done.1, bf16[1,128,5120]{2,1,0:T(8,128)(2,1)} %collective-permute-done.13.refs_1_, bf16[1,128,5120]{2,1,0:T(8,128)(2,1)S(1)} %collective-permute-done.3.refs_2_, ...), custom_call_target="tpu_custom_call" | custom-call | flops 1342177280 | bytes 7864320 | tf_op jit(solution)/shard_map/project/pallas_call | solution.py:82
  63.0 1.9 %collective-permute-start.17 = (bf16[4,128,256]{2,1,0:T(8,128)(2,1)S(1)}, bf16[4,128,256]{2,1,0:T(8,128)(2,1)S(1)}, u32[]{:S(2)}, u32[]{:S(2)}) collective-permute-start(bf16[4,128,256]{2,1,0:T(8,128)(2,1)S(1)} %get-tuple-element.37), channel_id=1, source_target_pairs={{0,0},{1,4},{2,2},{3,6},{4,1},{5,5},{6,3},{7,7},{8,16},{9,20},{10,... | collective-permute-start | bytes 786440 | tf_op jit(solution)/shard_map/ppermute | solution.py:467
  65.0 5.7 %collective-permute-start.18 = (bf16[4,128,256]{2,1,0:T(8,128)(2,1)S(1)}, bf16[4,128,256]{2,1,0:T(8,128)(2,1)S(1)}, u32[]{:S(2)}, u32[]{:S(2)}) collective-permute-start(bf16[4,128,256]{2,1,0:T(8,128)(2,1)S(1)} %get-tuple-element.38), channel_id=1, source_target_pairs={{0,16},{1,20},{2,18},{3,22},{4,17},{5,21},{6,19},{7,23},{8,0},{9,4... | collective-permute-start | bytes 786440 | tf_op jit(solution)/shard_map/ppermute | solution.py:467
  70.7 11.1 %collective-permute-done.18 = bf16[4,128,256]{2,1,0:T(8,128)(2,1)S(1)} collective-permute-done((bf16[4,128,256]{2,1,0:T(8,128)(2,1)S(1)}, bf16[4,128,256]{2,1,0:T(8,128)(2,1)S(1)}, u32[]{:S(2)}, u32[]{:S(2)}) %collective-permute-start.18) | collective-permute-done | bytes 262176 | tf_op jit(solution)/shard_map/ppermute | solution.py:467
  81.8 11.5 %collective-permute-start.20 = (bf16[8,128,256]{2,1,0:T(8,128)(2,1)S(1)}, bf16[8,128,256]{2,1,0:T(8,128)(2,1)S(1)}, u32[]{:S(2)}, u32[]{:S(2)}) collective-permute-start(bf16[8,128,256]{2,1,0:T(8,128)(2,1)S(1)} %constant_dynamic-update-slice_fusion.refs_0_), channel_id=1, source_target_pairs={{0,1},{1,0},{2,3},{3,2},{4,5},{5,4},{6,7},{7,6},{8,9},{9,8},{10,11... | collective-permute-start | bytes 1572872 | tf_op jit(solution)/shard_map/ppermute | solution.py:20
  93.5 1.4 %collective-permute-done.20.refs_1_ = bf16[8,128,256]{2,1,0:T(8,128)(2,1)S(1)} collective-permute-done((bf16[8,128,256]{2,1,0:T(8,128)(2,1)S(1)}, bf16[8,128,256]{2,1,0:T(8,128)(2,1)S(1)}, u32[]{:S(2)}, u32[]{:S(2)}) %collective-permute-start.20) | collective-permute-done | bytes 524320 | tf_op jit(solution)/shard_map/ppermute | solution.py:20
  94.9 1.3 %copy-done.18 = f32[5,256,256]{2,1,0:T(8,128)S(1)} copy-done((f32[5,256,256]{2,1,0:T(8,128)S(1)}, f32[5,256,256]{2,1,0:T(8,128)}, u32[]{:S(2)}) %copy-start.18) | copy-done | bytes 1310744
  96.2 1.0 copy-done.20
  97.2 1.1 copy-done.22
  98.3 7.2 %column.1 = (f32[5,256,128]{2,1,0:T(8,128)S(1)}, f32[5,256,256]{2,1,0:T(8,128)S(1)}) custom-call(s32[28,3]{1,0:T(8,128)S(1)} %copy.11.reuse, s32[3]{0:T(128)S(1)} %pad_add_fusion.meta, bf16[5,256,128]{2,1,0:T(8,128)(2,1)S(1)} %copy-done.20, f32[5,256,128]{2,1,0:T(8,128)S(1)} %copy-done.22, f32[5,256,256]{2,1,0:T(8,128)S(1)} %copy-done.18, ...), custom_call_target="tpu_custom_call" | custom-call | flops 1174405120 | bytes 917504 | tf_op jit(solution)/shard_map/column/pallas_call | solution.py:291
  105.5 1.3 %collective-permute-done.19.refs_0_ = bf16[8,128,256]{2,1,0:T(8,128)(2,1)S(1)} collective-permute-done((bf16[8,128,256]{2,1,0:T(8,128)(2,1)S(1)}, bf16[8,128,256]{2,1,0:T(8,128)(2,1)S(1)}, u32[]{:S(2)}, u32[]{:S(2)}) %collective-permute-start.19) | collective-permute-done | bytes 524320 | tf_op jit(solution)/shard_map/ppermute | solution.py:20
  106.9 0.8 collective-permute-start.21
  107.7 1.5 %collective-permute-done.21.refs_1_ = bf16[8,128,256]{2,1,0:T(8,128)(2,1)S(1)} collective-permute-done((bf16[8,128,256]{2,1,0:T(8,128)(2,1)S(1)}, bf16[8,128,256]{2,1,0:T(8,128)(2,1)S(1)}, u32[]{:S(2)}, u32[]{:S(2)}) %collective-permute-start.21) | collective-permute-done | bytes 524320 | tf_op jit(solution)/shard_map/ppermute | solution.py:20
  109.3 9.3 %beside.1 = bf16[256,640]{1,0:T(8,128)(2,1)} custom-call(s32[28,3]{1,0:T(8,128)S(1)} %copy.11.reuse, s32[3]{0:T(128)S(1)} %pad_add_fusion.meta, bf16[5,256,128]{2,1,0:T(8,128)(2,1)S(1)} %copy-done.20, f32[5,256,128]{2,1,0:T(8,128)S(1)} %get-tuple-element.42.top_in, f32[5,256,256]{2,1,0:T(8,128)S(1)} %get-tuple-element.43.sum_in, ...), custom_call_target="tpu_custom_call" | custom-call | flops 1174405120 | bytes 917504 | tf_op jit(solution)/shard_map/beside/pallas_call | solution.py:291
  (83 shorter events, 5.2 us)
Async XLA Ops:
  0.0 5.5 %copy-start.24 = (s32[28,3]{0,1:T(4,128)S(1)}, s32[28,3]{0,1:T(4,128)}, u32[]{:S(2)}) copy-start(s32[28,3]{0,1:T(4,128)} %param.13) | copy-start | bytes 1012
  0.0 15.3 %copy-start.23 = (bf16[256,256]{1,0:T(8,128)(2,1)S(1)}, bf16[256,256]{1,0:T(8,128)(2,1)}, u32[]{:S(2)}) copy-start(bf16[256,256]{1,0:T(8,128)(2,1)} %param.8) | copy-start | bytes 393220
  1.1 2.7 %collective-permute-start = (bf16[320,256]{1,0:T(8,128)(2,1)S(1)}, bf16[320,256]{1,0:T(8,128)(2,1)S(1)}, u32[]{:S(2)}, u32[]{:S(2)}) collective-permute-start(bf16[320,256]{1,0:T(8,128)(2,1)S(1)} %get-tuple-element.56), channel_id=1, source_target_pairs={{0,1},{1,0},{2,3},{3,2},{4,5},{5,4},{6,7},{7,6},{8,9},{9,8},{10,11... | collective-permute-start | bytes 491528 | tf_op jit(solution)/shard_map/ppermute | solution.py:20
  1.8 43.4 %collective-permute-start.3 = (bf16[1,128,5120]{2,1,0:T(8,128)(2,1)}, bf16[1,128,5120]{2,1,0:T(8,128)(2,1)S(1)}, u32[]{:S(2)}, u32[]{:S(2)}) collective-permute-start(bf16[1,128,5120]{2,1,0:T(8,128)(2,1)} %refs_0_.1), channel_id=1, source_target_pairs={{0,16},{16,0},{1,17},{17,1},{2,18},{18,2},{3,19},{19,3},{4,20},{20... | collective-permute-start | bytes 3932168 | tf_op jit(solution)/shard_map/ppermute | solution.py:20
  3.9 11.1 %collective-permute-start.1 = (bf16[640,256]{1,0:T(8,128)(2,1)S(1)}, bf16[640,256]{1,0:T(8,128)(2,1)}, u32[]{:S(2)}, u32[]{:S(2)}) collective-permute-start(bf16[640,256]{1,0:T(8,128)(2,1)S(1)} %maximum_select_fusion.refs_4_), channel_id=1, source_target_pairs={{0,4},{1,5},{2,6},{3,7},{4,8},{5,9},{6,10},{7,11},{8,12},{9,13},{1... | collective-permute-start | bytes 983048 | tf_op jit(solution)/shard_map/ppermute | solution.py:346
  5.3 9.7 %collective-permute-start.5 = (bf16[640,256]{1,0:T(8,128)(2,1)S(1)}, bf16[640,256]{1,0:T(8,128)(2,1)S(1)}, u32[]{:S(2)}, u32[]{:S(2)}) collective-permute-start(bf16[640,256]{1,0:T(8,128)(2,1)S(1)} %maximum_select_fusion.refs_4_), channel_id=1, source_target_pairs={{0,2},{1,3},{2,0},{3,1},{4,6},{5,7},{6,4},{7,5},{8,10},{9,11},{10,... | collective-permute-start | bytes 983048 | tf_op jit(solution)/shard_map/ppermute | solution.py:20
  5.5 16.5 %collective-permute-start.4 = (bf16[640,256]{1,0:T(8,128)(2,1)S(1)}, bf16[640,256]{1,0:T(8,128)(2,1)}, u32[]{:S(2)}, u32[]{:S(2)}) collective-permute-start(bf16[640,256]{1,0:T(8,128)(2,1)S(1)} %maximum_select_fusion.refs_4_), channel_id=1, source_target_pairs={{0,12},{1,13},{2,14},{3,15},{4,0},{5,1},{6,2},{7,3},{8,4},{9,5},{1... | collective-permute-start | bytes 983048 | tf_op jit(solution)/shard_map/ppermute | solution.py:346
  15.0 16.0 %copy-start.2 = (bf16[640,256]{1,0:T(8,128)(2,1)}, bf16[640,256]{1,0:T(8,128)(2,1)S(1)}, u32[]{:S(2)}) copy-start(bf16[640,256]{1,0:T(8,128)(2,1)S(1)} %collective-permute-done.5.refs_5_) | copy-start | bytes 983044
  15.0 7.6 %collective-permute-start.6 = (bf16[640,256]{1,0:T(8,128)(2,1)}, bf16[640,256]{1,0:T(8,128)(2,1)S(1)}, u32[]{:S(2)}, u32[]{:S(2)}) collective-permute-start(bf16[640,256]{1,0:T(8,128)(2,1)} %collective-permute-done.1.refs_6_), channel_id=1, source_target_pairs={{0,2},{1,3},{2,0},{3,1},{4,6},{5,7},{6,4},{7,5},{8,10},{9,11},{10,... | collective-permute-start | bytes 983048 | tf_op jit(solution)/shard_map/ppermute | solution.py:20
  15.3 15.8 %copy-start = (bf16[2,128,1024]{2,1,0:T(8,128)(2,1)S(1)}, bf16[2,128,1024]{2,1,0:T(8,128)(2,1)}, u32[]{:S(2)}) copy-start(bf16[2,128,1024]{2,1,0:T(8,128)(2,1)} %refs_12_.1) | copy-start | bytes 1572868
  16.7 12.0 %collective-permute-start.10 = (bf16[256,256]{1,0:T(8,128)(2,1)S(1)}, bf16[256,256]{1,0:T(8,128)(2,1)S(1)}, u32[]{:S(2)}, u32[]{:S(2)}) collective-permute-start(bf16[256,256]{1,0:T(8,128)(2,1)S(1)} %pad_maximum_fusion.5.refs_0_), channel_id=1, source_target_pairs={{0,2},{1,3},{2,0},{3,1},{4,6},{5,7},{6,4},{7,5},{8,10},{9,11},{10,... | collective-permute-start | bytes 393224 | tf_op jit(solution)/shard_map/ppermute | solution.py:20
  18.8 26.4 %collective-permute-start.2 = (bf16[640,256]{1,0:T(8,128)(2,1)}, bf16[640,256]{1,0:T(8,128)(2,1)}, u32[]{:S(2)}, u32[]{:S(2)}) collective-permute-start(bf16[640,256]{1,0:T(8,128)(2,1)} %collective-permute-done.1.refs_6_), channel_id=1, source_target_pairs={{0,4},{1,5},{2,6},{3,7},{4,8},{5,9},{6,10},{7,11},{8,12},{9,13},{1... | collective-permute-start | bytes 983048 | tf_op jit(solution)/shard_map/ppermute | solution.py:346
  22.6 10.4 %copy-start.4 = (bf16[640,256]{1,0:T(8,128)(2,1)}, bf16[640,256]{1,0:T(8,128)(2,1)S(1)}, u32[]{:S(2)}) copy-start(bf16[640,256]{1,0:T(8,128)(2,1)S(1)} %collective-permute-done.6.refs_7_) | copy-start | bytes 983044
  22.6 22.6 %collective-permute-start.7 = (bf16[640,256]{1,0:T(8,128)(2,1)}, bf16[640,256]{1,0:T(8,128)(2,1)}, u32[]{:S(2)}, u32[]{:S(2)}) collective-permute-start(bf16[640,256]{1,0:T(8,128)(2,1)} %collective-permute-done.4.refs_8_), channel_id=1, source_target_pairs={{0,2},{1,3},{2,0},{3,1},{4,6},{5,7},{6,4},{7,5},{8,10},{9,11},{10,... | collective-permute-start | bytes 983048 | tf_op jit(solution)/shard_map/ppermute | solution.py:20
  23.0 8.7 %collective-permute-start.9 = (bf16[256,256]{1,0:T(8,128)(2,1)S(1)}, bf16[256,256]{1,0:T(8,128)(2,1)S(1)}, u32[]{:S(2)}, u32[]{:S(2)}) collective-permute-start(bf16[256,256]{1,0:T(8,128)(2,1)S(1)} %pad_maximum_fusion.5.refs_0_), channel_id=1, source_target_pairs={{0,1},{1,0},{2,3},{3,2},{4,5},{5,4},{6,7},{7,6},{8,9},{9,8},{10,11... | collective-permute-start | bytes 393224 | tf_op jit(solution)/shard_map/ppermute | solution.py:20
  28.0 0.7 copy-start.6
  28.7 3.7 %collective-permute-start.11 = (bf16[256,256]{1,0:T(8,128)(2,1)S(1)}, bf16[256,256]{1,0:T(8,128)(2,1)S(1)}, u32[]{:S(2)}, u32[]{:S(2)}) collective-permute-start(bf16[256,256]{1,0:T(8,128)(2,1)S(1)} %collective-permute-done.10.refs_2_), channel_id=1, source_target_pairs={{0,1},{1,0},{2,3},{3,2},{4,5},{5,4},{6,7},{7,6},{8,9},{9,8},{10,11... | collective-permute-start | bytes 393224 | tf_op jit(solution)/shard_map/ppermute | solution.py:20
  30.3 0.6 copy-start.11
  31.7 0.6 copy-start.13
  32.3 0.6 copy-start.15
  33.0 0.9 copy-start.7
  33.9 0.9 copy-start.8
  34.8 0.9 copy-start.9
  35.7 1.0 copy-start.10
  36.7 0.9 copy-start.12
  37.6 0.9 copy-start.14
  38.5 0.9 copy-start.16
  39.4 8.1 %copy-start.1 = (bf16[1,128,5120]{2,1,0:T(8,128)(2,1)S(1)}, bf16[1,128,5120]{2,1,0:T(8,128)(2,1)}, u32[]{:S(2)}) copy-start(bf16[1,128,5120]{2,1,0:T(8,128)(2,1)} %refs_0_.1) | copy-start | bytes 3932164
  43.2 1.1 copy-start.17
  44.4 0.8 copy-start.21
  45.2 3.6 %copy-start.19 = (bf16[5,256,128]{2,1,0:T(8,128)(2,1)}, bf16[5,256,128]{2,1,0:T(8,128)(2,1)S(1)}, u32[]{:S(2)}) copy-start(bf16[5,256,128]{2,1,0:T(8,128)(2,1)S(1)} %get-tuple-element.31.turned) | copy-start | bytes 983044
  45.2 3.0 %collective-permute-start.12 = (s32[28,3]{0,1:T(4,128)S(1)}, s32[28,3]{0,1:T(4,128)S(1)}, u32[]{:S(2)}, u32[]{:S(2)}) collective-permute-start(s32[28,3]{0,1:T(4,128)S(1)} %copy-done.24), channel_id=1, source_target_pairs={{0,16},{16,0},{1,17},{17,1},{2,18},{18,2},{3,19},{19,3},{4,20},{20... | collective-permute-start | bytes 1016 | tf_op jit(solution)/shard_map/ppermute | solution.py:20
  45.6 13.0 %collective-permute-start.8 = (bf16[1,128,5120]{2,1,0:T(8,128)(2,1)S(1)}, bf16[1,128,5120]{2,1,0:T(8,128)(2,1)}, u32[]{:S(2)}, u32[]{:S(2)}) collective-permute-start(bf16[1,128,5120]{2,1,0:T(8,128)(2,1)S(1)} %collective-permute-done.3.refs_2_), channel_id=1, source_target_pairs={{0,1},{1,0},{2,3},{3,2},{4,5},{5,4},{6,7},{7,6},{8,9},{9,8},{10,11... | collective-permute-start | bytes 3932168 | tf_op jit(solution)/shard_map/ppermute | solution.py:20
  46.3 7.7 %collective-permute-start.15 = (bf16[2,128,512]{2,1,0:T(8,128)(2,1)}, bf16[2,128,512]{2,1,0:T(8,128)(2,1)}, u32[]{:S(2)}, u32[]{:S(2)}) collective-permute-start(bf16[2,128,512]{2,1,0:T(8,128)(2,1)} %constant_dynamic-slice_fusion.2), channel_id=1, source_target_pairs={{0,16},{16,0},{1,17},{17,1},{2,18},{18,2},{3,19},{19,3},{4,20},{20... | collective-permute-start | bytes 786440 | tf_op jit(solution)/shard_map/ppermute | solution.py:20
  47.5 11.1 %collective-permute-start.13 = (bf16[1,128,5120]{2,1,0:T(8,128)(2,1)S(1)}, bf16[1,128,5120]{2,1,0:T(8,128)(2,1)}, u32[]{:S(2)}, u32[]{:S(2)}) collective-permute-start(bf16[1,128,5120]{2,1,0:T(8,128)(2,1)S(1)} %copy-done.1), channel_id=1, source_target_pairs={{0,1},{1,0},{2,3},{3,2},{4,5},{5,4},{6,7},{7,6},{8,9},{9,8},{10,11... | collective-permute-start | bytes 3932168 | tf_op jit(solution)/shard_map/ppermute | solution.py:20
  48.3 10.3 %collective-permute-start.14 = (bf16[640,256]{1,0:T(8,128)(2,1)}, bf16[640,256]{1,0:T(8,128)(2,1)}, u32[]{:S(2)}, u32[]{:S(2)}) collective-permute-start(bf16[640,256]{1,0:T(8,128)(2,1)} %collective-permute-done.2.refs_10_), channel_id=1, source_target_pairs={{0,2},{1,3},{2,0},{3,1},{4,6},{5,7},{6,4},{7,5},{8,10},{9,11},{10,... | collective-permute-start | bytes 983048 | tf_op jit(solution)/shard_map/ppermute | solution.py:20
  54.9 3.7 %copy-start.3 = (bf16[640,256]{1,0:T(8,128)(2,1)S(1)}, bf16[640,256]{1,0:T(8,128)(2,1)}, u32[]{:S(2)}) copy-start(bf16[640,256]{1,0:T(8,128)(2,1)} %copy-done.2) | copy-start | bytes 983044
  54.9 3.7 %copy-start.5 = (bf16[640,256]{1,0:T(8,128)(2,1)S(1)}, bf16[640,256]{1,0:T(8,128)(2,1)}, u32[]{:S(2)}) copy-start(bf16[640,256]{1,0:T(8,128)(2,1)} %copy-done.4) | copy-start | bytes 983044
  55.9 2.7 %collective-permute-start.16 = (bf16[4,128,256]{2,1,0:T(8,128)(2,1)S(1)}, bf16[4,128,256]{2,1,0:T(8,128)(2,1)S(1)}, u32[]{:S(2)}, u32[]{:S(2)}) collective-permute-start(bf16[4,128,256]{2,1,0:T(8,128)(2,1)S(1)} %pad_maximum_fusion), channel_id=1, source_target_pairs={{0,1},{1,0},{2,3},{3,2},{4,5},{5,4},{6,7},{7,6},{8,9},{9,8},{10,11... | collective-permute-start | bytes 786440 | tf_op jit(solution)/shard_map/ppermute | solution.py:20
  63.0 7.7 %collective-permute-start.17 = (bf16[4,128,256]{2,1,0:T(8,128)(2,1)S(1)}, bf16[4,128,256]{2,1,0:T(8,128)(2,1)S(1)}, u32[]{:S(2)}, u32[]{:S(2)}) collective-permute-start(bf16[4,128,256]{2,1,0:T(8,128)(2,1)S(1)} %get-tuple-element.37), channel_id=1, source_target_pairs={{0,0},{1,4},{2,2},{3,6},{4,1},{5,5},{6,3},{7,7},{8,16},{9,20},{10,... | collective-permute-start | bytes 786440 | tf_op jit(solution)/shard_map/ppermute | solution.py:467
  65.0 16.8 %collective-permute-start.18 = (bf16[4,128,256]{2,1,0:T(8,128)(2,1)S(1)}, bf16[4,128,256]{2,1,0:T(8,128)(2,1)S(1)}, u32[]{:S(2)}, u32[]{:S(2)}) collective-permute-start(bf16[4,128,256]{2,1,0:T(8,128)(2,1)S(1)} %get-tuple-element.38), channel_id=1, source_target_pairs={{0,16},{1,20},{2,18},{3,22},{4,17},{5,21},{6,19},{7,23},{8,0},{9,4... | collective-permute-start | bytes 786440 | tf_op jit(solution)/shard_map/ppermute | solution.py:467
  81.8 13.1 %collective-permute-start.20 = (bf16[8,128,256]{2,1,0:T(8,128)(2,1)S(1)}, bf16[8,128,256]{2,1,0:T(8,128)(2,1)S(1)}, u32[]{:S(2)}, u32[]{:S(2)}) collective-permute-start(bf16[8,128,256]{2,1,0:T(8,128)(2,1)S(1)} %constant_dynamic-update-slice_fusion.refs_0_), channel_id=1, source_target_pairs={{0,1},{1,0},{2,3},{3,2},{4,5},{5,4},{6,7},{7,6},{8,9},{9,8},{10,11... | collective-permute-start | bytes 1572872 | tf_op jit(solution)/shard_map/ppermute | solution.py:20
  93.4 13.5 %collective-permute-start.19 = (bf16[8,128,256]{2,1,0:T(8,128)(2,1)S(1)}, bf16[8,128,256]{2,1,0:T(8,128)(2,1)S(1)}, u32[]{:S(2)}, u32[]{:S(2)}) collective-permute-start(bf16[8,128,256]{2,1,0:T(8,128)(2,1)S(1)} %constant_dynamic-update-slice_fusion.refs_0_), channel_id=1, source_target_pairs={{0,2},{1,3},{2,0},{3,1},{4,6},{5,7},{6,4},{7,5},{8,10},{9,11},{10,... | collective-permute-start | bytes 1572872 | tf_op jit(solution)/shard_map/ppermute | solution.py:20
  94.9 1.3 %copy-start.18 = (f32[5,256,256]{2,1,0:T(8,128)S(1)}, f32[5,256,256]{2,1,0:T(8,128)}, u32[]{:S(2)}) copy-start(f32[5,256,256]{2,1,0:T(8,128)} %copy-done.17) | copy-start | bytes 3932164
  96.2 1.0 copy-start.20
  97.2 1.1 copy-start.22
  106.9 2.4 %collective-permute-start.21 = (bf16[8,128,256]{2,1,0:T(8,128)(2,1)S(1)}, bf16[8,128,256]{2,1,0:T(8,128)(2,1)S(1)}, u32[]{:S(2)}, u32[]{:S(2)}) collective-permute-start(bf16[8,128,256]{2,1,0:T(8,128)(2,1)S(1)} %collective-permute-done.19.refs_0_), channel_id=1, source_target_pairs={{0,1},{1,0},{2,3},{3,2},{4,5},{5,4},{6,7},{7,6},{8,9},{9,8},{10,11... | collective-permute-start | bytes 1572872 | tf_op jit(solution)/shard_map/ppermute | solution.py:20

commit v3 on v1

--- a/solution.py
+++ b/solution.py
@@ -253,13 +253,13 @@
     device = slot // slots
     source, relative = device // 4, meta[1] ^ (device % 4)
     shift = (meta[0] - source) & 3
-    return (relative & 1) * 2 + (relative >> 1), (shift ^ (shift >> 1)) * slots + slot % slots
+    return (relative & 1) * 6 + (shift ^ (shift >> 1)), (relative >> 1) * slots + slot % slots
 
 
 def fresh_place(group_size, meta, device):
     source, spot = device // group_size, device % group_size
     holder = (spot - (spot & 1)) + (source & 1)
-    index = ((source >> 1) ^ meta[2]) * 2 + ((spot ^ meta[0]) & 1)
+    index = ((source >> 1) ^ meta[2]) * 2 + ((spot ^ (meta[0] >> 1)) & 1)
     return meta[1] ^ holder, index
 
 
@@ -338,8 +338,8 @@
 
     hidden_across = swap(prefix_hidden, "grp", 1, parts)
 
-    target = 2 * side + core
-    spare = 2 * side + (1 - core)
+    target = 2 * core + side
+    spare = 2 * (1 - core) + side
     mine = lax.dynamic_slice_in_dim(kv_weight, target * PAIR, PAIR, 1)
     other = exchange(lax.dynamic_slice_in_dim(kv_weight, spare * PAIR, PAIR, 1), 1)
     chip_rows = jnp.where(
@@ -361,25 +361,31 @@
             step = shift * group_size
             return lax.ppermute(value, "kv", [(i, (i + step) % devices) for i in range(devices)])
 
-        own_part = stored_for(page_store, head)
-        others = [
-            to_plane(stored_for(page_store, (head + shift) & (HEADS - 1)), shift)
-            for shift in (1, 3, 2)
-        ]
-        near = to_plane(chip_rows, 1)
-        again, others = lax.optimization_barrier((chip_rows, others))
-        back = to_plane(again, 3)
+        near, back = to_plane(chip_rows, 1), to_plane(chip_rows, 3)
         beside_own = exchange(chip_rows, 2)
+        store_beside = exchange(page_store, 2)
         far = to_plane(near, 1)
         near_sent, _ = lax.optimization_barrier((near, beside_own))
         beside_near = exchange(near_sent, 2)
-        back_sent, _ = lax.optimization_barrier((back, beside_near))
+        back_sent, store_beside, _ = lax.optimization_barrier((back, store_beside, beside_near))
         beside_back = exchange(back_sent, 2)
-        far_sent, hidden_mine, hidden_passed, reuse_sent, _ = lax.optimization_barrier(
-            (far, prefix_hidden, hidden_across, reuse, beside_back)
+        far_sent, hidden_mine, hidden_passed, reuse_sent, stores, _ = lax.optimization_barrier(
+            (far, prefix_hidden, hidden_across, reuse, (page_store, store_beside), beside_back)
         )
         hidden_core = exchange(hidden_mine, 1)
         beside_far = exchange(far_sent, 2)
+        def parts_for(shift):
+            return as_pages(*[stored_for(store, (head + shift) & (HEADS - 1)) for store in stores])
+
+        others = [
+            lax.ppermute(
+                parts_for(shift),
+                "kv",
+                [(i, (i + shift * group_size) % devices) for i in range(devices)],
+            )
+            for shift in (1, 3, 2)
+        ]
+        own_parts = parts_for(0)
         weights = [chip_rows, beside_own, near, beside_near, back, beside_back, far, beside_far]
         for shift in (0, 1, 3, 2):
             chip = (((head - shift) & (HEADS - 1)) << 1) | (slice_index >> 1)
@@ -408,10 +414,10 @@
     own_block = jnp.concatenate([own_keys.astype(jnp.bfloat16), ext_kv[:, HEAD_DIM:]], axis=1)
 
     if group_size == 4:
-        gathered, beside_far = lax.optimization_barrier(
-            (as_pages(own_part, *others, own_block), weights[-1])
-        )
-        gathered_beside = exchange(gathered, 2)
+        own_sent, _ = lax.optimization_barrier((own_block, weights[5]))
+        block_beside = as_pages(exchange(own_sent, 2))
+        own_pages = as_pages(own_block)
+        own_cores = [exchange(own_parts, 1), exchange(own_pages, 1)]
 
     def page_numbers(table):
         match = (table[:, 0] == 0)[:, None] & (
@@ -445,7 +451,7 @@
                 plane, spot = device // group_size, device % group_size
                 to_part = (part & ~1) | ((plane >> 1) ^ turn)
                 to_spot = (spot & ~1) | (plane & 1)
-                to_head = 2 * (part & 1) + (spot & 1)
+                to_head = 2 * (spot & 1) + (part & 1)
                 routes.append(
                     (part * devices + device, to_part * devices + to_head * group_size + to_spot)
                 )
@@ -462,10 +468,18 @@
         return [pieces[relative] for relative in range(group_size)]
 
     if group_size == 4:
-        pieces, _ = lax.optimization_barrier(([gathered, gathered_beside], received))
-        pieces += [exchange(piece, 1) for piece in pieces]
+        others, block_beside = lax.optimization_barrier(
+            ((others, block_beside), received)
+        )[0]
+        pieces = [own_parts, *others, own_pages, block_beside]
+        pieces += [
+            own_cores[0],
+            *[exchange(piece, 1) for piece in others],
+            own_cores[1],
+            exchange(block_beside, 1),
+        ]
         place = place_apart
-        extension_at = lambda relative: ((relative & 1) * 2 + (relative >> 1), HEADS * slots)
+        extension_at = lambda relative: ((relative & 1) * 6 + 4 + (relative >> 1), 0)
     else:
         per_head = page_store.reshape(slots, page_rows, HEADS, PAIR).transpose(2, 0, 1, 3)
         arrived = between_planes(per_head.reshape(HEADS * slots, page_rows, PAIR))

time: 107 us -> 107 us (level)
  local copies, waits for them, and re-layouts: 8.3 us -> 5.64 us
  waiting for transfers between devices: 41.9 us -> 39.7 us
  starting transfers between devices: 28.4 us -> 30.5 us
  Pallas kernels: 20.9 us -> 22.9 us
    ppermute x6 -> x3, waiting for transfers between devices: 17.9 us -> 4.84 us  [to_plane(): lax.ppermute(value, 'kv', [(i, (i + step) % devices) for i in range(devic...]
    ppermute x0 -> x3, waiting for transfers between devices: none -> 9.61 us  [on_device(): lax.ppermute(parts_for(shift), 'kv', [(i, (i + shift * group_size) % devi...]
    ppermute x0 -> x3, starting transfers between devices: none -> 4.38 us  [on_device(): lax.ppermute(parts_for(shift), 'kv', [(i, (i + shift * group_size) % devi...]
    unnamed x20 -> x22, local copies, waits for them, and re-layouts: 5.49 us -> 2.73 us
    ppermute x15 -> x20, starting transfers between devices: 17.6 us -> 15.2 us  [swap(): return lax.ppermute(value, axis, [(i, i ^ bit) for i in range(count)])]
    pallas_call x1, Pallas kernels: 5.69 us -> 8.06 us  [attend_late(): pl.pallas_call(functools.partial(late_kernel, group_size), in_specs=[in_s...]
    ppermute x2, starting transfers between devices: 4.2 us -> 6.23 us  [on_device(): received.append(lax.ppermute(message, ('grp', 'kv'), routes))]
    ppermute x15 -> x20, waiting for transfers between devices: 23.2 us -> 25.2 us  [swap(): return lax.ppermute(value, axis, [(i, i ^ bit) for i in range(count)])]
  transfers between devices with their start and end apart: 23 -> 28, of which waited for: 12 -> 9; matrix products, arithmetic and copies ran while one was open for 11% -> 9% of each run, Pallas kernels for 14% -> 14%
where the time goes in v3:
time: 107 us
  waiting for transfers between devices  39.7 us (37%)
  starting transfers between devices  30.5 us (29%)
  Pallas kernels  22.9 us (21%)
  other arithmetic  7.52 us (7%)
  local copies, waits for them, and re-layouts  5.64 us (5%)
    ppermute x20, waiting for transfers between devices, swap(): return lax.ppermute(value, axis, [(i, i ^ bit) for i in range(count)])  25.2 us
    ppermute x20, starting transfers between devices, swap(): return lax.ppermute(value, axis, [(i, i ^ bit) for i in range(count)])  15.2 us
    pallas_call x1, Pallas kernels, attend_early(): pl.pallas_call(functools.partial(early_kernel, place, extension_at, len(p...  11.8 us
    ppermute x3, waiting for transfers between devices, on_device(): lax.ppermute(parts_for(shift), 'kv', [(i, (i + shift * group_size) % devi...  9.61 us
    pallas_call x1, Pallas kernels, attend_late(): pl.pallas_call(functools.partial(late_kernel, group_size), in_specs=[in_s...  8.06 us
    ppermute x2, starting transfers between devices, on_device(): received.append(lax.ppermute(message, ('grp', 'kv'), routes))  6.23 us
    ppermute x3, waiting for transfers between devices, to_plane(): lax.ppermute(value, 'kv', [(i, (i + step) % devices) for i in range(devic...  4.84 us
    ppermute x3, starting transfers between devices, to_plane(): lax.ppermute(value, 'kv', [(i, (i + step) % devices) for i in range(devic...  4.75 us
  transfers between devices with their start and end apart: 28, of which 9 were waited for; matrix products, arithmetic and copies ran while one was open for 9% of the time, Pallas kernels for 14%

profile of v3, /device:TPU:5, one launch (start us, length us, event | category | flops | bytes accessed | tf_op | source)
XLA Modules:
  0.0 106.6 jit_solution(6906194628270473703)
XLA Ops:
  0.0 1.0 constant_dynamic-slice_fusion.9
  1.0 0.7 collective-permute-start
  1.8 1.2 %collective-permute-start.3 = (bf16[1,128,5120]{2,1,0:T(8,128)(2,1)}, bf16[1,128,5120]{2,1,0:T(8,128)(2,1)S(1)}, u32[]{:S(2)}, u32[]{:S(2)}) collective-permute-start(bf16[1,128,5120]{2,1,0:T(8,128)(2,1)} %refs_0_.1), channel_id=1, source_target_pairs={{0,16},{16,0},{1,17},{17,1},{2,18},{18,2},{3,19},{19,3},{4,20},{20... | collective-permute-start | bytes 3932168 | tf_op jit(solution)/shard_map/ppermute | solution.py:20
  3.0 0.2 collective-permute-start.5
  3.2 1.2 %compare_bitcast_fusion.1 = pred[28]{0:T(512)(128)(4,1)} fusion(s32[28,3]{0,1:T(4,128)} %param.13), kind=kLoop, calls=%fused_computation.36 | loop fusion | flops 28 | bytes 140 | tf_op jit(solution)/shard_map/and | solution.py:423
  4.6 0.8 dynamic-slice_convert_fusion
  5.5 1.3 %collective-permute-start.1 = (bf16[640,256]{1,0:T(8,128)(2,1)S(1)}, bf16[640,256]{1,0:T(8,128)(2,1)S(1)}, u32[]{:S(2)}, u32[]{:S(2)}) collective-permute-start(bf16[640,256]{1,0:T(8,128)(2,1)S(1)} %maximum_select_fusion.refs_4_), channel_id=1, source_target_pairs={{0,4},{1,5},{2,6},{3,7},{4,8},{5,9},{6,10},{7,11},{8,12},{9,13},{1... | collective-permute-start | bytes 983048 | tf_op jit(solution)/shard_map/ppermute | solution.py:362
  6.8 1.2 %collective-permute-start.6 = (bf16[640,256]{1,0:T(8,128)(2,1)S(1)}, bf16[640,256]{1,0:T(8,128)(2,1)S(1)}, u32[]{:S(2)}, u32[]{:S(2)}) collective-permute-start(bf16[640,256]{1,0:T(8,128)(2,1)S(1)} %maximum_select_fusion.refs_4_), channel_id=1, source_target_pairs={{0,2},{1,3},{2,0},{3,1},{4,6},{5,7},{6,4},{7,5},{8,10},{9,11},{10,... | collective-permute-start | bytes 983048 | tf_op jit(solution)/shard_map/ppermute | solution.py:20
  8.1 0.6 pad_add_fusion.1
  8.6 0.6 slice_bitcast_fusion.1
  9.2 2.1 %collective-permute-start.4 = (bf16[640,256]{1,0:T(8,128)(2,1)S(1)}, bf16[640,256]{1,0:T(8,128)(2,1)}, u32[]{:S(2)}, u32[]{:S(2)}) collective-permute-start(bf16[640,256]{1,0:T(8,128)(2,1)S(1)} %maximum_select_fusion.refs_4_), channel_id=1, source_target_pairs={{0,12},{1,13},{2,14},{3,15},{4,0},{5,1},{6,2},{7,3},{8,4},{9,5},{1... | collective-permute-start | bytes 983048 | tf_op jit(solution)/shard_map/ppermute | solution.py:362
  11.3 4.8 %collective-permute-done.1.refs_6_ = bf16[640,256]{1,0:T(8,128)(2,1)S(1)} collective-permute-done((bf16[640,256]{1,0:T(8,128)(2,1)S(1)}, bf16[640,256]{1,0:T(8,128)(2,1)S(1)}, u32[]{:S(2)}, u32[]{:S(2)}) %collective-permute-start.1) | collective-permute-done | bytes 327712 | tf_op jit(solution)/shard_map/ppermute | solution.py:362
  16.1 7.4 %collective-permute-done.6.refs_5_ = bf16[640,256]{1,0:T(8,128)(2,1)S(1)} collective-permute-done((bf16[640,256]{1,0:T(8,128)(2,1)S(1)}, bf16[640,256]{1,0:T(8,128)(2,1)S(1)}, u32[]{:S(2)}, u32[]{:S(2)}) %collective-permute-start.6) | collective-permute-done | bytes 327712 | tf_op jit(solution)/shard_map/ppermute | solution.py:20
  23.5 0.7 copy-done.1
  24.2 0.2 collective-permute-start.7
  24.5 1.3 %collective-permute-start.2 = (bf16[640,256]{1,0:T(8,128)(2,1)S(1)}, bf16[640,256]{1,0:T(8,128)(2,1)S(1)}, u32[]{:S(2)}, u32[]{:S(2)}) collective-permute-start(bf16[640,256]{1,0:T(8,128)(2,1)S(1)} %collective-permute-done.1.refs_6_), channel_id=1, source_target_pairs={{0,4},{1,5},{2,6},{3,7},{4,8},{5,9},{6,10},{7,11},{8,12},{9,13},{1... | collective-permute-start | bytes 983048 | tf_op jit(solution)/shard_map/ppermute | solution.py:362
  25.8 0.9 fusion.6
  26.7 0.5 fusion.3
  27.2 5.2 %collective-permute-done.7.refs_7_ = bf16[640,256]{1,0:T(8,128)(2,1)} collective-permute-done((bf16[640,256]{1,0:T(8,128)(2,1)S(1)}, bf16[640,256]{1,0:T(8,128)(2,1)}, u32[]{:S(2)}, u32[]{:S(2)}) %collective-permute-start.7) | collective-permute-done | bytes 327712 | tf_op jit(solution)/shard_map/ppermute | solution.py:20
  32.5 0.2 collective-permute-start.8
  32.7 1.7 %fusion.1 = (bf16[256,128]{1,0:T(8,128)(2,1)S(1)}, f32[256,128]{1,0:T(8,128)S(1)}, f32[256,128]{1,0:T(8,128)}) fusion(f32[256,64]{1,0:T(8,128)S(1)} %get-tuple-element.82, f32[256,64]{1,0:T(8,128)S(1)} %get-tuple-element.83, bf16[256,256]{1,0:T(8,128)(2,1)} %param.8, f32[256,64]{1,0:T(8,128)S(1)} %get-tuple-element.75, f32[256,64]{1,0:T(8,128)S(1)} %get-tuple-element.74, ...), kind=kLoop, calls=%fused_computation.15 | loop fusion | flops 262144 | bytes 720896 | tf_op jit(solution)/shard_map/convert_element_type | solution.py:414
  34.4 5.5 %collective-permute-done.8.refs_9_ = bf16[640,256]{1,0:T(8,128)(2,1)S(1)} collective-permute-done((bf16[640,256]{1,0:T(8,128)(2,1)}, bf16[640,256]{1,0:T(8,128)(2,1)S(1)}, u32[]{:S(2)}, u32[]{:S(2)}) %collective-permute-start.8) | collective-permute-done | bytes 327712 | tf_op jit(solution)/shard_map/ppermute | solution.py:20
  39.9 0.2 collective-permute-start.19
  40.1 3.3 %collective-permute-start.9 = (bf16[1,128,5120]{2,1,0:T(8,128)(2,1)S(1)}, bf16[1,128,5120]{2,1,0:T(8,128)(2,1)S(1)}, u32[]{:S(2)}, u32[]{:S(2)}) collective-permute-start(bf16[1,128,5120]{2,1,0:T(8,128)(2,1)S(1)} %copy-done), channel_id=1, source_target_pairs={{0,1},{1,0},{2,3},{3,2},{4,5},{5,4},{6,7},{7,6},{8,9},{9,8},{10,11... | collective-permute-start | bytes 3932168 | tf_op jit(solution)/shard_map/ppermute | solution.py:20
  43.5 1.2 %collective-permute-start.11 = (bf16[640,256]{1,0:T(8,128)(2,1)S(1)}, bf16[640,256]{1,0:T(8,128)(2,1)S(1)}, u32[]{:S(2)}, u32[]{:S(2)}) collective-permute-start(bf16[640,256]{1,0:T(8,128)(2,1)S(1)} %collective-permute-done.2.refs_10_), channel_id=1, source_target_pairs={{0,2},{1,3},{2,0},{3,1},{4,6},{5,7},{6,4},{7,5},{8,10},{9,11},{10,... | collective-permute-start | bytes 983048 | tf_op jit(solution)/shard_map/ppermute | solution.py:20
  44.7 0.3 collective-permute-start.12
  45.0 1.2 %constant_dynamic-slice_fusion = (bf16[2,128,256]{2,1,0:T(8,128)(2,1)S(1)}, bf16[2,128,256]{2,1,0:T(8,128)(2,1)S(1)}, bf16[2,128,256]{2,1,0:T(8,128)(2,1)S(1)}, ...) fusion(bf16[2,128,1024]{2,1,0:T(8,128)(2,1)} %collective-permut, ...), kind=kLoop, calls=%fused_computation.22 | loop fusion | bytes 2097168 | tf_op jit(solution)/shard_map/dynamic_slice | solution.py:355
  46.3 1.3 %collective-permute-done.12 = s32[28,3]{0,1:T(4,128)S(1)} collective-permute-done((s32[28,3]{0,1:T(4,128)S(1)}, s32[28,3]{0,1:T(4,128)S(1)}, u32[]{:S(2)}, u32[]{:S(2)}) %collective-permute-start.12) | collective-permute-done | bytes 368 | tf_op jit(solution)/shard_map/ppermute | solution.py:20
  47.5 1.1 %collective-permute-start.16 = (bf16[4,128,256]{2,1,0:T(8,128)(2,1)S(1)}, bf16[4,128,256]{2,1,0:T(8,128)(2,1)}, u32[]{:S(2)}, u32[]{:S(2)}) collective-permute-start(bf16[4,128,256]{2,1,0:T(8,128)(2,1)S(1)} %bitcast.53), channel_id=1, source_target_pairs={{0,4},{1,5},{2,6},{3,7},{4,8},{5,9},{6,10},{7,11},{8,12},{9,13},{1... | collective-permute-start | bytes 786440 | tf_op jit(solution)/shard_map/ppermute | solution.py:381
  48.7 0.2 fusion.4
  49.0 1.0 fusion.2
  50.0 3.2 %collective-permute-done.11.refs_11_ = bf16[640,256]{1,0:T(8,128)(2,1)S(1)} collective-permute-done((bf16[640,256]{1,0:T(8,128)(2,1)S(1)}, bf16[640,256]{1,0:T(8,128)(2,1)S(1)}, u32[]{:S(2)}, u32[]{:S(2)}) %collective-permute-start.11) | collective-permute-done | bytes 327712 | tf_op jit(solution)/shard_map/ppermute | solution.py:20
  53.2 3.2 %collective-permute-start.17 = (bf16[4,128,256]{2,1,0:T(8,128)(2,1)S(1)}, bf16[4,128,256]{2,1,0:T(8,128)(2,1)}, u32[]{:S(2)}, u32[]{:S(2)}) collective-permute-start(bf16[4,128,256]{2,1,0:T(8,128)(2,1)S(1)} %bitcast.52), channel_id=1, source_target_pairs={{0,12},{1,13},{2,14},{3,15},{4,0},{5,1},{6,2},{7,3},{8,4},{9,5},{1... | collective-permute-start | bytes 786440 | tf_op jit(solution)/shard_map/ppermute | solution.py:381
  56.4 0.2 pad_maximum_fusion
  56.7 3.0 %project.1 = (bf16[2,128,256]{2,1,0:T(8,128)(2,1)S(1)}, bf16[2,128,256]{2,1,0:T(8,128)(2,1)S(1)}) custom-call(s32[10]{0:T(128)S(1)} %stack.71.meta, bf16[1,128,5120]{2,1,0:T(8,128)(2,1)S(1)} %copy-done, bf16[1,128,5120]{2,1,0:T(8,128)(2,1)S(1)} %collective-permute-done.9.refs_1_, bf16[1,128,5120]{2,1,0:T(8,128)(2,1)S(1)} %collective-permute-done.3.refs_2_, ...), custom_call_target="tpu_custom_call" | custom-call | flops 1342177280 | bytes 7864320 | tf_op jit(solution)/shard_map/project/pallas_call | solution.py:66
  59.8 6.2 %collective-permute-start.13 = (bf16[2,128,256]{2,1,0:T(8,128)(2,1)S(1)}, bf16[2,128,256]{2,1,0:T(8,128)(2,1)S(1)}, u32[]{:S(2)}, u32[]{:S(2)}) collective-permute-start(bf16[2,128,256]{2,1,0:T(8,128)(2,1)S(1)} %get-tuple-element.35), channel_id=1, source_target_pairs={{0,0},{1,8},{2,2},{3,10},{4,1},{5,9},{6,3},{7,11},{8,16},{9,24},{1... | collective-permute-start | bytes 393224 | tf_op jit(solution)/shard_map/ppermute | solution.py:458
  66.2 0.5 collective-permute-start.24
  66.7 9.6 %collective-permute-done.18.refs_3_ = bf16[4,128,256]{2,1,0:T(8,128)(2,1)} collective-permute-done((bf16[4,128,256]{2,1,0:T(8,128)(2,1)S(1)}, bf16[4,128,256]{2,1,0:T(8,128)(2,1)}, u32[]{:S(2)}, u32[]{:S(2)}) %collective-permute-start.18) | collective-permute-done | bytes 262176 | tf_op jit(solution)/shard_map/ppermute | solution.py:381
  76.3 4.3 %collective-permute-start.21 = (bf16[4,128,256]{2,1,0:T(8,128)(2,1)}, bf16[4,128,256]{2,1,0:T(8,128)(2,1)S(1)}, u32[]{:S(2)}, u32[]{:S(2)}) collective-permute-start(bf16[4,128,256]{2,1,0:T(8,128)(2,1)} %collective-permute-done.16.refs_1_), channel_id=1, source_target_pairs={{0,1},{1,0},{2,3},{3,2},{4,5},{5,4},{6,7},{7,6},{8,9},{9,8},{10,11... | collective-permute-start | bytes 786440 | tf_op jit(solution)/shard_map/ppermute | solution.py:20
  80.5 0.5 collective-permute-start.23
  81.2 0.4 collective-permute-start.15
  81.7 1.1 %collective-permute-done.25.refs_11_ = bf16[2,128,256]{2,1,0:T(8,128)(2,1)S(1)} collective-permute-done((bf16[2,128,256]{2,1,0:T(8,128)(2,1)}, bf16[2,128,256]{2,1,0:T(8,128)(2,1)S(1)}, u32[]{:S(2)}, u32[]{:S(2)}) %collective-permute-start.25) | collective-permute-done | bytes 131104 | tf_op jit(solution)/shard_map/ppermute | solution.py:20
  82.9 0.4 collective-permute-start.26
  83.2 0.9 copy-done.3
  84.1 1.0 copy-done.4
  85.1 11.8 %early.1 = (bf16[5,256,128]{2,1,0:T(8,128)(2,1)S(1)}, f32[5,256,128]{2,1,0:T(8,128)S(1)}, f32[5,256,256]{2,1,0:T(8,128)S(1)}) custom-call(s32[28,3]{1,0:T(8,128)S(1)} %copy.11.reuse, s32[3]{0:T(128)S(1)} %pad_add_fusion.meta, bf16[256,640]{1,0:T(8,128)(2,1)S(1)} %copy-done.4, f32[256,128]{1,0:T(8,128)S(1)} %copy-done.3, ...), custom_call_target="tpu_custom_call" | custom-call | flops 2348810240 | bytes 1835008 | tf_op jit(solution)/shard_map/early/pallas_call | solution.py:222
  97.0 1.5 %collective-permute-done.27.refs_3_ = bf16[4,128,256]{2,1,0:T(8,128)(2,1)S(1)} collective-permute-done((bf16[4,128,256]{2,1,0:T(8,128)(2,1)S(1)}, bf16[4,128,256]{2,1,0:T(8,128)(2,1)S(1)}, u32[]{:S(2)}, u32[]{:S(2)}) %collective-permute-start.27) | collective-permute-done | bytes 262176 | tf_op jit(solution)/shard_map/ppermute | solution.py:20
  98.5 8.1 %late.1 = bf16[256,640]{1,0:T(8,128)(2,1)} custom-call(s32[28,3]{1,0:T(8,128)S(1)} %copy.11.reuse, s32[3]{0:T(128)S(1)} %pad_add_fusion.meta, bf16[5,256,128]{2,1,0:T(8,128)(2,1)S(1)} %get-tuple-element.47.turned, f32[5,256,128]{2,1,0:T(8,128)S(1)} %get-tuple-element.48.top_in, f32[5,256,256]{2,1,0:T(8,128)S(1)} %get-tuple-element.49.sum_in, ...), custom_call_target="tpu_custom_call" | custom-call | flops 1174405120 | bytes 917504 | tf_op jit(solution)/shard_map/late/pallas_call | solution.py:297
  (60 shorter events, 1.2 us)
Async XLA Ops:
  0.0 8.6 %copy-start.6 = (s32[28,3]{0,1:T(4,128)S(1)}, s32[28,3]{0,1:T(4,128)}, u32[]{:S(2)}) copy-start(s32[28,3]{0,1:T(4,128)} %param.13) | copy-start | bytes 1012
  1.0 4.3 %collective-permute-start = (bf16[320,256]{1,0:T(8,128)(2,1)S(1)}, bf16[320,256]{1,0:T(8,128)(2,1)S(1)}, u32[]{:S(2)}, u32[]{:S(2)}) collective-permute-start(bf16[320,256]{1,0:T(8,128)(2,1)S(1)} %get-tuple-element.56), channel_id=1, source_target_pairs={{0,1},{1,0},{2,3},{3,2},{4,5},{5,4},{6,7},{7,6},{8,9},{9,8},{10,11... | collective-permute-start | bytes 491528 | tf_op jit(solution)/shard_map/ppermute | solution.py:20
  1.8 38.4 %collective-permute-start.3 = (bf16[1,128,5120]{2,1,0:T(8,128)(2,1)}, bf16[1,128,5120]{2,1,0:T(8,128)(2,1)S(1)}, u32[]{:S(2)}, u32[]{:S(2)}) collective-permute-start(bf16[1,128,5120]{2,1,0:T(8,128)(2,1)} %refs_0_.1), channel_id=1, source_target_pairs={{0,16},{16,0},{1,17},{17,1},{2,18},{18,2},{3,19},{19,3},{4,20},{20... | collective-permute-start | bytes 3932168 | tf_op jit(solution)/shard_map/ppermute | solution.py:20
  3.0 24.2 %collective-permute-start.5 = (bf16[2,128,1024]{2,1,0:T(8,128)(2,1)}, bf16[2,128,1024]{2,1,0:T(8,128)(2,1)}, u32[]{:S(2)}, u32[]{:S(2)}) collective-permute-start(bf16[2,128,1024]{2,1,0:T(8,128)(2,1)} %param.9), channel_id=1, source_target_pairs={{0,2},{1,3},{2,0},{3,1},{4,6},{5,7},{6,4},{7,5},{8,10},{9,11},{10,... | collective-permute-start | bytes 1572872 | tf_op jit(solution)/shard_map/ppermute | solution.py:20
  5.5 34.7 %copy-start = (bf16[1,128,5120]{2,1,0:T(8,128)(2,1)S(1)}, bf16[1,128,5120]{2,1,0:T(8,128)(2,1)}, u32[]{:S(2)}) copy-start(bf16[1,128,5120]{2,1,0:T(8,128)(2,1)} %refs_0_.1) | copy-start | bytes 3932164
  5.5 10.7 %collective-permute-start.1 = (bf16[640,256]{1,0:T(8,128)(2,1)S(1)}, bf16[640,256]{1,0:T(8,128)(2,1)S(1)}, u32[]{:S(2)}, u32[]{:S(2)}) collective-permute-start(bf16[640,256]{1,0:T(8,128)(2,1)S(1)} %maximum_select_fusion.refs_4_), channel_id=1, source_target_pairs={{0,4},{1,5},{2,6},{3,7},{4,8},{5,9},{6,10},{7,11},{8,12},{9,13},{1... | collective-permute-start | bytes 983048 | tf_op jit(solution)/shard_map/ppermute | solution.py:362
  6.8 16.7 %collective-permute-start.6 = (bf16[640,256]{1,0:T(8,128)(2,1)S(1)}, bf16[640,256]{1,0:T(8,128)(2,1)S(1)}, u32[]{:S(2)}, u32[]{:S(2)}) collective-permute-start(bf16[640,256]{1,0:T(8,128)(2,1)S(1)} %maximum_select_fusion.refs_4_), channel_id=1, source_target_pairs={{0,2},{1,3},{2,0},{3,1},{4,6},{5,7},{6,4},{7,5},{8,10},{9,11},{10,... | collective-permute-start | bytes 983048 | tf_op jit(solution)/shard_map/ppermute | solution.py:20
  9.2 18.0 %collective-permute-start.4 = (bf16[640,256]{1,0:T(8,128)(2,1)S(1)}, bf16[640,256]{1,0:T(8,128)(2,1)}, u32[]{:S(2)}, u32[]{:S(2)}) collective-permute-start(bf16[640,256]{1,0:T(8,128)(2,1)S(1)} %maximum_select_fusion.refs_4_), channel_id=1, source_target_pairs={{0,12},{1,13},{2,14},{3,15},{4,0},{5,1},{6,2},{7,3},{8,4},{9,5},{1... | collective-permute-start | bytes 983048 | tf_op jit(solution)/shard_map/ppermute | solution.py:362
  23.5 0.7 copy-start.1
  24.2 8.2 %collective-permute-start.7 = (bf16[640,256]{1,0:T(8,128)(2,1)S(1)}, bf16[640,256]{1,0:T(8,128)(2,1)}, u32[]{:S(2)}, u32[]{:S(2)}) collective-permute-start(bf16[640,256]{1,0:T(8,128)(2,1)S(1)} %collective-permute-done.1.refs_6_), channel_id=1, source_target_pairs={{0,2},{1,3},{2,0},{3,1},{4,6},{5,7},{6,4},{7,5},{8,10},{9,11},{10,... | collective-permute-start | bytes 983048 | tf_op jit(solution)/shard_map/ppermute | solution.py:20
  24.5 20.5 %copy-start.5 = (bf16[2,128,1024]{2,1,0:T(8,128)(2,1)S(1)}, bf16[2,128,1024]{2,1,0:T(8,128)(2,1)}, u32[]{:S(2)}) copy-start(bf16[2,128,1024]{2,1,0:T(8,128)(2,1)} %param.9) | copy-start | bytes 1572868
  24.5 15.7 %collective-permute-start.2 = (bf16[640,256]{1,0:T(8,128)(2,1)S(1)}, bf16[640,256]{1,0:T(8,128)(2,1)S(1)}, u32[]{:S(2)}, u32[]{:S(2)}) collective-permute-start(bf16[640,256]{1,0:T(8,128)(2,1)S(1)} %collective-permute-done.1.refs_6_), channel_id=1, source_target_pairs={{0,4},{1,5},{2,6},{3,7},{4,8},{5,9},{6,10},{7,11},{8,12},{9,13},{1... | collective-permute-start | bytes 983048 | tf_op jit(solution)/shard_map/ppermute | solution.py:362
  32.5 7.4 %collective-permute-start.8 = (bf16[640,256]{1,0:T(8,128)(2,1)}, bf16[640,256]{1,0:T(8,128)(2,1)S(1)}, u32[]{:S(2)}, u32[]{:S(2)}) collective-permute-start(bf16[640,256]{1,0:T(8,128)(2,1)} %collective-permute-done.4.refs_8_), channel_id=1, source_target_pairs={{0,2},{1,3},{2,0},{3,1},{4,6},{5,7},{6,4},{7,5},{8,10},{9,11},{10,... | collective-permute-start | bytes 983048 | tf_op jit(solution)/shard_map/ppermute | solution.py:20
  39.9 26.1 %collective-permute-start.19 = (bf16[256,256]{1,0:T(8,128)(2,1)S(1)}, bf16[256,256]{1,0:T(8,128)(2,1)}, u32[]{:S(2)}, u32[]{:S(2)}) collective-permute-start(bf16[256,256]{1,0:T(8,128)(2,1)S(1)} %pad_maximum_fusion.8), channel_id=1, source_target_pairs={{0,2},{1,3},{2,0},{3,1},{4,6},{5,7},{6,4},{7,5},{8,10},{9,11},{10,... | collective-permute-start | bytes 393224 | tf_op jit(solution)/shard_map/ppermute | solution.py:20
  40.1 16.5 %collective-permute-start.9 = (bf16[1,128,5120]{2,1,0:T(8,128)(2,1)S(1)}, bf16[1,128,5120]{2,1,0:T(8,128)(2,1)S(1)}, u32[]{:S(2)}, u32[]{:S(2)}) collective-permute-start(bf16[1,128,5120]{2,1,0:T(8,128)(2,1)S(1)} %copy-done), channel_id=1, source_target_pairs={{0,1},{1,0},{2,3},{3,2},{4,5},{5,4},{6,7},{7,6},{8,9},{9,8},{10,11... | collective-permute-start | bytes 3932168 | tf_op jit(solution)/shard_map/ppermute | solution.py:20
  43.4 13.3 %collective-permute-start.10 = (bf16[1,128,5120]{2,1,0:T(8,128)(2,1)S(1)}, bf16[1,128,5120]{2,1,0:T(8,128)(2,1)S(1)}, u32[]{:S(2)}, u32[]{:S(2)}) collective-permute-start(bf16[1,128,5120]{2,1,0:T(8,128)(2,1)S(1)} %collective-permute-done.3.refs_2_), channel_id=1, source_target_pairs={{0,1},{1,0},{2,3},{3,2},{4,5},{5,4},{6,7},{7,6},{8,9},{9,8},{10,11... | collective-permute-start | bytes 3932168 | tf_op jit(solution)/shard_map/ppermute | solution.py:20
  43.5 9.7 %collective-permute-start.11 = (bf16[640,256]{1,0:T(8,128)(2,1)S(1)}, bf16[640,256]{1,0:T(8,128)(2,1)S(1)}, u32[]{:S(2)}, u32[]{:S(2)}) collective-permute-start(bf16[640,256]{1,0:T(8,128)(2,1)S(1)} %collective-permute-done.2.refs_10_), channel_id=1, source_target_pairs={{0,2},{1,3},{2,0},{3,1},{4,6},{5,7},{6,4},{7,5},{8,10},{9,11},{10,... | collective-permute-start | bytes 983048 | tf_op jit(solution)/shard_map/ppermute | solution.py:20
  44.7 2.8 %collective-permute-start.12 = (s32[28,3]{0,1:T(4,128)S(1)}, s32[28,3]{0,1:T(4,128)S(1)}, u32[]{:S(2)}, u32[]{:S(2)}) collective-permute-start(s32[28,3]{0,1:T(4,128)S(1)} %copy-done.6), channel_id=1, source_target_pairs={{0,16},{16,0},{1,17},{17,1},{2,18},{18,2},{3,19},{19,3},{4,20},{20... | collective-permute-start | bytes 1016 | tf_op jit(solution)/shard_map/ppermute | solution.py:20
  46.2 2.5 %copy-start.7 = (pred[28]{0:T(512)(128)(4,1)S(1)}, pred[28]{0:T(512)(128)(4,1)}, u32[]{:S(2)}) copy-start(pred[28]{0:T(512)(128)(4,1)} %compare_bitcast_fusion.1) | copy-start | bytes 88
  46.2 2.5 %copy-start.8 = (s32[2]{0:T(128)S(1)}, s32[2]{0:T(128)}, u32[]{:S(2)}) copy-start(s32[2]{0:T(128)} %pad_add_fusion.1) | copy-start | bytes 28
  46.2 2.5 %copy-start.9 = (s32[28]{0:T(128)S(1)}, s32[28]{0:T(128)}, u32[]{:S(2)}) copy-start(s32[28]{0:T(128)} %slice_bitcast_fusion.1) | copy-start | bytes 340
  46.3 10.5 %copy-start.2 = (bf16[640,256]{1,0:T(8,128)(2,1)S(1)}, bf16[640,256]{1,0:T(8,128)(2,1)}, u32[]{:S(2)}) copy-start(bf16[640,256]{1,0:T(8,128)(2,1)} %copy-done.1) | copy-start | bytes 983044
  47.5 18.5 %collective-permute-start.16 = (bf16[4,128,256]{2,1,0:T(8,128)(2,1)S(1)}, bf16[4,128,256]{2,1,0:T(8,128)(2,1)}, u32[]{:S(2)}, u32[]{:S(2)}) collective-permute-start(bf16[4,128,256]{2,1,0:T(8,128)(2,1)S(1)} %bitcast.53), channel_id=1, source_target_pairs={{0,4},{1,5},{2,6},{3,7},{4,8},{5,9},{6,10},{7,11},{8,12},{9,13},{1... | collective-permute-start | bytes 786440 | tf_op jit(solution)/shard_map/ppermute | solution.py:381
  53.2 13.0 %collective-permute-start.17 = (bf16[4,128,256]{2,1,0:T(8,128)(2,1)S(1)}, bf16[4,128,256]{2,1,0:T(8,128)(2,1)}, u32[]{:S(2)}, u32[]{:S(2)}) collective-permute-start(bf16[4,128,256]{2,1,0:T(8,128)(2,1)S(1)} %bitcast.52), channel_id=1, source_target_pairs={{0,12},{1,13},{2,14},{3,15},{4,0},{5,1},{6,2},{7,3},{8,4},{9,5},{1... | collective-permute-start | bytes 786440 | tf_op jit(solution)/shard_map/ppermute | solution.py:381
  56.6 19.6 %collective-permute-start.18 = (bf16[4,128,256]{2,1,0:T(8,128)(2,1)S(1)}, bf16[4,128,256]{2,1,0:T(8,128)(2,1)}, u32[]{:S(2)}, u32[]{:S(2)}) collective-permute-start(bf16[4,128,256]{2,1,0:T(8,128)(2,1)S(1)} %bitcast.51), channel_id=1, source_target_pairs={{0,8},{1,9},{2,10},{3,11},{4,12},{5,13},{6,14},{7,15},{8,0},{9,1},... | collective-permute-start | bytes 786440 | tf_op jit(solution)/shard_map/ppermute | solution.py:381
  59.8 16.5 %collective-permute-start.13 = (bf16[2,128,256]{2,1,0:T(8,128)(2,1)S(1)}, bf16[2,128,256]{2,1,0:T(8,128)(2,1)S(1)}, u32[]{:S(2)}, u32[]{:S(2)}) collective-permute-start(bf16[2,128,256]{2,1,0:T(8,128)(2,1)S(1)} %get-tuple-element.35), channel_id=1, source_target_pairs={{0,0},{1,8},{2,2},{3,10},{4,1},{5,9},{6,3},{7,11},{8,16},{9,24},{1... | collective-permute-start | bytes 393224 | tf_op jit(solution)/shard_map/ppermute | solution.py:458
  66.0 10.3 %collective-permute-start.14 = (bf16[2,128,256]{2,1,0:T(8,128)(2,1)S(1)}, bf16[2,128,256]{2,1,0:T(8,128)(2,1)S(1)}, u32[]{:S(2)}, u32[]{:S(2)}) collective-permute-start(bf16[2,128,256]{2,1,0:T(8,128)(2,1)S(1)} %get-tuple-element.36), channel_id=1, source_target_pairs={{0,16},{1,24},{2,18},{3,26},{4,17},{5,25},{6,19},{7,27},{8,0},{9,8... | collective-permute-start | bytes 393224 | tf_op jit(solution)/shard_map/ppermute | solution.py:458
  66.1 15.1 %collective-permute-start.20 = (bf16[4,128,256]{2,1,0:T(8,128)(2,1)S(1)}, bf16[4,128,256]{2,1,0:T(8,128)(2,1)S(1)}, u32[]{:S(2)}, u32[]{:S(2)}) collective-permute-start(bf16[4,128,256]{2,1,0:T(8,128)(2,1)S(1)} %bitcast.38), channel_id=1, source_target_pairs={{0,1},{1,0},{2,3},{3,2},{4,5},{5,4},{6,7},{7,6},{8,9},{9,8},{10,11... | collective-permute-start | bytes 786440 | tf_op jit(solution)/shard_map/ppermute | solution.py:20
  66.2 14.9 %collective-permute-start.24 = (bf16[2,128,256]{2,1,0:T(8,128)(2,1)S(1)}, bf16[2,128,256]{2,1,0:T(8,128)(2,1)S(1)}, u32[]{:S(2)}, u32[]{:S(2)}) collective-permute-start(bf16[2,128,256]{2,1,0:T(8,128)(2,1)S(1)} %bitcast.40), channel_id=1, source_target_pairs={{0,1},{1,0},{2,3},{3,2},{4,5},{5,4},{6,7},{7,6},{8,9},{9,8},{10,11... | collective-permute-start | bytes 393224 | tf_op jit(solution)/shard_map/ppermute | solution.py:20
  76.3 6.9 %collective-permute-start.21 = (bf16[4,128,256]{2,1,0:T(8,128)(2,1)}, bf16[4,128,256]{2,1,0:T(8,128)(2,1)S(1)}, u32[]{:S(2)}, u32[]{:S(2)}) collective-permute-start(bf16[4,128,256]{2,1,0:T(8,128)(2,1)} %collective-permute-done.16.refs_1_), channel_id=1, source_target_pairs={{0,1},{1,0},{2,3},{3,2},{4,5},{5,4},{6,7},{7,6},{8,9},{9,8},{10,11... | collective-permute-start | bytes 786440 | tf_op jit(solution)/shard_map/ppermute | solution.py:20
  80.5 2.7 %collective-permute-start.22 = (bf16[4,128,256]{2,1,0:T(8,128)(2,1)}, bf16[4,128,256]{2,1,0:T(8,128)(2,1)S(1)}, u32[]{:S(2)}, u32[]{:S(2)}) collective-permute-start(bf16[4,128,256]{2,1,0:T(8,128)(2,1)} %collective-permute-done.17.refs_2_), channel_id=1, source_target_pairs={{0,1},{1,0},{2,3},{3,2},{4,5},{5,4},{6,7},{7,6},{8,9},{9,8},{10,11... | collective-permute-start | bytes 786440 | tf_op jit(solution)/shard_map/ppermute | solution.py:20
  80.5 2.7 %collective-permute-start.23 = (bf16[4,128,256]{2,1,0:T(8,128)(2,1)}, bf16[4,128,256]{2,1,0:T(8,128)(2,1)S(1)}, u32[]{:S(2)}, u32[]{:S(2)}) collective-permute-start(bf16[4,128,256]{2,1,0:T(8,128)(2,1)} %collective-permute-done.18.refs_3_), channel_id=1, source_target_pairs={{0,1},{1,0},{2,3},{3,2},{4,5},{5,4},{6,7},{7,6},{8,9},{9,8},{10,11... | collective-permute-start | bytes 786440 | tf_op jit(solution)/shard_map/ppermute | solution.py:20
  81.1 1.8 %collective-permute-start.25 = (bf16[2,128,256]{2,1,0:T(8,128)(2,1)}, bf16[2,128,256]{2,1,0:T(8,128)(2,1)S(1)}, u32[]{:S(2)}, u32[]{:S(2)}) collective-permute-start(bf16[2,128,256]{2,1,0:T(8,128)(2,1)} %bitcast.32.refs_5_), channel_id=1, source_target_pairs={{0,1},{1,0},{2,3},{3,2},{4,5},{5,4},{6,7},{7,6},{8,9},{9,8},{10,11... | collective-permute-start | bytes 393224 | tf_op jit(solution)/shard_map/ppermute | solution.py:20
  81.2 15.7 %collective-permute-start.15 = (bf16[4,128,256]{2,1,0:T(8,128)(2,1)S(1)}, bf16[4,128,256]{2,1,0:T(8,128)(2,1)S(1)}, u32[]{:S(2)}, u32[]{:S(2)}) collective-permute-start(bf16[4,128,256]{2,1,0:T(8,128)(2,1)S(1)} %constant_dynamic-update-slice_fusion.refs_0_), channel_id=1, source_target_pairs={{0,2},{1,3},{2,0},{3,1},{4,6},{5,7},{6,4},{7,5},{8,10},{9,11},{10,... | collective-permute-start | bytes 786440 | tf_op jit(solution)/shard_map/ppermute | solution.py:20
  82.9 14.2 %collective-permute-start.26 = (bf16[4,128,256]{2,1,0:T(8,128)(2,1)S(1)}, bf16[4,128,256]{2,1,0:T(8,128)(2,1)S(1)}, u32[]{:S(2)}, u32[]{:S(2)}) collective-permute-start(bf16[4,128,256]{2,1,0:T(8,128)(2,1)S(1)} %constant_dynamic-update-slice_fusion.refs_0_), channel_id=1, source_target_pairs={{0,1},{1,0},{2,3},{3,2},{4,5},{5,4},{6,7},{7,6},{8,9},{9,8},{10,11... | collective-permute-start | bytes 786440 | tf_op jit(solution)/shard_map/ppermute | solution.py:20
  83.2 0.9 copy-start.3
  84.1 1.0 copy-start.4
  96.9 1.6 %collective-permute-start.27 = (bf16[4,128,256]{2,1,0:T(8,128)(2,1)S(1)}, bf16[4,128,256]{2,1,0:T(8,128)(2,1)S(1)}, u32[]{:S(2)}, u32[]{:S(2)}) collective-permute-start(bf16[4,128,256]{2,1,0:T(8,128)(2,1)S(1)} %collective-permute-done.15.refs_2_), channel_id=1, source_target_pairs={{0,1},{1,0},{2,3},{3,2},{4,5},{5,4},{6,7},{7,6},{8,9},{9,8},{10,11... | collective-permute-start | bytes 786440 | tf_op jit(solution)/shard_map/ppermute | solution.py:20

commit v4 on v3

--- a/solution.py
+++ b/solution.py
@@ -11,6 +11,7 @@
 HEAD_DIM = 128
 PAIR = 2 * HEAD_DIM
 HEADS = 4
+ONES = 16
 
 ROPE_BASE = 1000000.0
 MASK_VALUE = -1e30
@@ -81,13 +82,13 @@
 
 def fold(query_ref, rows, top_ref, sum_ref, mask=None, first=False):
     key_rows, value_rows = rows[:, :HEAD_DIM], rows[:, HEAD_DIM:]
-    copies = rows.shape[0] // HEAD_DIM
-    extended = jnp.concatenate([value_rows, jnp.ones_like(value_rows)], axis=1)
+    values = value_rows.astype(jnp.float32).T.astype(jnp.bfloat16)
+    extended = jnp.concatenate([values, jnp.ones((ONES, rows.shape[0]), jnp.bfloat16)], axis=0)
 
     def scores_of(group):
         scores = lax.dot_general(
+            key_rows,
             query_ref[group],
-            key_rows,
             (((1,), (1,)), ((), ())),
             preferred_element_type=jnp.float32,
         )
@@ -98,21 +99,16 @@
         scores = ahead
         if group + 1 < GQ:
             ahead = scores_of(group + 1)
-        row_top = jnp.broadcast_to(
-            jnp.max(scores, axis=1, keepdims=True), (scores.shape[0], HEAD_DIM)
-        )
+        top = jnp.max(scores, axis=0, keepdims=True)
         if not first:
             old_top = top_ref[group]
-            row_top = jnp.maximum(old_top, row_top)
-        weights = jnp.exp(scores - jnp.concatenate([row_top] * copies, axis=1))
-        product = jnp.dot(
-            weights.astype(jnp.bfloat16), extended, preferred_element_type=jnp.float32
-        )
+            top = jnp.maximum(old_top, top)
+        weights = jnp.exp(scores - top).astype(jnp.bfloat16)
+        product = jnp.dot(extended, weights, preferred_element_type=jnp.float32)
         if not first:
-            shrink = jnp.exp(old_top - row_top)
-            product += sum_ref[group] * jnp.concatenate([shrink, shrink], axis=1)
+            product += sum_ref[group] * jnp.exp(old_top - top)
         sum_ref[group] = product
-        top_ref[group] = row_top
+        top_ref[group] = top
 
 
 def fold_pages(query_ref, buffer, wait_page, count, top_ref, sum_ref):
@@ -196,7 +192,7 @@
 
     for relative in range(group_size):
         block_copy(relative).wait()
-    attend(0, mask=columns <= rows, first=True)
+    attend(0, mask=rows <= columns, first=True)
 
     def earlier(index, carry):
         attend(index ^ slice_index)
@@ -225,8 +221,8 @@
         out_specs=[in_vmem] * 3,
         out_shape=[
             jax.ShapeDtypeStruct(shape, jnp.bfloat16),
-            jax.ShapeDtypeStruct(shape, jnp.float32),
-            jax.ShapeDtypeStruct((GQ, row_count, PAIR), jnp.float32),
+            jax.ShapeDtypeStruct((GQ, 1, row_count), jnp.float32),
+            jax.ShapeDtypeStruct((GQ, HEAD_DIM + ONES, row_count), jnp.float32),
         ],
         scratch_shapes=[
             pltpu.VMEM((page_count, page_rows, PAIR), jnp.bfloat16),
@@ -277,13 +273,11 @@
     fold_pages(turned, buffer, wait_page, count, top_ref, sum_ref)
     for group in range(GQ):
         first_top, last_top = top_in[group], top_ref[group]
-        row_top = jnp.maximum(first_top, last_top)
-        first_share, last_share = jnp.exp(first_top - row_top), jnp.exp(last_top - row_top)
-        total = sum_in[group] * jnp.concatenate([first_share, first_share], axis=1)
-        total += sum_ref[group] * jnp.concatenate([last_share, last_share], axis=1)
-        out[:, group * HEAD_DIM : (group + 1) * HEAD_DIM] = (
-            total[:, :HEAD_DIM] / total[:, HEAD_DIM:]
-        ).astype(out.dtype)
+        top = jnp.maximum(first_top, last_top)
+        total = sum_in[group] * jnp.exp(first_top - top)
+        total += sum_ref[group] * jnp.exp(last_top - top)
+        result = total[:HEAD_DIM] / total[HEAD_DIM : HEAD_DIM + 1]
+        out[:, group * HEAD_DIM : (group + 1) * HEAD_DIM] = result.T.astype(out.dtype)
 
 
 def attend_late(reuse, meta, turned, top, total, pieces):
@@ -363,7 +357,7 @@
 
         near, back = to_plane(chip_rows, 1), to_plane(chip_rows, 3)
         beside_own = exchange(chip_rows, 2)
-        store_beside = exchange(page_store, 2)
+        store_beside = exchange(lax.optimization_barrier((page_store, chip_rows))[0], 2)
         far = to_plane(near, 1)
         near_sent, _ = lax.optimization_barrier((near, beside_own))
         beside_near = exchange(near_sent, 2)

time: 107 us -> 109 us (1.019)
  waiting for transfers between devices: 39.7 us -> 42.3 us
  starting transfers between devices: 30.5 us -> 29.1 us
  Pallas kernels: 22.9 us -> 24.1 us
    ppermute x3, waiting for transfers between devices: 4.84 us -> 10.5 us  [to_plane(): lax.ppermute(value, 'kv', [(i, (i + step) % devices) for i in range(devic...]
    ppermute x20, waiting for transfers between devices: 25.2 us -> 22.1 us  [swap(): return lax.ppermute(value, axis, [(i, i ^ bit) for i in range(count)])]
    pallas_call x1, Pallas kernels: 11.8 us -> 13.3 us  [attend_early(): pl.pallas_call(functools.partial(early_kernel, place, extension_at, len(p...]
  transfers between devices with their start and end apart: 28 -> 28, of which waited for: 9 -> 10; matrix products, arithmetic and copies ran while one was open for 9% -> 9% of each run, Pallas kernels for 14% -> 15%
where the time goes in v4:
time: 109 us
  waiting for transfers between devices  42.3 us (39%)
  starting transfers between devices  29.1 us (27%)
  Pallas kernels  24.1 us (22%)
  other arithmetic  7.51 us (7%)
  local copies, waits for them, and re-layouts  5.64 us (5%)
    ppermute x20, waiting for transfers between devices, swap(): return lax.ppermute(value, axis, [(i, i ^ bit) for i in range(count)])  22.1 us
    ppermute x20, starting transfers between devices, swap(): return lax.ppermute(value, axis, [(i, i ^ bit) for i in range(count)])  14.8 us
    pallas_call x1, Pallas kernels, attend_early(): pl.pallas_call(functools.partial(early_kernel, place, extension_at, len(p...  13.3 us
    ppermute x3, waiting for transfers between devices, to_plane(): lax.ppermute(value, 'kv', [(i, (i + step) % devices) for i in range(devic...  10.5 us
    ppermute x3, waiting for transfers between devices, on_device(): lax.ppermute(parts_for(shift), 'kv', [(i, (i + shift * group_size) % devi...  9.68 us
    pallas_call x1, Pallas kernels, attend_late(): pl.pallas_call(functools.partial(late_kernel, group_size), in_specs=[in_s...  7.77 us
    ppermute x2, starting transfers between devices, on_device(): received.append(lax.ppermute(message, ('grp', 'kv'), routes))  6.63 us
    ppermute x3, starting transfers between devices, on_device(): lax.ppermute(parts_for(shift), 'kv', [(i, (i + shift * group_size) % devi...  3.95 us
  transfers between devices with their start and end apart: 28, of which 10 were waited for; matrix products, arithmetic and copies ran while one was open for 9% of the time, Pallas kernels for 15%

profile of v4, /device:TPU:5, one launch (start us, length us, event | category | flops | bytes accessed | tf_op | source)
XLA Modules:
  0.0 109.0 jit_solution(7622546004695047362)
XLA Ops:
  0.0 1.0 constant_dynamic-slice_fusion.9
  1.0 0.7 collective-permute-start
  1.8 1.2 %collective-permute-start.3 = (bf16[1,128,5120]{2,1,0:T(8,128)(2,1)}, bf16[1,128,5120]{2,1,0:T(8,128)(2,1)S(1)}, u32[]{:S(2)}, u32[]{:S(2)}) collective-permute-start(bf16[1,128,5120]{2,1,0:T(8,128)(2,1)} %refs_0_.1), channel_id=1, source_target_pairs={{0,16},{16,0},{1,17},{17,1},{2,18},{18,2},{3,19},{19,3},{4,20},{20... | collective-permute-start | bytes 3932168 | tf_op jit(solution)/shard_map/ppermute | solution.py:21
  3.0 1.2 %compare_bitcast_fusion.1 = pred[28]{0:T(512)(128)(4,1)} fusion(s32[28,3]{0,1:T(4,128)} %param.13), kind=kLoop, calls=%fused_computation.36 | loop fusion | flops 28 | bytes 140 | tf_op jit(solution)/shard_map/and | solution.py:417
  4.3 0.8 dynamic-slice_convert_fusion
  5.3 1.3 %collective-permute-start.1 = (bf16[640,256]{1,0:T(8,128)(2,1)S(1)}, bf16[640,256]{1,0:T(8,128)(2,1)S(1)}, u32[]{:S(2)}, u32[]{:S(2)}) collective-permute-start(bf16[640,256]{1,0:T(8,128)(2,1)S(1)} %maximum_select_fusion.refs_4_), channel_id=1, source_target_pairs={{0,4},{1,5},{2,6},{3,7},{4,8},{5,9},{6,10},{7,11},{8,12},{9,13},{1... | collective-permute-start | bytes 983048 | tf_op jit(solution)/shard_map/ppermute | solution.py:356
  6.6 0.2 collective-permute-start.6
  6.8 0.6 pad_add_fusion.1
  7.4 0.6 slice_bitcast_fusion.1
  8.0 2.1 %collective-permute-start.4 = (bf16[640,256]{1,0:T(8,128)(2,1)S(1)}, bf16[640,256]{1,0:T(8,128)(2,1)}, u32[]{:S(2)}, u32[]{:S(2)}) collective-permute-start(bf16[640,256]{1,0:T(8,128)(2,1)S(1)} %maximum_select_fusion.refs_4_), channel_id=1, source_target_pairs={{0,12},{1,13},{2,14},{3,15},{4,0},{5,1},{6,2},{7,3},{8,4},{9,5},{1... | collective-permute-start | bytes 983048 | tf_op jit(solution)/shard_map/ppermute | solution.py:356
  10.1 1.2 %collective-permute-start.5 = (bf16[2,128,1024]{2,1,0:T(8,128)(2,1)}, bf16[2,128,1024]{2,1,0:T(8,128)(2,1)}, u32[]{:S(2)}, u32[]{:S(2)}) collective-permute-start(bf16[2,128,1024]{2,1,0:T(8,128)(2,1)} %param.9), channel_id=1, source_target_pairs={{0,2},{1,3},{2,0},{3,1},{4,6},{5,7},{6,4},{7,5},{8,10},{9,11},{10,... | collective-permute-start | bytes 1572872 | tf_op jit(solution)/shard_map/ppermute | solution.py:21
  11.3 4.9 %collective-permute-done.1.refs_6_ = bf16[640,256]{1,0:T(8,128)(2,1)S(1)} collective-permute-done((bf16[640,256]{1,0:T(8,128)(2,1)S(1)}, bf16[640,256]{1,0:T(8,128)(2,1)S(1)}, u32[]{:S(2)}, u32[]{:S(2)}) %collective-permute-start.1) | collective-permute-done | bytes 327712 | tf_op jit(solution)/shard_map/ppermute | solution.py:356
  16.3 0.7 copy-done.1
  17.0 0.2 collective-permute-start.7
  17.2 0.3 collective-permute-start.2
  17.5 0.9 fusion.6
  18.4 0.5 fusion.3
  18.9 5.5 %collective-permute-done.4.refs_8_ = bf16[640,256]{1,0:T(8,128)(2,1)} collective-permute-done((bf16[640,256]{1,0:T(8,128)(2,1)S(1)}, bf16[640,256]{1,0:T(8,128)(2,1)}, u32[]{:S(2)}, u32[]{:S(2)}) %collective-permute-start.4) | collective-permute-done | bytes 327712 | tf_op jit(solution)/shard_map/ppermute | solution.py:356
  24.5 2.1 %collective-permute-done.5 = bf16[2,128,1024]{2,1,0:T(8,128)(2,1)} collective-permute-done((bf16[2,128,1024]{2,1,0:T(8,128)(2,1)}, bf16[2,128,1024]{2,1,0:T(8,128)(2,1)}, u32[]{:S(2)}, u32[]{:S(2)}) %collective-permute-start.5) | collective-permute-done | bytes 524320 | tf_op jit(solution)/shard_map/ppermute | solution.py:21
  26.6 7.0 %collective-permute-done.7.refs_7_ = bf16[640,256]{1,0:T(8,128)(2,1)} collective-permute-done((bf16[640,256]{1,0:T(8,128)(2,1)S(1)}, bf16[640,256]{1,0:T(8,128)(2,1)}, u32[]{:S(2)}, u32[]{:S(2)}) %collective-permute-start.7) | collective-permute-done | bytes 327712 | tf_op jit(solution)/shard_map/ppermute | solution.py:21
  33.6 0.2 collective-permute-start.8
  33.8 1.7 %fusion.1 = (bf16[256,128]{1,0:T(8,128)(2,1)S(1)}, f32[256,128]{1,0:T(8,128)S(1)}, f32[256,128]{1,0:T(8,128)}) fusion(f32[256,64]{1,0:T(8,128)S(1)} %get-tuple-element.84, f32[256,64]{1,0:T(8,128)S(1)} %get-tuple-element.85, bf16[256,256]{1,0:T(8,128)(2,1)} %param.8, f32[256,64]{1,0:T(8,128)S(1)} %get-tuple-element.77, f32[256,64]{1,0:T(8,128)S(1)} %get-tuple-element.76, ...), kind=kLoop, calls=%fused_computation.15 | loop fusion | flops 262144 | bytes 720896 | tf_op jit(solution)/shard_map/convert_element_type | solution.py:408
  35.5 6.0 %collective-permute-done.8.refs_9_ = bf16[640,256]{1,0:T(8,128)(2,1)S(1)} collective-permute-done((bf16[640,256]{1,0:T(8,128)(2,1)}, bf16[640,256]{1,0:T(8,128)(2,1)S(1)}, u32[]{:S(2)}, u32[]{:S(2)}) %collective-permute-start.8) | collective-permute-done | bytes 327712 | tf_op jit(solution)/shard_map/ppermute | solution.py:21
  41.8 2.8 %collective-permute-start.9 = (bf16[1,128,5120]{2,1,0:T(8,128)(2,1)S(1)}, bf16[1,128,5120]{2,1,0:T(8,128)(2,1)S(1)}, u32[]{:S(2)}, u32[]{:S(2)}) collective-permute-start(bf16[1,128,5120]{2,1,0:T(8,128)(2,1)S(1)} %copy-done), channel_id=1, source_target_pairs={{0,1},{1,0},{2,3},{3,2},{4,5},{5,4},{6,7},{7,6},{8,9},{9,8},{10,11... | collective-permute-start | bytes 3932168 | tf_op jit(solution)/shard_map/ppermute | solution.py:21
  44.6 1.2 %collective-permute-start.11 = (bf16[640,256]{1,0:T(8,128)(2,1)S(1)}, bf16[640,256]{1,0:T(8,128)(2,1)S(1)}, u32[]{:S(2)}, u32[]{:S(2)}) collective-permute-start(bf16[640,256]{1,0:T(8,128)(2,1)S(1)} %collective-permute-done.2.refs_10_), channel_id=1, source_target_pairs={{0,2},{1,3},{2,0},{3,1},{4,6},{5,7},{6,4},{7,5},{8,10},{9,11},{10,... | collective-permute-start | bytes 983048 | tf_op jit(solution)/shard_map/ppermute | solution.py:21
  45.8 0.3 collective-permute-start.12
  46.1 1.2 %constant_dynamic-slice_fusion = (bf16[2,128,256]{2,1,0:T(8,128)(2,1)S(1)}, bf16[2,128,256]{2,1,0:T(8,128)(2,1)S(1)}, bf16[2,128,256]{2,1,0:T(8,128)(2,1)S(1)}, ...) fusion(bf16[2,128,1024]{2,1,0:T(8,128)(2,1)} %collective-permut, ...), kind=kLoop, calls=%fused_computation.22 | loop fusion | bytes 2097168 | tf_op jit(solution)/shard_map/dynamic_slice | solution.py:349
  47.4 1.3 %collective-permute-done.12 = s32[28,3]{0,1:T(4,128)S(1)} collective-permute-done((s32[28,3]{0,1:T(4,128)S(1)}, s32[28,3]{0,1:T(4,128)S(1)}, u32[]{:S(2)}, u32[]{:S(2)}) %collective-permute-start.12) | collective-permute-done | bytes 368 | tf_op jit(solution)/shard_map/ppermute | solution.py:21
  48.7 1.3 %collective-permute-start.16 = (bf16[4,128,256]{2,1,0:T(8,128)(2,1)S(1)}, bf16[4,128,256]{2,1,0:T(8,128)(2,1)}, u32[]{:S(2)}, u32[]{:S(2)}) collective-permute-start(bf16[4,128,256]{2,1,0:T(8,128)(2,1)S(1)} %bitcast.53), channel_id=1, source_target_pairs={{0,4},{1,5},{2,6},{3,7},{4,8},{5,9},{6,10},{7,11},{8,12},{9,13},{1... | collective-permute-start | bytes 786440 | tf_op jit(solution)/shard_map/ppermute | solution.py:375
  50.4 1.0 fusion.2
  51.4 3.0 %collective-permute-done.11.refs_11_ = bf16[640,256]{1,0:T(8,128)(2,1)S(1)} collective-permute-done((bf16[640,256]{1,0:T(8,128)(2,1)S(1)}, bf16[640,256]{1,0:T(8,128)(2,1)S(1)}, u32[]{:S(2)}, u32[]{:S(2)}) %collective-permute-start.11) | collective-permute-done | bytes 327712 | tf_op jit(solution)/shard_map/ppermute | solution.py:21
  54.3 2.4 %collective-permute-start.17 = (bf16[4,128,256]{2,1,0:T(8,128)(2,1)S(1)}, bf16[4,128,256]{2,1,0:T(8,128)(2,1)}, u32[]{:S(2)}, u32[]{:S(2)}) collective-permute-start(bf16[4,128,256]{2,1,0:T(8,128)(2,1)S(1)} %bitcast.52), channel_id=1, source_target_pairs={{0,12},{1,13},{2,14},{3,15},{4,0},{5,1},{6,2},{7,3},{8,4},{9,5},{1... | collective-permute-start | bytes 786440 | tf_op jit(solution)/shard_map/ppermute | solution.py:375
  56.9 0.3 collective-permute-start.18
  57.2 3.0 %project.1 = (bf16[2,128,256]{2,1,0:T(8,128)(2,1)S(1)}, bf16[2,128,256]{2,1,0:T(8,128)(2,1)S(1)}) custom-call(s32[10]{0:T(128)S(1)} %stack.71.meta, bf16[1,128,5120]{2,1,0:T(8,128)(2,1)S(1)} %copy-done, bf16[1,128,5120]{2,1,0:T(8,128)(2,1)S(1)} %collective-permute-done.9.refs_1_, bf16[1,128,5120]{2,1,0:T(8,128)(2,1)S(1)} %collective-permute-done.3.refs_2_, ...), custom_call_target="tpu_custom_call" | custom-call | flops 1342177280 | bytes 7864320 | tf_op jit(solution)/shard_map/project/pallas_call | solution.py:67
  60.3 6.0 %collective-permute-start.13 = (bf16[2,128,256]{2,1,0:T(8,128)(2,1)S(1)}, bf16[2,128,256]{2,1,0:T(8,128)(2,1)S(1)}, u32[]{:S(2)}, u32[]{:S(2)}) collective-permute-start(bf16[2,128,256]{2,1,0:T(8,128)(2,1)S(1)} %get-tuple-element.37), channel_id=1, source_target_pairs={{0,0},{1,8},{2,2},{3,10},{4,1},{5,9},{6,3},{7,11},{8,16},{9,24},{1... | collective-permute-start | bytes 393224 | tf_op jit(solution)/shard_map/ppermute | solution.py:452
  66.3 0.6 collective-permute-start.14
  66.9 0.5 collective-permute-start.20
  67.5 9.7 %collective-permute-done.18.refs_3_ = bf16[4,128,256]{2,1,0:T(8,128)(2,1)} collective-permute-done((bf16[4,128,256]{2,1,0:T(8,128)(2,1)S(1)}, bf16[4,128,256]{2,1,0:T(8,128)(2,1)}, u32[]{:S(2)}, u32[]{:S(2)}) %collective-permute-start.18) | collective-permute-done | bytes 262176 | tf_op jit(solution)/shard_map/ppermute | solution.py:375
  77.2 4.5 %collective-permute-start.21 = (bf16[4,128,256]{2,1,0:T(8,128)(2,1)}, bf16[4,128,256]{2,1,0:T(8,128)(2,1)S(1)}, u32[]{:S(2)}, u32[]{:S(2)}) collective-permute-start(bf16[4,128,256]{2,1,0:T(8,128)(2,1)} %collective-permute-done.16.refs_1_), channel_id=1, source_target_pairs={{0,1},{1,0},{2,3},{3,2},{4,5},{5,4},{6,7},{7,6},{8,9},{9,8},{10,11... | collective-permute-start | bytes 786440 | tf_op jit(solution)/shard_map/ppermute | solution.py:21
  81.7 0.5 collective-permute-start.23
  82.3 0.3 collective-permute-start.15
  82.8 1.2 %collective-permute-done.25.refs_11_ = bf16[2,128,256]{2,1,0:T(8,128)(2,1)S(1)} collective-permute-done((bf16[2,128,256]{2,1,0:T(8,128)(2,1)}, bf16[2,128,256]{2,1,0:T(8,128)(2,1)S(1)}, u32[]{:S(2)}, u32[]{:S(2)}) %collective-permute-start.25) | collective-permute-done | bytes 131104 | tf_op jit(solution)/shard_map/ppermute | solution.py:21
  84.0 0.4 collective-permute-start.26
  84.4 0.9 copy-done.3
  85.3 1.0 copy-done.4
  86.2 13.3 %early.1 = (bf16[5,256,128]{2,1,0:T(8,128)(2,1)S(1)}, f32[5,1,256]{2,1,0:T(1,128)S(1)}, f32[5,144,256]{2,1,0:T(8,128)S(1)}) custom-call(s32[28,3]{1,0:T(8,128)S(1)} %copy.11.reuse, s32[3]{0:T(128)S(1)} %pad_add_fusion.meta, bf16[256,640]{1,0:T(8,128)(2,1)S(1)} %copy-done.4, f32[256,128]{1,0:T(8,128)S(1)} %copy-done.3, ...), custom_call_target="tpu_custom_call" | custom-call | flops 2348810240 | bytes 1835008 | tf_op jit(solution)/shard_map/early/pallas_call | solution.py:218
  99.7 1.5 %collective-permute-done.27.refs_3_ = bf16[4,128,256]{2,1,0:T(8,128)(2,1)S(1)} collective-permute-done((bf16[4,128,256]{2,1,0:T(8,128)(2,1)S(1)}, bf16[4,128,256]{2,1,0:T(8,128)(2,1)S(1)}, u32[]{:S(2)}, u32[]{:S(2)}) %collective-permute-start.27) | collective-permute-done | bytes 262176 | tf_op jit(solution)/shard_map/ppermute | solution.py:21
  101.2 7.8 %late.1 = bf16[256,640]{1,0:T(8,128)(2,1)} custom-call(s32[28,3]{1,0:T(8,128)S(1)} %copy.11.reuse, s32[3]{0:T(128)S(1)} %pad_add_fusion.meta, bf16[5,256,128]{2,1,0:T(8,128)(2,1)S(1)} %get-tuple-element.49.turned, f32[5,1,256]{2,1,0:T(1,128)S(1)} %get-tuple-element.50.top_in, f32[5,144,256]{2,1,0:T(8,128)S(1)} %get-tuple-element.51.sum_in, ...), custom_call_target="tpu_custom_call" | custom-call | flops 1174405120 | bytes 917504 | tf_op jit(solution)/shard_map/late/pallas_call | solution.py:291
  (60 shorter events, 1.7 us)
Async XLA Ops:
  0.0 7.4 %copy-start.6 = (s32[28,3]{0,1:T(4,128)S(1)}, s32[28,3]{0,1:T(4,128)}, u32[]{:S(2)}) copy-start(s32[28,3]{0,1:T(4,128)} %param.13) | copy-start | bytes 1012
  1.0 4.1 %collective-permute-start = (bf16[320,256]{1,0:T(8,128)(2,1)S(1)}, bf16[320,256]{1,0:T(8,128)(2,1)S(1)}, u32[]{:S(2)}, u32[]{:S(2)}) collective-permute-start(bf16[320,256]{1,0:T(8,128)(2,1)S(1)} %get-tuple-element.58), channel_id=1, source_target_pairs={{0,1},{1,0},{2,3},{3,2},{4,5},{5,4},{6,7},{7,6},{8,9},{9,8},{10,11... | collective-permute-start | bytes 491528 | tf_op jit(solution)/shard_map/ppermute | solution.py:21
  1.8 40.0 %collective-permute-start.3 = (bf16[1,128,5120]{2,1,0:T(8,128)(2,1)}, bf16[1,128,5120]{2,1,0:T(8,128)(2,1)S(1)}, u32[]{:S(2)}, u32[]{:S(2)}) collective-permute-start(bf16[1,128,5120]{2,1,0:T(8,128)(2,1)} %refs_0_.1), channel_id=1, source_target_pairs={{0,16},{16,0},{1,17},{17,1},{2,18},{18,2},{3,19},{19,3},{4,20},{20... | collective-permute-start | bytes 3932168 | tf_op jit(solution)/shard_map/ppermute | solution.py:21
  5.2 36.5 %copy-start = (bf16[1,128,5120]{2,1,0:T(8,128)(2,1)S(1)}, bf16[1,128,5120]{2,1,0:T(8,128)(2,1)}, u32[]{:S(2)}) copy-start(bf16[1,128,5120]{2,1,0:T(8,128)(2,1)} %refs_0_.1) | copy-start | bytes 3932164
  5.3 11.0 %collective-permute-start.1 = (bf16[640,256]{1,0:T(8,128)(2,1)S(1)}, bf16[640,256]{1,0:T(8,128)(2,1)S(1)}, u32[]{:S(2)}, u32[]{:S(2)}) collective-permute-start(bf16[640,256]{1,0:T(8,128)(2,1)S(1)} %maximum_select_fusion.refs_4_), channel_id=1, source_target_pairs={{0,4},{1,5},{2,6},{3,7},{4,8},{5,9},{6,10},{7,11},{8,12},{9,13},{1... | collective-permute-start | bytes 983048 | tf_op jit(solution)/shard_map/ppermute | solution.py:356
  6.6 9.6 %collective-permute-start.6 = (bf16[640,256]{1,0:T(8,128)(2,1)S(1)}, bf16[640,256]{1,0:T(8,128)(2,1)S(1)}, u32[]{:S(2)}, u32[]{:S(2)}) collective-permute-start(bf16[640,256]{1,0:T(8,128)(2,1)S(1)} %maximum_select_fusion.refs_4_), channel_id=1, source_target_pairs={{0,2},{1,3},{2,0},{3,1},{4,6},{5,7},{6,4},{7,5},{8,10},{9,11},{10,... | collective-permute-start | bytes 983048 | tf_op jit(solution)/shard_map/ppermute | solution.py:21
  8.0 16.5 %collective-permute-start.4 = (bf16[640,256]{1,0:T(8,128)(2,1)S(1)}, bf16[640,256]{1,0:T(8,128)(2,1)}, u32[]{:S(2)}, u32[]{:S(2)}) collective-permute-start(bf16[640,256]{1,0:T(8,128)(2,1)S(1)} %maximum_select_fusion.refs_4_), channel_id=1, source_target_pairs={{0,12},{1,13},{2,14},{3,15},{4,0},{5,1},{6,2},{7,3},{8,4},{9,5},{1... | collective-permute-start | bytes 983048 | tf_op jit(solution)/shard_map/ppermute | solution.py:356
  10.1 16.5 %collective-permute-start.5 = (bf16[2,128,1024]{2,1,0:T(8,128)(2,1)}, bf16[2,128,1024]{2,1,0:T(8,128)(2,1)}, u32[]{:S(2)}, u32[]{:S(2)}) collective-permute-start(bf16[2,128,1024]{2,1,0:T(8,128)(2,1)} %param.9), channel_id=1, source_target_pairs={{0,2},{1,3},{2,0},{3,1},{4,6},{5,7},{6,4},{7,5},{8,10},{9,11},{10,... | collective-permute-start | bytes 1572872 | tf_op jit(solution)/shard_map/ppermute | solution.py:21
  16.2 0.7 copy-start.1
  17.0 16.6 %collective-permute-start.7 = (bf16[640,256]{1,0:T(8,128)(2,1)S(1)}, bf16[640,256]{1,0:T(8,128)(2,1)}, u32[]{:S(2)}, u32[]{:S(2)}) collective-permute-start(bf16[640,256]{1,0:T(8,128)(2,1)S(1)} %collective-permute-done.1.refs_6_), channel_id=1, source_target_pairs={{0,2},{1,3},{2,0},{3,1},{4,6},{5,7},{6,4},{7,5},{8,10},{9,11},{10,... | collective-permute-start | bytes 983048 | tf_op jit(solution)/shard_map/ppermute | solution.py:21
  17.2 28.9 %copy-start.5 = (bf16[2,128,1024]{2,1,0:T(8,128)(2,1)S(1)}, bf16[2,128,1024]{2,1,0:T(8,128)(2,1)}, u32[]{:S(2)}) copy-start(bf16[2,128,1024]{2,1,0:T(8,128)(2,1)} %param.9) | copy-start | bytes 1572868
  17.2 24.6 %collective-permute-start.2 = (bf16[640,256]{1,0:T(8,128)(2,1)S(1)}, bf16[640,256]{1,0:T(8,128)(2,1)S(1)}, u32[]{:S(2)}, u32[]{:S(2)}) collective-permute-start(bf16[640,256]{1,0:T(8,128)(2,1)S(1)} %collective-permute-done.1.refs_6_), channel_id=1, source_target_pairs={{0,4},{1,5},{2,6},{3,7},{4,8},{5,9},{6,10},{7,11},{8,12},{9,13},{1... | collective-permute-start | bytes 983048 | tf_op jit(solution)/shard_map/ppermute | solution.py:356
  33.6 7.9 %collective-permute-start.8 = (bf16[640,256]{1,0:T(8,128)(2,1)}, bf16[640,256]{1,0:T(8,128)(2,1)S(1)}, u32[]{:S(2)}, u32[]{:S(2)}) collective-permute-start(bf16[640,256]{1,0:T(8,128)(2,1)} %collective-permute-done.4.refs_8_), channel_id=1, source_target_pairs={{0,2},{1,3},{2,0},{3,1},{4,6},{5,7},{6,4},{7,5},{8,10},{9,11},{10,... | collective-permute-start | bytes 983048 | tf_op jit(solution)/shard_map/ppermute | solution.py:21
  41.5 24.7 %collective-permute-start.19 = (bf16[256,256]{1,0:T(8,128)(2,1)S(1)}, bf16[256,256]{1,0:T(8,128)(2,1)}, u32[]{:S(2)}, u32[]{:S(2)}) collective-permute-start(bf16[256,256]{1,0:T(8,128)(2,1)S(1)} %pad_maximum_fusion.8), channel_id=1, source_target_pairs={{0,2},{1,3},{2,0},{3,1},{4,6},{5,7},{6,4},{7,5},{8,10},{9,11},{10,... | collective-permute-start | bytes 393224 | tf_op jit(solution)/shard_map/ppermute | solution.py:21
  41.8 15.1 %collective-permute-start.9 = (bf16[1,128,5120]{2,1,0:T(8,128)(2,1)S(1)}, bf16[1,128,5120]{2,1,0:T(8,128)(2,1)S(1)}, u32[]{:S(2)}, u32[]{:S(2)}) collective-permute-start(bf16[1,128,5120]{2,1,0:T(8,128)(2,1)S(1)} %copy-done), channel_id=1, source_target_pairs={{0,1},{1,0},{2,3},{3,2},{4,5},{5,4},{6,7},{7,6},{8,9},{9,8},{10,11... | collective-permute-start | bytes 3932168 | tf_op jit(solution)/shard_map/ppermute | solution.py:21
  44.5 12.7 %collective-permute-start.10 = (bf16[1,128,5120]{2,1,0:T(8,128)(2,1)S(1)}, bf16[1,128,5120]{2,1,0:T(8,128)(2,1)S(1)}, u32[]{:S(2)}, u32[]{:S(2)}) collective-permute-start(bf16[1,128,5120]{2,1,0:T(8,128)(2,1)S(1)} %collective-permute-done.3.refs_2_), channel_id=1, source_target_pairs={{0,1},{1,0},{2,3},{3,2},{4,5},{5,4},{6,7},{7,6},{8,9},{9,8},{10,11... | collective-permute-start | bytes 3932168 | tf_op jit(solution)/shard_map/ppermute | solution.py:21
  44.6 9.7 %collective-permute-start.11 = (bf16[640,256]{1,0:T(8,128)(2,1)S(1)}, bf16[640,256]{1,0:T(8,128)(2,1)S(1)}, u32[]{:S(2)}, u32[]{:S(2)}) collective-permute-start(bf16[640,256]{1,0:T(8,128)(2,1)S(1)} %collective-permute-done.2.refs_10_), channel_id=1, source_target_pairs={{0,2},{1,3},{2,0},{3,1},{4,6},{5,7},{6,4},{7,5},{8,10},{9,11},{10,... | collective-permute-start | bytes 983048 | tf_op jit(solution)/shard_map/ppermute | solution.py:21
  45.8 2.8 %collective-permute-start.12 = (s32[28,3]{0,1:T(4,128)S(1)}, s32[28,3]{0,1:T(4,128)S(1)}, u32[]{:S(2)}, u32[]{:S(2)}) collective-permute-start(s32[28,3]{0,1:T(4,128)S(1)} %copy-done.6), channel_id=1, source_target_pairs={{0,16},{16,0},{1,17},{17,1},{2,18},{18,2},{3,19},{19,3},{4,20},{20... | collective-permute-start | bytes 1016 | tf_op jit(solution)/shard_map/ppermute | solution.py:21
  47.3 2.7 %copy-start.7 = (pred[28]{0:T(512)(128)(4,1)S(1)}, pred[28]{0:T(512)(128)(4,1)}, u32[]{:S(2)}) copy-start(pred[28]{0:T(512)(128)(4,1)} %compare_bitcast_fusion.1) | copy-start | bytes 88
  47.3 2.7 %copy-start.8 = (s32[2]{0:T(128)S(1)}, s32[2]{0:T(128)}, u32[]{:S(2)}) copy-start(s32[2]{0:T(128)} %pad_add_fusion.1) | copy-start | bytes 28
  47.3 2.7 %copy-start.9 = (s32[28]{0:T(128)S(1)}, s32[28]{0:T(128)}, u32[]{:S(2)}) copy-start(s32[28]{0:T(128)} %slice_bitcast_fusion.1) | copy-start | bytes 340
  47.4 9.8 %copy-start.2 = (bf16[640,256]{1,0:T(8,128)(2,1)S(1)}, bf16[640,256]{1,0:T(8,128)(2,1)}, u32[]{:S(2)}) copy-start(bf16[640,256]{1,0:T(8,128)(2,1)} %copy-done.1) | copy-start | bytes 983044
  48.7 18.2 %collective-permute-start.16 = (bf16[4,128,256]{2,1,0:T(8,128)(2,1)S(1)}, bf16[4,128,256]{2,1,0:T(8,128)(2,1)}, u32[]{:S(2)}, u32[]{:S(2)}) collective-permute-start(bf16[4,128,256]{2,1,0:T(8,128)(2,1)S(1)} %bitcast.53), channel_id=1, source_target_pairs={{0,4},{1,5},{2,6},{3,7},{4,8},{5,9},{6,10},{7,11},{8,12},{9,13},{1... | collective-permute-start | bytes 786440 | tf_op jit(solution)/shard_map/ppermute | solution.py:375
  54.3 13.1 %collective-permute-start.17 = (bf16[4,128,256]{2,1,0:T(8,128)(2,1)S(1)}, bf16[4,128,256]{2,1,0:T(8,128)(2,1)}, u32[]{:S(2)}, u32[]{:S(2)}) collective-permute-start(bf16[4,128,256]{2,1,0:T(8,128)(2,1)S(1)} %bitcast.52), channel_id=1, source_target_pairs={{0,12},{1,13},{2,14},{3,15},{4,0},{5,1},{6,2},{7,3},{8,4},{9,5},{1... | collective-permute-start | bytes 786440 | tf_op jit(solution)/shard_map/ppermute | solution.py:375
  56.9 20.3 %collective-permute-start.18 = (bf16[4,128,256]{2,1,0:T(8,128)(2,1)S(1)}, bf16[4,128,256]{2,1,0:T(8,128)(2,1)}, u32[]{:S(2)}, u32[]{:S(2)}) collective-permute-start(bf16[4,128,256]{2,1,0:T(8,128)(2,1)S(1)} %bitcast.51), channel_id=1, source_target_pairs={{0,8},{1,9},{2,10},{3,11},{4,12},{5,13},{6,14},{7,15},{8,0},{9,1},... | collective-permute-start | bytes 786440 | tf_op jit(solution)/shard_map/ppermute | solution.py:375
  60.3 16.9 %collective-permute-start.13 = (bf16[2,128,256]{2,1,0:T(8,128)(2,1)S(1)}, bf16[2,128,256]{2,1,0:T(8,128)(2,1)S(1)}, u32[]{:S(2)}, u32[]{:S(2)}) collective-permute-start(bf16[2,128,256]{2,1,0:T(8,128)(2,1)S(1)} %get-tuple-element.37), channel_id=1, source_target_pairs={{0,0},{1,8},{2,2},{3,10},{4,1},{5,9},{6,3},{7,11},{8,16},{9,24},{1... | collective-permute-start | bytes 393224 | tf_op jit(solution)/shard_map/ppermute | solution.py:452
  66.3 10.9 %collective-permute-start.14 = (bf16[2,128,256]{2,1,0:T(8,128)(2,1)S(1)}, bf16[2,128,256]{2,1,0:T(8,128)(2,1)S(1)}, u32[]{:S(2)}, u32[]{:S(2)}) collective-permute-start(bf16[2,128,256]{2,1,0:T(8,128)(2,1)S(1)} %get-tuple-element.38), channel_id=1, source_target_pairs={{0,16},{1,24},{2,18},{3,26},{4,17},{5,25},{6,19},{7,27},{8,0},{9,8... | collective-permute-start | bytes 393224 | tf_op jit(solution)/shard_map/ppermute | solution.py:452
  66.9 15.4 %collective-permute-start.20 = (bf16[4,128,256]{2,1,0:T(8,128)(2,1)S(1)}, bf16[4,128,256]{2,1,0:T(8,128)(2,1)S(1)}, u32[]{:S(2)}, u32[]{:S(2)}) collective-permute-start(bf16[4,128,256]{2,1,0:T(8,128)(2,1)S(1)} %bitcast.38), channel_id=1, source_target_pairs={{0,1},{1,0},{2,3},{3,2},{4,5},{5,4},{6,7},{7,6},{8,9},{9,8},{10,11... | collective-permute-start | bytes 786440 | tf_op jit(solution)/shard_map/ppermute | solution.py:21
  67.4 14.8 %collective-permute-start.24 = (bf16[2,128,256]{2,1,0:T(8,128)(2,1)S(1)}, bf16[2,128,256]{2,1,0:T(8,128)(2,1)S(1)}, u32[]{:S(2)}, u32[]{:S(2)}) collective-permute-start(bf16[2,128,256]{2,1,0:T(8,128)(2,1)S(1)} %bitcast.40), channel_id=1, source_target_pairs={{0,1},{1,0},{2,3},{3,2},{4,5},{5,4},{6,7},{7,6},{8,9},{9,8},{10,11... | collective-permute-start | bytes 393224 | tf_op jit(solution)/shard_map/ppermute | solution.py:21
  77.2 7.2 %collective-permute-start.21 = (bf16[4,128,256]{2,1,0:T(8,128)(2,1)}, bf16[4,128,256]{2,1,0:T(8,128)(2,1)S(1)}, u32[]{:S(2)}, u32[]{:S(2)}) collective-permute-start(bf16[4,128,256]{2,1,0:T(8,128)(2,1)} %collective-permute-done.16.refs_1_), channel_id=1, source_target_pairs={{0,1},{1,0},{2,3},{3,2},{4,5},{5,4},{6,7},{7,6},{8,9},{9,8},{10,11... | collective-permute-start | bytes 786440 | tf_op jit(solution)/shard_map/ppermute | solution.py:21
  81.7 2.7 %collective-permute-start.22 = (bf16[4,128,256]{2,1,0:T(8,128)(2,1)}, bf16[4,128,256]{2,1,0:T(8,128)(2,1)S(1)}, u32[]{:S(2)}, u32[]{:S(2)}) collective-permute-start(bf16[4,128,256]{2,1,0:T(8,128)(2,1)} %collective-permute-done.17.refs_2_), channel_id=1, source_target_pairs={{0,1},{1,0},{2,3},{3,2},{4,5},{5,4},{6,7},{7,6},{8,9},{9,8},{10,11... | collective-permute-start | bytes 786440 | tf_op jit(solution)/shard_map/ppermute | solution.py:21
  81.7 2.7 %collective-permute-start.23 = (bf16[4,128,256]{2,1,0:T(8,128)(2,1)}, bf16[4,128,256]{2,1,0:T(8,128)(2,1)S(1)}, u32[]{:S(2)}, u32[]{:S(2)}) collective-permute-start(bf16[4,128,256]{2,1,0:T(8,128)(2,1)} %collective-permute-done.18.refs_3_), channel_id=1, source_target_pairs={{0,1},{1,0},{2,3},{3,2},{4,5},{5,4},{6,7},{7,6},{8,9},{9,8},{10,11... | collective-permute-start | bytes 786440 | tf_op jit(solution)/shard_map/ppermute | solution.py:21
  82.2 1.8 %collective-permute-start.25 = (bf16[2,128,256]{2,1,0:T(8,128)(2,1)}, bf16[2,128,256]{2,1,0:T(8,128)(2,1)S(1)}, u32[]{:S(2)}, u32[]{:S(2)}) collective-permute-start(bf16[2,128,256]{2,1,0:T(8,128)(2,1)} %bitcast.32.refs_5_), channel_id=1, source_target_pairs={{0,1},{1,0},{2,3},{3,2},{4,5},{5,4},{6,7},{7,6},{8,9},{9,8},{10,11... | collective-permute-start | bytes 393224 | tf_op jit(solution)/shard_map/ppermute | solution.py:21
  82.3 17.3 %collective-permute-start.15 = (bf16[4,128,256]{2,1,0:T(8,128)(2,1)S(1)}, bf16[4,128,256]{2,1,0:T(8,128)(2,1)S(1)}, u32[]{:S(2)}, u32[]{:S(2)}) collective-permute-start(bf16[4,128,256]{2,1,0:T(8,128)(2,1)S(1)} %constant_dynamic-update-slice_fusion.refs_0_), channel_id=1, source_target_pairs={{0,2},{1,3},{2,0},{3,1},{4,6},{5,7},{6,4},{7,5},{8,10},{9,11},{10,... | collective-permute-start | bytes 786440 | tf_op jit(solution)/shard_map/ppermute | solution.py:21
  84.0 15.7 %collective-permute-start.26 = (bf16[4,128,256]{2,1,0:T(8,128)(2,1)S(1)}, bf16[4,128,256]{2,1,0:T(8,128)(2,1)S(1)}, u32[]{:S(2)}, u32[]{:S(2)}) collective-permute-start(bf16[4,128,256]{2,1,0:T(8,128)(2,1)S(1)} %constant_dynamic-update-slice_fusion.refs_0_), channel_id=1, source_target_pairs={{0,1},{1,0},{2,3},{3,2},{4,5},{5,4},{6,7},{7,6},{8,9},{9,8},{10,11... | collective-permute-start | bytes 786440 | tf_op jit(solution)/shard_map/ppermute | solution.py:21
  84.4 0.9 copy-start.3
  85.3 1.0 copy-start.4
  99.6 1.6 %collective-permute-start.27 = (bf16[4,128,256]{2,1,0:T(8,128)(2,1)S(1)}, bf16[4,128,256]{2,1,0:T(8,128)(2,1)S(1)}, u32[]{:S(2)}, u32[]{:S(2)}) collective-permute-start(bf16[4,128,256]{2,1,0:T(8,128)(2,1)S(1)} %collective-permute-done.15.refs_2_), channel_id=1, source_target_pairs={{0,1},{1,0},{2,3},{3,2},{4,5},{5,4},{6,7},{7,6},{8,9},{9,8},{10,11... | collective-permute-start | bytes 786440 | tf_op jit(solution)/shard_map/ppermute | solution.py:21

commit v5 on v3

--- a/solution.py
+++ b/solution.py
@@ -104,10 +104,9 @@
         if not first:
             old_top = top_ref[group]
             row_top = jnp.maximum(old_top, row_top)
-        weights = jnp.exp(scores - jnp.concatenate([row_top] * copies, axis=1))
-        product = jnp.dot(
-            weights.astype(jnp.bfloat16), extended, preferred_element_type=jnp.float32
-        )
+        below = scores - jnp.concatenate([row_top] * copies, axis=1)
+        weights = jnp.exp(below.astype(jnp.bfloat16))
+        product = jnp.dot(weights, extended, preferred_element_type=jnp.float32)
         if not first:
             shrink = jnp.exp(old_top - row_top)
             product += sum_ref[group] * jnp.concatenate([shrink, shrink], axis=1)
@@ -362,12 +361,14 @@
             return lax.ppermute(value, "kv", [(i, (i + step) % devices) for i in range(devices)])
 
         near, back = to_plane(chip_rows, 1), to_plane(chip_rows, 3)
-        beside_own = exchange(chip_rows, 2)
         store_beside = exchange(page_store, 2)
         far = to_plane(near, 1)
-        near_sent, _ = lax.optimization_barrier((near, beside_own))
+        near_sent, own_sent, store_beside = lax.optimization_barrier(
+            (near, chip_rows, store_beside)
+        )
         beside_near = exchange(near_sent, 2)
-        back_sent, store_beside, _ = lax.optimization_barrier((back, store_beside, beside_near))
+        beside_own = exchange(own_sent, 2)
+        back_sent, _ = lax.optimization_barrier((back, beside_near))
         beside_back = exchange(back_sent, 2)
         far_sent, hidden_mine, hidden_passed, reuse_sent, stores, _ = lax.optimization_barrier(
             (far, prefix_hidden, hidden_across, reuse, (page_store, store_beside), beside_back)

time: 107 us -> 107 us (level)
  starting transfers between devices: 30.5 us -> 44.5 us
  waiting for transfers between devices: 39.7 us -> 28 us
  Pallas kernels: 22.9 us -> 21.5 us
    ppermute x20, waiting for transfers between devices: 25.2 us -> 8.01 us  [swap(): return lax.ppermute(value, axis, [(i, i ^ bit) for i in range(count)])]
    ppermute x3, starting transfers between devices: 4.38 us -> 13.6 us  [on_device(): lax.ppermute(parts_for(shift), 'kv', [(i, (i + shift * group_size) % devi...]
    ppermute x3, waiting for transfers between devices: 4.84 us -> 12.2 us  [to_plane(): lax.ppermute(value, 'kv', [(i, (i + step) % devices) for i in range(devic...]
    ppermute x20, starting transfers between devices: 15.2 us -> 20.9 us  [swap(): return lax.ppermute(value, axis, [(i, i ^ bit) for i in range(count)])]
    ppermute x3, waiting for transfers between devices: 9.61 us -> 5.24 us  [on_device(): lax.ppermute(parts_for(shift), 'kv', [(i, (i + shift * group_size) % devi...]
    pallas_call x1, Pallas kernels: 8.06 us -> 4.99 us  [attend_late(): pl.pallas_call(functools.partial(late_kernel, group_size), in_specs=[in_s...]
    ppermute x2, waiting for transfers between devices: 0.01 us -> 2.52 us  [on_device(): received.append(lax.ppermute(message, ('grp', 'kv'), routes))]
    pallas_call x1, Pallas kernels: 11.8 us -> 13.6 us  [attend_early(): pl.pallas_call(functools.partial(early_kernel, place, extension_at, len(p...]
  transfers between devices with their start and end apart: 28 -> 28, of which waited for: 9 -> 9; matrix products, arithmetic and copies ran while one was open for 9% -> 9% of each run, Pallas kernels for 14% -> 15%
where the time goes in v5:
time: 107 us
  starting transfers between devices  44.5 us (42%)
  waiting for transfers between devices  28 us (26%)
  Pallas kernels  21.5 us (20%)
  other arithmetic  7.57 us (7%)
  local copies, waits for them, and re-layouts  4.84 us (5%)
    ppermute x20, starting transfers between devices, swap(): return lax.ppermute(value, axis, [(i, i ^ bit) for i in range(count)])  20.9 us
    pallas_call x1, Pallas kernels, attend_early(): pl.pallas_call(functools.partial(early_kernel, place, extension_at, len(p...  13.6 us
    ppermute x3, starting transfers between devices, on_device(): lax.ppermute(parts_for(shift), 'kv', [(i, (i + shift * group_size) % devi...  13.6 us
    ppermute x3, waiting for transfers between devices, to_plane(): lax.ppermute(value, 'kv', [(i, (i + step) % devices) for i in range(devic...  12.2 us
    ppermute x20, waiting for transfers between devices, swap(): return lax.ppermute(value, axis, [(i, i ^ bit) for i in range(count)])  8.01 us
    ppermute x2, starting transfers between devices, on_device(): received.append(lax.ppermute(message, ('grp', 'kv'), routes))  6.65 us
    ppermute x3, waiting for transfers between devices, on_device(): lax.ppermute(parts_for(shift), 'kv', [(i, (i + shift * group_size) % devi...  5.24 us
    pallas_call x1, Pallas kernels, attend_late(): pl.pallas_call(functools.partial(late_kernel, group_size), in_specs=[in_s...  4.99 us
  transfers between devices with their start and end apart: 28, of which 9 were waited for; matrix products, arithmetic and copies ran while one was open for 9% of the time, Pallas kernels for 15%

profile of v5, /device:TPU:5, one launch (start us, length us, event | category | flops | bytes accessed | tf_op | source)
XLA Modules:
  0.0 106.8 jit_solution(13099234318239990977)
XLA Ops:
  0.0 1.0 constant_dynamic-slice_fusion.9
  1.0 0.7 collective-permute-start
  1.8 1.2 %collective-permute-start.3 = (bf16[1,128,5120]{2,1,0:T(8,128)(2,1)}, bf16[1,128,5120]{2,1,0:T(8,128)(2,1)S(1)}, u32[]{:S(2)}, u32[]{:S(2)}) collective-permute-start(bf16[1,128,5120]{2,1,0:T(8,128)(2,1)} %refs_0_.1), channel_id=1, source_target_pairs={{0,16},{16,0},{1,17},{17,1},{2,18},{18,2},{3,19},{19,3},{4,20},{20... | collective-permute-start | bytes 3932168 | tf_op jit(solution)/shard_map/ppermute | solution.py:20
  3.0 0.2 collective-permute-start.4
  3.2 1.2 %compare_bitcast_fusion.1 = pred[28]{0:T(512)(128)(4,1)} fusion(s32[28,3]{0,1:T(4,128)} %param.13), kind=kLoop, calls=%fused_computation.36 | loop fusion | flops 28 | bytes 140 | tf_op jit(solution)/shard_map/and | solution.py:424
  4.6 0.8 dynamic-slice_convert_fusion
  5.5 1.3 %collective-permute-start.1 = (bf16[640,256]{1,0:T(8,128)(2,1)S(1)}, bf16[640,256]{1,0:T(8,128)(2,1)S(1)}, u32[]{:S(2)}, u32[]{:S(2)}) collective-permute-start(bf16[640,256]{1,0:T(8,128)(2,1)S(1)} %maximum_select_fusion.refs_4_), channel_id=1, source_target_pairs={{0,4},{1,5},{2,6},{3,7},{4,8},{5,9},{6,10},{7,11},{8,12},{9,13},{1... | collective-permute-start | bytes 983048 | tf_op jit(solution)/shard_map/ppermute | solution.py:361
  6.8 0.6 pad_add_fusion.1
  7.4 0.5 slice_bitcast_fusion.1
  7.9 2.0 %collective-permute-start.5 = (bf16[640,256]{1,0:T(8,128)(2,1)S(1)}, bf16[640,256]{1,0:T(8,128)(2,1)}, u32[]{:S(2)}, u32[]{:S(2)}) collective-permute-start(bf16[640,256]{1,0:T(8,128)(2,1)S(1)} %maximum_select_fusion.refs_4_), channel_id=1, source_target_pairs={{0,12},{1,13},{2,14},{3,15},{4,0},{5,1},{6,2},{7,3},{8,4},{9,5},{1... | collective-permute-start | bytes 983048 | tf_op jit(solution)/shard_map/ppermute | solution.py:361
  9.9 6.2 %collective-permute-done.1.refs_6_ = bf16[640,256]{1,0:T(8,128)(2,1)S(1)} collective-permute-done((bf16[640,256]{1,0:T(8,128)(2,1)S(1)}, bf16[640,256]{1,0:T(8,128)(2,1)S(1)}, u32[]{:S(2)}, u32[]{:S(2)}) %collective-permute-start.1) | collective-permute-done | bytes 327712 | tf_op jit(solution)/shard_map/ppermute | solution.py:361
  16.1 0.9 fusion.6
  17.1 1.3 %collective-permute-start.6 = (bf16[640,256]{1,0:T(8,128)(2,1)S(1)}, bf16[640,256]{1,0:T(8,128)(2,1)S(1)}, u32[]{:S(2)}, u32[]{:S(2)}) collective-permute-start(bf16[640,256]{1,0:T(8,128)(2,1)S(1)} %collective-permute-done.1.refs_6_), channel_id=1, source_target_pairs={{0,2},{1,3},{2,0},{3,1},{4,6},{5,7},{6,4},{7,5},{8,10},{9,11},{10,... | collective-permute-start | bytes 983048 | tf_op jit(solution)/shard_map/ppermute | solution.py:20
  18.4 0.5 fusion.3
  18.9 6.1 %collective-permute-done.5.refs_8_ = bf16[640,256]{1,0:T(8,128)(2,1)} collective-permute-done((bf16[640,256]{1,0:T(8,128)(2,1)S(1)}, bf16[640,256]{1,0:T(8,128)(2,1)}, u32[]{:S(2)}, u32[]{:S(2)}) %collective-permute-start.5) | collective-permute-done | bytes 327712 | tf_op jit(solution)/shard_map/ppermute | solution.py:361
  25.0 1.2 %collective-permute-start.7 = (bf16[640,256]{1,0:T(8,128)(2,1)}, bf16[640,256]{1,0:T(8,128)(2,1)S(1)}, u32[]{:S(2)}, u32[]{:S(2)}) collective-permute-start(bf16[640,256]{1,0:T(8,128)(2,1)} %collective-permute-done.5.refs_8_), channel_id=1, source_target_pairs={{0,2},{1,3},{2,0},{3,1},{4,6},{5,7},{6,4},{7,5},{8,10},{9,11},{10,... | collective-permute-start | bytes 983048 | tf_op jit(solution)/shard_map/ppermute | solution.py:20
  26.3 1.7 %fusion.1 = (bf16[256,128]{1,0:T(8,128)(2,1)S(1)}, f32[256,128]{1,0:T(8,128)S(1)}, f32[256,128]{1,0:T(8,128)}) fusion(f32[256,64]{1,0:T(8,128)S(1)} %get-tuple-element.84, f32[256,64]{1,0:T(8,128)S(1)} %get-tuple-element.85, bf16[256,256]{1,0:T(8,128)(2,1)} %param.8, f32[256,64]{1,0:T(8,128)S(1)} %get-tuple-element.77, f32[256,64]{1,0:T(8,128)S(1)} %get-tuple-element.76, ...), kind=kLoop, calls=%fused_computation.15 | loop fusion | flops 262144 | bytes 720896 | tf_op jit(solution)/shard_map/convert_element_type | solution.py:415
  27.9 0.3 collective-permute-start.10
  28.2 3.9 %collective-permute-done.7.refs_9_ = bf16[640,256]{1,0:T(8,128)(2,1)S(1)} collective-permute-done((bf16[640,256]{1,0:T(8,128)(2,1)}, bf16[640,256]{1,0:T(8,128)(2,1)S(1)}, u32[]{:S(2)}, u32[]{:S(2)}) %collective-permute-start.7) | collective-permute-done | bytes 327712 | tf_op jit(solution)/shard_map/ppermute | solution.py:20
  32.2 1.2 %collective-permute-start.19 = (bf16[256,256]{1,0:T(8,128)(2,1)S(1)}, bf16[256,256]{1,0:T(8,128)(2,1)}, u32[]{:S(2)}, u32[]{:S(2)}) collective-permute-start(bf16[256,256]{1,0:T(8,128)(2,1)S(1)} %pad_maximum_fusion.8), channel_id=1, source_target_pairs={{0,2},{1,3},{2,0},{3,1},{4,6},{5,7},{6,4},{7,5},{8,10},{9,11},{10,... | collective-permute-start | bytes 393224 | tf_op jit(solution)/shard_map/ppermute | solution.py:20
  33.4 6.3 %collective-permute-start.8 = (bf16[1,128,5120]{2,1,0:T(8,128)(2,1)S(1)}, bf16[1,128,5120]{2,1,0:T(8,128)(2,1)S(1)}, u32[]{:S(2)}, u32[]{:S(2)}) collective-permute-start(bf16[1,128,5120]{2,1,0:T(8,128)(2,1)S(1)} %copy-done), channel_id=1, source_target_pairs={{0,1},{1,0},{2,3},{3,2},{4,5},{5,4},{6,7},{7,6},{8,9},{9,8},{10,11... | collective-permute-start | bytes 3932168 | tf_op jit(solution)/shard_map/ppermute | solution.py:20
  39.8 0.3 collective-permute-start.12
  40.1 1.2 %constant_dynamic-slice_fusion = (bf16[2,128,256]{2,1,0:T(8,128)(2,1)S(1)}, bf16[2,128,256]{2,1,0:T(8,128)(2,1)S(1)}, bf16[2,128,256]{2,1,0:T(8,128)(2,1)S(1)}, ...) fusion(bf16[2,128,1024]{2,1,0:T(8,128)(2,1)} %collective-permut, ...), kind=kLoop, calls=%fused_computation.22 | loop fusion | bytes 2097168 | tf_op jit(solution)/shard_map/dynamic_slice | solution.py:354
  41.4 1.2 %collective-permute-done.12 = s32[28,3]{0,1:T(4,128)S(1)} collective-permute-done((s32[28,3]{0,1:T(4,128)S(1)}, s32[28,3]{0,1:T(4,128)S(1)}, u32[]{:S(2)}, u32[]{:S(2)}) %collective-permute-start.12) | collective-permute-done | bytes 368 | tf_op jit(solution)/shard_map/ppermute | solution.py:20
  42.5 0.2 collective-permute-start.11
  42.8 0.2 fusion.4
  43.2 1.0 fusion.2
  44.2 6.1 %collective-permute-start.16 = (bf16[4,128,256]{2,1,0:T(8,128)(2,1)S(1)}, bf16[4,128,256]{2,1,0:T(8,128)(2,1)}, u32[]{:S(2)}, u32[]{:S(2)}) collective-permute-start(bf16[4,128,256]{2,1,0:T(8,128)(2,1)S(1)} %bitcast.53), channel_id=1, source_target_pairs={{0,4},{1,5},{2,6},{3,7},{4,8},{5,9},{6,10},{7,11},{8,12},{9,13},{1... | collective-permute-start | bytes 786440 | tf_op jit(solution)/shard_map/ppermute | solution.py:382
  50.3 0.2 collective-permute-done.11.refs_11_
  50.5 7.3 %collective-permute-start.17 = (bf16[4,128,256]{2,1,0:T(8,128)(2,1)S(1)}, bf16[4,128,256]{2,1,0:T(8,128)(2,1)}, u32[]{:S(2)}, u32[]{:S(2)}) collective-permute-start(bf16[4,128,256]{2,1,0:T(8,128)(2,1)S(1)} %bitcast.52), channel_id=1, source_target_pairs={{0,12},{1,13},{2,14},{3,15},{4,0},{5,1},{6,2},{7,3},{8,4},{9,5},{1... | collective-permute-start | bytes 786440 | tf_op jit(solution)/shard_map/ppermute | solution.py:382
  57.8 0.2 pad_maximum_fusion
  58.0 0.2 collective-permute-start.18
  58.2 2.9 %project.1 = (bf16[2,128,256]{2,1,0:T(8,128)(2,1)S(1)}, bf16[2,128,256]{2,1,0:T(8,128)(2,1)S(1)}) custom-call(s32[10]{0:T(128)S(1)} %stack.71.meta, bf16[1,128,5120]{2,1,0:T(8,128)(2,1)S(1)} %copy-done, bf16[1,128,5120]{2,1,0:T(8,128)(2,1)S(1)} %collective-permute-done.8.refs_1_, bf16[1,128,5120]{2,1,0:T(8,128)(2,1)S(1)} %collective-permute-done.3.refs_2_, ...), custom_call_target="tpu_custom_call" | custom-call | flops 1342177280 | bytes 7864320 | tf_op jit(solution)/shard_map/project/pallas_call | solution.py:66
  61.1 6.6 %collective-permute-start.13 = (bf16[2,128,256]{2,1,0:T(8,128)(2,1)S(1)}, bf16[2,128,256]{2,1,0:T(8,128)(2,1)S(1)}, u32[]{:S(2)}, u32[]{:S(2)}) collective-permute-start(bf16[2,128,256]{2,1,0:T(8,128)(2,1)S(1)} %get-tuple-element.37), channel_id=1, source_target_pairs={{0,0},{1,8},{2,2},{3,10},{4,1},{5,9},{6,3},{7,11},{8,16},{9,24},{1... | collective-permute-start | bytes 393224 | tf_op jit(solution)/shard_map/ppermute | solution.py:459
  67.8 0.4 collective-permute-start.20
  68.3 0.1 collective-permute-start.24
  68.4 5.2 %collective-permute-done.18.refs_3_ = bf16[4,128,256]{2,1,0:T(8,128)(2,1)} collective-permute-done((bf16[4,128,256]{2,1,0:T(8,128)(2,1)S(1)}, bf16[4,128,256]{2,1,0:T(8,128)(2,1)}, u32[]{:S(2)}, u32[]{:S(2)}) %collective-permute-start.18) | collective-permute-done | bytes 262176 | tf_op jit(solution)/shard_map/ppermute | solution.py:382
  73.6 2.5 %collective-permute-done.14 = bf16[2,128,256]{2,1,0:T(8,128)(2,1)S(1)} collective-permute-done((bf16[2,128,256]{2,1,0:T(8,128)(2,1)S(1)}, bf16[2,128,256]{2,1,0:T(8,128)(2,1)S(1)}, u32[]{:S(2)}, u32[]{:S(2)}) %collective-permute-start.14) | collective-permute-done | bytes 131104 | tf_op jit(solution)/shard_map/ppermute | solution.py:459
  76.2 5.8 %collective-permute-start.21 = (bf16[4,128,256]{2,1,0:T(8,128)(2,1)}, bf16[4,128,256]{2,1,0:T(8,128)(2,1)S(1)}, u32[]{:S(2)}, u32[]{:S(2)}) collective-permute-start(bf16[4,128,256]{2,1,0:T(8,128)(2,1)} %collective-permute-done.16.refs_1_), channel_id=1, source_target_pairs={{0,1},{1,0},{2,3},{3,2},{4,5},{5,4},{6,7},{7,6},{8,9},{9,8},{10,11... | collective-permute-start | bytes 786440 | tf_op jit(solution)/shard_map/ppermute | solution.py:20
  82.0 0.5 collective-permute-start.23
  82.6 0.3 collective-permute-start.15
  83.2 1.1 %collective-permute-done.25.refs_11_ = bf16[2,128,256]{2,1,0:T(8,128)(2,1)S(1)} collective-permute-done((bf16[2,128,256]{2,1,0:T(8,128)(2,1)}, bf16[2,128,256]{2,1,0:T(8,128)(2,1)S(1)}, u32[]{:S(2)}, u32[]{:S(2)}) %collective-permute-start.25) | collective-permute-done | bytes 131104 | tf_op jit(solution)/shard_map/ppermute | solution.py:20
  84.3 0.4 collective-permute-start.26
  84.7 0.9 copy-done.1
  85.6 1.0 copy-done.2
  86.6 13.6 %early.1 = (bf16[5,256,128]{2,1,0:T(8,128)(2,1)S(1)}, f32[5,256,128]{2,1,0:T(8,128)S(1)}, f32[5,256,256]{2,1,0:T(8,128)S(1)}) custom-call(s32[28,3]{1,0:T(8,128)S(1)} %copy.11.reuse, s32[3]{0:T(128)S(1)} %pad_add_fusion.meta, bf16[256,640]{1,0:T(8,128)(2,1)S(1)} %copy-done.2, f32[256,128]{1,0:T(8,128)S(1)} %copy-done.1, ...), custom_call_target="tpu_custom_call" | custom-call | flops 2348810240 | bytes 1835008 | tf_op jit(solution)/shard_map/early/pallas_call | solution.py:221
  100.3 1.5 %collective-permute-done.27.refs_3_ = bf16[4,128,256]{2,1,0:T(8,128)(2,1)S(1)} collective-permute-done((bf16[4,128,256]{2,1,0:T(8,128)(2,1)S(1)}, bf16[4,128,256]{2,1,0:T(8,128)(2,1)S(1)}, u32[]{:S(2)}, u32[]{:S(2)}) %collective-permute-start.27) | collective-permute-done | bytes 262176 | tf_op jit(solution)/shard_map/ppermute | solution.py:20
  101.8 5.0 %late.1 = bf16[256,640]{1,0:T(8,128)(2,1)} custom-call(s32[28,3]{1,0:T(8,128)S(1)} %copy.11.reuse, s32[3]{0:T(128)S(1)} %pad_add_fusion.meta, bf16[5,256,128]{2,1,0:T(8,128)(2,1)S(1)} %get-tuple-element.49.turned, f32[5,256,128]{2,1,0:T(8,128)S(1)} %get-tuple-element.50.top_in, f32[5,256,256]{2,1,0:T(8,128)S(1)} %get-tuple-element.51.sum_in, ...), custom_call_target="tpu_custom_call" | custom-call | flops 1174405120 | bytes 917504 | tf_op jit(solution)/shard_map/late/pallas_call | solution.py:296
  (56 shorter events, 1.0 us)
Async XLA Ops:
  0.0 7.4 %copy-start.4 = (s32[28,3]{0,1:T(4,128)S(1)}, s32[28,3]{0,1:T(4,128)}, u32[]{:S(2)}) copy-start(s32[28,3]{0,1:T(4,128)} %param.13) | copy-start | bytes 1012
  1.0 4.3 %collective-permute-start = (bf16[320,256]{1,0:T(8,128)(2,1)S(1)}, bf16[320,256]{1,0:T(8,128)(2,1)S(1)}, u32[]{:S(2)}, u32[]{:S(2)}) collective-permute-start(bf16[320,256]{1,0:T(8,128)(2,1)S(1)} %get-tuple-element.58), channel_id=1, source_target_pairs={{0,1},{1,0},{2,3},{3,2},{4,5},{5,4},{6,7},{7,6},{8,9},{9,8},{10,11... | collective-permute-start | bytes 491528 | tf_op jit(solution)/shard_map/ppermute | solution.py:20
  1.8 31.6 %collective-permute-start.3 = (bf16[1,128,5120]{2,1,0:T(8,128)(2,1)}, bf16[1,128,5120]{2,1,0:T(8,128)(2,1)S(1)}, u32[]{:S(2)}, u32[]{:S(2)}) collective-permute-start(bf16[1,128,5120]{2,1,0:T(8,128)(2,1)} %refs_0_.1), channel_id=1, source_target_pairs={{0,16},{16,0},{1,17},{17,1},{2,18},{18,2},{3,19},{19,3},{4,20},{20... | collective-permute-start | bytes 3932168 | tf_op jit(solution)/shard_map/ppermute | solution.py:20
  3.0 14.1 %collective-permute-start.4 = (bf16[2,128,1024]{2,1,0:T(8,128)(2,1)}, bf16[2,128,1024]{2,1,0:T(8,128)(2,1)}, u32[]{:S(2)}, u32[]{:S(2)}) collective-permute-start(bf16[2,128,1024]{2,1,0:T(8,128)(2,1)} %param.9), channel_id=1, source_target_pairs={{0,2},{1,3},{2,0},{3,1},{4,6},{5,7},{6,4},{7,5},{8,10},{9,11},{10,... | collective-permute-start | bytes 1572872 | tf_op jit(solution)/shard_map/ppermute | solution.py:20
  5.4 28.0 %copy-start = (bf16[1,128,5120]{2,1,0:T(8,128)(2,1)S(1)}, bf16[1,128,5120]{2,1,0:T(8,128)(2,1)}, u32[]{:S(2)}) copy-start(bf16[1,128,5120]{2,1,0:T(8,128)(2,1)} %refs_0_.1) | copy-start | bytes 3932164
  5.5 10.7 %collective-permute-start.1 = (bf16[640,256]{1,0:T(8,128)(2,1)S(1)}, bf16[640,256]{1,0:T(8,128)(2,1)S(1)}, u32[]{:S(2)}, u32[]{:S(2)}) collective-permute-start(bf16[640,256]{1,0:T(8,128)(2,1)S(1)} %maximum_select_fusion.refs_4_), channel_id=1, source_target_pairs={{0,4},{1,5},{2,6},{3,7},{4,8},{5,9},{6,10},{7,11},{8,12},{9,13},{1... | collective-permute-start | bytes 983048 | tf_op jit(solution)/shard_map/ppermute | solution.py:361
  7.9 17.1 %collective-permute-start.5 = (bf16[640,256]{1,0:T(8,128)(2,1)S(1)}, bf16[640,256]{1,0:T(8,128)(2,1)}, u32[]{:S(2)}, u32[]{:S(2)}) collective-permute-start(bf16[640,256]{1,0:T(8,128)(2,1)S(1)} %maximum_select_fusion.refs_4_), channel_id=1, source_target_pairs={{0,12},{1,13},{2,14},{3,15},{4,0},{5,1},{6,2},{7,3},{8,4},{9,5},{1... | collective-permute-start | bytes 983048 | tf_op jit(solution)/shard_map/ppermute | solution.py:361
  16.1 23.9 %copy-start.3 = (bf16[2,128,1024]{2,1,0:T(8,128)(2,1)S(1)}, bf16[2,128,1024]{2,1,0:T(8,128)(2,1)}, u32[]{:S(2)}) copy-start(bf16[2,128,1024]{2,1,0:T(8,128)(2,1)} %param.9) | copy-start | bytes 1572868
  16.1 17.3 %collective-permute-start.2 = (bf16[640,256]{1,0:T(8,128)(2,1)S(1)}, bf16[640,256]{1,0:T(8,128)(2,1)S(1)}, u32[]{:S(2)}, u32[]{:S(2)}) collective-permute-start(bf16[640,256]{1,0:T(8,128)(2,1)S(1)} %collective-permute-done.1.refs_6_), channel_id=1, source_target_pairs={{0,4},{1,5},{2,6},{3,7},{4,8},{5,9},{6,10},{7,11},{8,12},{9,13},{1... | collective-permute-start | bytes 983048 | tf_op jit(solution)/shard_map/ppermute | solution.py:361
  17.1 7.9 %collective-permute-start.6 = (bf16[640,256]{1,0:T(8,128)(2,1)S(1)}, bf16[640,256]{1,0:T(8,128)(2,1)S(1)}, u32[]{:S(2)}, u32[]{:S(2)}) collective-permute-start(bf16[640,256]{1,0:T(8,128)(2,1)S(1)} %collective-permute-done.1.refs_6_), channel_id=1, source_target_pairs={{0,2},{1,3},{2,0},{3,1},{4,6},{5,7},{6,4},{7,5},{8,10},{9,11},{10,... | collective-permute-start | bytes 983048 | tf_op jit(solution)/shard_map/ppermute | solution.py:20
  25.0 7.2 %collective-permute-start.7 = (bf16[640,256]{1,0:T(8,128)(2,1)}, bf16[640,256]{1,0:T(8,128)(2,1)S(1)}, u32[]{:S(2)}, u32[]{:S(2)}) collective-permute-start(bf16[640,256]{1,0:T(8,128)(2,1)} %collective-permute-done.5.refs_8_), channel_id=1, source_target_pairs={{0,2},{1,3},{2,0},{3,1},{4,6},{5,7},{6,4},{7,5},{8,10},{9,11},{10,... | collective-permute-start | bytes 983048 | tf_op jit(solution)/shard_map/ppermute | solution.py:20
  27.9 16.2 %collective-permute-start.10 = (bf16[640,256]{1,0:T(8,128)(2,1)S(1)}, bf16[640,256]{1,0:T(8,128)(2,1)S(1)}, u32[]{:S(2)}, u32[]{:S(2)}) collective-permute-start(bf16[640,256]{1,0:T(8,128)(2,1)S(1)} %maximum_select_fusion.refs_4_), channel_id=1, source_target_pairs={{0,2},{1,3},{2,0},{3,1},{4,6},{5,7},{6,4},{7,5},{8,10},{9,11},{10,... | collective-permute-start | bytes 983048 | tf_op jit(solution)/shard_map/ppermute | solution.py:20
  32.2 35.5 %collective-permute-start.19 = (bf16[256,256]{1,0:T(8,128)(2,1)S(1)}, bf16[256,256]{1,0:T(8,128)(2,1)}, u32[]{:S(2)}, u32[]{:S(2)}) collective-permute-start(bf16[256,256]{1,0:T(8,128)(2,1)S(1)} %pad_maximum_fusion.8), channel_id=1, source_target_pairs={{0,2},{1,3},{2,0},{3,1},{4,6},{5,7},{6,4},{7,5},{8,10},{9,11},{10,... | collective-permute-start | bytes 393224 | tf_op jit(solution)/shard_map/ppermute | solution.py:20
  33.4 24.5 %collective-permute-start.8 = (bf16[1,128,5120]{2,1,0:T(8,128)(2,1)S(1)}, bf16[1,128,5120]{2,1,0:T(8,128)(2,1)S(1)}, u32[]{:S(2)}, u32[]{:S(2)}) collective-permute-start(bf16[1,128,5120]{2,1,0:T(8,128)(2,1)S(1)} %copy-done), channel_id=1, source_target_pairs={{0,1},{1,0},{2,3},{3,2},{4,5},{5,4},{6,7},{7,6},{8,9},{9,8},{10,11... | collective-permute-start | bytes 3932168 | tf_op jit(solution)/shard_map/ppermute | solution.py:20
  39.7 18.4 %collective-permute-start.9 = (bf16[1,128,5120]{2,1,0:T(8,128)(2,1)S(1)}, bf16[1,128,5120]{2,1,0:T(8,128)(2,1)S(1)}, u32[]{:S(2)}, u32[]{:S(2)}) collective-permute-start(bf16[1,128,5120]{2,1,0:T(8,128)(2,1)S(1)} %collective-permute-done.3.refs_2_), channel_id=1, source_target_pairs={{0,1},{1,0},{2,3},{3,2},{4,5},{5,4},{6,7},{7,6},{8,9},{9,8},{10,11... | collective-permute-start | bytes 3932168 | tf_op jit(solution)/shard_map/ppermute | solution.py:20
  39.8 2.7 %collective-permute-start.12 = (s32[28,3]{0,1:T(4,128)S(1)}, s32[28,3]{0,1:T(4,128)S(1)}, u32[]{:S(2)}, u32[]{:S(2)}) collective-permute-start(s32[28,3]{0,1:T(4,128)S(1)} %copy-done.4), channel_id=1, source_target_pairs={{0,16},{16,0},{1,17},{17,1},{2,18},{18,2},{3,19},{19,3},{4,20},{20... | collective-permute-start | bytes 1016 | tf_op jit(solution)/shard_map/ppermute | solution.py:20
  41.3 1.5 %copy-start.5 = (pred[28]{0:T(512)(128)(4,1)S(1)}, pred[28]{0:T(512)(128)(4,1)}, u32[]{:S(2)}) copy-start(pred[28]{0:T(512)(128)(4,1)} %compare_bitcast_fusion.1) | copy-start | bytes 88
  41.3 1.5 %copy-start.6 = (s32[2]{0:T(128)S(1)}, s32[2]{0:T(128)}, u32[]{:S(2)}) copy-start(s32[2]{0:T(128)} %pad_add_fusion.1) | copy-start | bytes 28
  41.3 1.5 %copy-start.7 = (s32[28]{0:T(128)S(1)}, s32[28]{0:T(128)}, u32[]{:S(2)}) copy-start(s32[28]{0:T(128)} %slice_bitcast_fusion.1) | copy-start | bytes 340
  42.5 7.9 %collective-permute-start.11 = (bf16[640,256]{1,0:T(8,128)(2,1)S(1)}, bf16[640,256]{1,0:T(8,128)(2,1)S(1)}, u32[]{:S(2)}, u32[]{:S(2)}) collective-permute-start(bf16[640,256]{1,0:T(8,128)(2,1)S(1)} %collective-permute-done.2.refs_10_), channel_id=1, source_target_pairs={{0,2},{1,3},{2,0},{3,1},{4,6},{5,7},{6,4},{7,5},{8,10},{9,11},{10,... | collective-permute-start | bytes 983048 | tf_op jit(solution)/shard_map/ppermute | solution.py:20
  44.2 23.7 %collective-permute-start.16 = (bf16[4,128,256]{2,1,0:T(8,128)(2,1)S(1)}, bf16[4,128,256]{2,1,0:T(8,128)(2,1)}, u32[]{:S(2)}, u32[]{:S(2)}) collective-permute-start(bf16[4,128,256]{2,1,0:T(8,128)(2,1)S(1)} %bitcast.53), channel_id=1, source_target_pairs={{0,4},{1,5},{2,6},{3,7},{4,8},{5,9},{6,10},{7,11},{8,12},{9,13},{1... | collective-permute-start | bytes 786440 | tf_op jit(solution)/shard_map/ppermute | solution.py:382
  50.5 17.8 %collective-permute-start.17 = (bf16[4,128,256]{2,1,0:T(8,128)(2,1)S(1)}, bf16[4,128,256]{2,1,0:T(8,128)(2,1)}, u32[]{:S(2)}, u32[]{:S(2)}) collective-permute-start(bf16[4,128,256]{2,1,0:T(8,128)(2,1)S(1)} %bitcast.52), channel_id=1, source_target_pairs={{0,12},{1,13},{2,14},{3,15},{4,0},{5,1},{6,2},{7,3},{8,4},{9,5},{1... | collective-permute-start | bytes 786440 | tf_op jit(solution)/shard_map/ppermute | solution.py:382
  58.0 15.7 %collective-permute-start.18 = (bf16[4,128,256]{2,1,0:T(8,128)(2,1)S(1)}, bf16[4,128,256]{2,1,0:T(8,128)(2,1)}, u32[]{:S(2)}, u32[]{:S(2)}) collective-permute-start(bf16[4,128,256]{2,1,0:T(8,128)(2,1)S(1)} %bitcast.51), channel_id=1, source_target_pairs={{0,8},{1,9},{2,10},{3,11},{4,12},{5,13},{6,14},{7,15},{8,0},{9,1},... | collective-permute-start | bytes 786440 | tf_op jit(solution)/shard_map/ppermute | solution.py:382
  61.1 12.5 %collective-permute-start.13 = (bf16[2,128,256]{2,1,0:T(8,128)(2,1)S(1)}, bf16[2,128,256]{2,1,0:T(8,128)(2,1)S(1)}, u32[]{:S(2)}, u32[]{:S(2)}) collective-permute-start(bf16[2,128,256]{2,1,0:T(8,128)(2,1)S(1)} %get-tuple-element.37), channel_id=1, source_target_pairs={{0,0},{1,8},{2,2},{3,10},{4,1},{5,9},{6,3},{7,11},{8,16},{9,24},{1... | collective-permute-start | bytes 393224 | tf_op jit(solution)/shard_map/ppermute | solution.py:459
  67.7 8.4 %collective-permute-start.14 = (bf16[2,128,256]{2,1,0:T(8,128)(2,1)S(1)}, bf16[2,128,256]{2,1,0:T(8,128)(2,1)S(1)}, u32[]{:S(2)}, u32[]{:S(2)}) collective-permute-start(bf16[2,128,256]{2,1,0:T(8,128)(2,1)S(1)} %get-tuple-element.38), channel_id=1, source_target_pairs={{0,16},{1,24},{2,18},{3,26},{4,17},{5,25},{6,19},{7,27},{8,0},{9,8... | collective-permute-start | bytes 393224 | tf_op jit(solution)/shard_map/ppermute | solution.py:459
  67.8 14.8 %collective-permute-start.20 = (bf16[4,128,256]{2,1,0:T(8,128)(2,1)S(1)}, bf16[4,128,256]{2,1,0:T(8,128)(2,1)S(1)}, u32[]{:S(2)}, u32[]{:S(2)}) collective-permute-start(bf16[4,128,256]{2,1,0:T(8,128)(2,1)S(1)} %bitcast.38), channel_id=1, source_target_pairs={{0,1},{1,0},{2,3},{3,2},{4,5},{5,4},{6,7},{7,6},{8,9},{9,8},{10,11... | collective-permute-start | bytes 786440 | tf_op jit(solution)/shard_map/ppermute | solution.py:20
  68.3 14.3 %collective-permute-start.24 = (bf16[2,128,256]{2,1,0:T(8,128)(2,1)S(1)}, bf16[2,128,256]{2,1,0:T(8,128)(2,1)S(1)}, u32[]{:S(2)}, u32[]{:S(2)}) collective-permute-start(bf16[2,128,256]{2,1,0:T(8,128)(2,1)S(1)} %bitcast.40), channel_id=1, source_target_pairs={{0,1},{1,0},{2,3},{3,2},{4,5},{5,4},{6,7},{7,6},{8,9},{9,8},{10,11... | collective-permute-start | bytes 393224 | tf_op jit(solution)/shard_map/ppermute | solution.py:20
  76.2 8.5 %collective-permute-start.21 = (bf16[4,128,256]{2,1,0:T(8,128)(2,1)}, bf16[4,128,256]{2,1,0:T(8,128)(2,1)S(1)}, u32[]{:S(2)}, u32[]{:S(2)}) collective-permute-start(bf16[4,128,256]{2,1,0:T(8,128)(2,1)} %collective-permute-done.16.refs_1_), channel_id=1, source_target_pairs={{0,1},{1,0},{2,3},{3,2},{4,5},{5,4},{6,7},{7,6},{8,9},{9,8},{10,11... | collective-permute-start | bytes 786440 | tf_op jit(solution)/shard_map/ppermute | solution.py:20
  82.0 2.7 %collective-permute-start.22 = (bf16[4,128,256]{2,1,0:T(8,128)(2,1)}, bf16[4,128,256]{2,1,0:T(8,128)(2,1)S(1)}, u32[]{:S(2)}, u32[]{:S(2)}) collective-permute-start(bf16[4,128,256]{2,1,0:T(8,128)(2,1)} %collective-permute-done.17.refs_2_), channel_id=1, source_target_pairs={{0,1},{1,0},{2,3},{3,2},{4,5},{5,4},{6,7},{7,6},{8,9},{9,8},{10,11... | collective-permute-start | bytes 786440 | tf_op jit(solution)/shard_map/ppermute | solution.py:20
  82.0 2.7 %collective-permute-start.23 = (bf16[4,128,256]{2,1,0:T(8,128)(2,1)}, bf16[4,128,256]{2,1,0:T(8,128)(2,1)S(1)}, u32[]{:S(2)}, u32[]{:S(2)}) collective-permute-start(bf16[4,128,256]{2,1,0:T(8,128)(2,1)} %collective-permute-done.18.refs_3_), channel_id=1, source_target_pairs={{0,1},{1,0},{2,3},{3,2},{4,5},{5,4},{6,7},{7,6},{8,9},{9,8},{10,11... | collective-permute-start | bytes 786440 | tf_op jit(solution)/shard_map/ppermute | solution.py:20
  82.5 1.8 %collective-permute-start.25 = (bf16[2,128,256]{2,1,0:T(8,128)(2,1)}, bf16[2,128,256]{2,1,0:T(8,128)(2,1)S(1)}, u32[]{:S(2)}, u32[]{:S(2)}) collective-permute-start(bf16[2,128,256]{2,1,0:T(8,128)(2,1)} %bitcast.32.refs_5_), channel_id=1, source_target_pairs={{0,1},{1,0},{2,3},{3,2},{4,5},{5,4},{6,7},{7,6},{8,9},{9,8},{10,11... | collective-permute-start | bytes 393224 | tf_op jit(solution)/shard_map/ppermute | solution.py:20
  82.6 17.5 %collective-permute-start.15 = (bf16[4,128,256]{2,1,0:T(8,128)(2,1)S(1)}, bf16[4,128,256]{2,1,0:T(8,128)(2,1)S(1)}, u32[]{:S(2)}, u32[]{:S(2)}) collective-permute-start(bf16[4,128,256]{2,1,0:T(8,128)(2,1)S(1)} %constant_dynamic-update-slice_fusion.refs_0_), channel_id=1, source_target_pairs={{0,2},{1,3},{2,0},{3,1},{4,6},{5,7},{6,4},{7,5},{8,10},{9,11},{10,... | collective-permute-start | bytes 786440 | tf_op jit(solution)/shard_map/ppermute | solution.py:20
  84.3 16.0 %collective-permute-start.26 = (bf16[4,128,256]{2,1,0:T(8,128)(2,1)S(1)}, bf16[4,128,256]{2,1,0:T(8,128)(2,1)S(1)}, u32[]{:S(2)}, u32[]{:S(2)}) collective-permute-start(bf16[4,128,256]{2,1,0:T(8,128)(2,1)S(1)} %constant_dynamic-update-slice_fusion.refs_0_), channel_id=1, source_target_pairs={{0,1},{1,0},{2,3},{3,2},{4,5},{5,4},{6,7},{7,6},{8,9},{9,8},{10,11... | collective-permute-start | bytes 786440 | tf_op jit(solution)/shard_map/ppermute | solution.py:20
  84.7 0.9 copy-start.1
  85.6 1.0 copy-start.2
  100.2 1.6 %collective-permute-start.27 = (bf16[4,128,256]{2,1,0:T(8,128)(2,1)S(1)}, bf16[4,128,256]{2,1,0:T(8,128)(2,1)S(1)}, u32[]{:S(2)}, u32[]{:S(2)}) collective-permute-start(bf16[4,128,256]{2,1,0:T(8,128)(2,1)S(1)} %collective-permute-done.15.refs_2_), channel_id=1, source_target_pairs={{0,1},{1,0},{2,3},{3,2},{4,5},{5,4},{6,7},{7,6},{8,9},{9,8},{10,11... | collective-permute-start | bytes 786440 | tf_op jit(solution)/shard_map/ppermute | solution.py:20
